TPU v7x, 32 devices: a whole 2x2x4 slice. The times are simulated.
32 devices in a mesh: groups: 2 (over x), slab: 16 (over z, y, core).
Axes of the slice: x: 2, y: 2, z: 4, core: 2. Of those that a mesh axis runs over, the one named last changes fastest.
Arguments:
- mean_volume: bfloat16 [131072, 256], P(('groups', 'slab')), parts along dimension 0, may hold values from -12 to 12
- components: bfloat16 [6, 131072, 256], P(None, ('groups', 'slab')), parts along dimension 1, may hold values from -12 to 12
- images: bfloat16 [128, 256, 256], P(('groups', 'slab')), parts along dimension 0, may hold values from -24 to 24
- tilt: int32 [128], P(('groups', 'slab')), parts along dimension 0, may hold values from -127 to 127, as said below
- shift: int32 [128], P(('groups', 'slab')), parts along dimension 0, may hold values from 0 to 127
- frac: int32 [128], P(('groups', 'slab')), parts along dimension 0, may hold values from 0 to 15
- noise_var: float32 [128], P(('groups', 'slab')), parts along dimension 0, may hold values from 0.1 to 1
Outputs:
- new_components: bfloat16 [6, 131072, 256], P(None, ('groups', 'slab')), parts along dimension 1
- latents: float32 [128, 6], P(('groups', 'slab')), parts along dimension 0
There are 2 independent parts, one for each index of `groups`. A program takes and returns all parts, laid end to end along the dimension named above; each array names one. Nothing has to cross between parts.
Inputs may be any that keep to these rules, and one draw needn't show every extreme that they name: The magnitude of tilt is 64 or more, and exactly 64 for every image whose index is a multiple of 4; hence at most 32 pixel rows of one image have their plane among one slab device's planes, and some image reaches that.
All inputs are finite; a program needn't handle non-finite values.
Results may differ from a plain program's by a relative error of at most 0.0076.
Values may be sent and summed in bfloat16 or wider, within the bound.
No kernel may reach another device: no remote copies, remote signals or barrier semaphores. Data moves between devices by JAX's collectives and lax.ppermute only.
A program may use at most 192 MiB of HBM per device.

v0:
```python
import jax
import jax.numpy as jnp
from jax import lax
from jax.sharding import PartitionSpec as P

GRID = 256
COMPS = 6
TILE = 128


peer_block = 8


def shifted(value, axis, steps):
    count = lax.axis_size(axis)
    initial, last = (max(0, -steps), min(count, count - steps))
    return lax.ppermute(value, axis, [(source, source + steps) for source in range(initial, last)])


def solve_small(matrix, right_side):
    factor = jnp.linalg.cholesky(matrix)
    order = matrix.shape[-1]
    forward = []
    for row_at in range(order):
        total = right_side[..., row_at]
        for col_at in range(row_at):
            total = total - factor[..., row_at, col_at] * forward[col_at]
        forward.append(total / factor[..., row_at, row_at])
    backward = [None] * order
    for row_at in reversed(range(order)):
        total = forward[row_at]
        for col_at in range(row_at + 1, order):
            total = total - factor[..., col_at, row_at] * backward[col_at]
        backward[row_at] = total / factor[..., row_at, row_at]
    return jnp.stack(backward, axis=-1)


def solve_latents(gram, project, noise_var):
    count = GRID * GRID
    system = (
        gram[:, 1:, 1:] / count + noise_var[:, None, None] * jnp.eye(COMPS, dtype=jnp.float32)[None]
    )
    target = (project[:, 1:] - gram[:, 1:, 0]) / count
    return solve_small(system, target)


def geometry(tilt):
    half = GRID // 2
    position = jnp.arange(GRID, dtype=jnp.int32)
    numerator = (position[None, :] - half) * tilt[:, None]
    whole_part = jnp.floor_divide(numerator, half)
    return (half + whole_part, numerator - whole_part * half)


def interp_matrix(params):
    local_cell = jnp.arange(TILE, dtype=jnp.int32)
    source = local_cell[:, None]
    target = local_cell[None, :]
    offset = params[..., 0][..., None, None]
    weight = params[..., 1][..., None, None].astype(jnp.float32) / 16.0
    first_hit = (source == (target + offset) % TILE).astype(jnp.float32)
    second_hit = (source == (target + offset + 1) % TILE).astype(jnp.float32)
    return ((1.0 - weight) * first_hit + weight * second_hit).astype(jnp.bfloat16)


def slot_weights(slot_ints, planes_up, block_count):
    half = GRID // 2
    plane_at = slot_ints[..., 0]
    live_slot = plane_at >= 0
    depth = slot_ints[..., 1].astype(jnp.float32) / half
    place = slot_ints[..., 2] * planes_up + jnp.maximum(plane_at, 0)
    grid_cells = jnp.arange(block_count * planes_up, dtype=jnp.int32)
    low_hit = (grid_cells == place[..., None]).astype(jnp.float32)
    high_hit = (grid_cells == place[..., None] + 1).astype(jnp.float32)
    mixing = (1.0 - depth)[..., None] * low_hit + depth[..., None] * high_hit
    return jnp.where(live_slot[..., None], mixing, 0.0)


def grouped(member):
    return member.reshape((member.shape[0] // peer_block, peer_block) + member.shape[1:])


def ungrouped(member):
    return member.reshape((member.shape[0] * member.shape[1],) + member.shape[2:])


def extract_block(volume_table, slot_ints, params, planes_up, block_count):
    mixing = slot_weights(slot_ints, planes_up, block_count).astype(jnp.bfloat16)
    blended = jnp.einsum(
        "bisq,sqm->bism", mixing, volume_table, preferred_element_type=jnp.float32
    ).astype(jnp.bfloat16)
    blocks, image_count, slot_count, width = blended.shape
    tiles = blended.reshape(blocks, image_count, slot_count, COMPS + 1, GRID // TILE, TILE)
    matrix = interp_matrix(params)
    result = jnp.einsum("biskmc,bicx->biskmx", tiles, matrix, preferred_element_type=jnp.float32)
    return result.reshape(blocks, image_count, slot_count, COMPS + 1, GRID).astype(jnp.bfloat16)


def spread_block(carry, pieces, planes_up, block_count):
    totals, weights = carry
    slot_ints, params, residual, latent = pieces
    mixing = slot_weights(slot_ints, planes_up, block_count)
    matrix = interp_matrix(params)
    blocks, image_count, slot_count, cells = residual.shape
    tiles = residual.reshape(blocks, image_count, slot_count, GRID // TILE, TILE)
    spread = jnp.einsum("bisnx,bicx->bisnc", tiles, matrix, preferred_element_type=jnp.float32)
    spread = spread.reshape(blocks, image_count, slot_count, GRID)
    latent_float = latent.astype(jnp.float32)
    scaled = mixing[..., None] * latent_float[:, :, None, None, :]
    totals = totals + jnp.einsum(
        "bisqk,bisx->sqkx", scaled, spread, precision=lax.Precision.HIGHEST
    )
    power = jnp.sum(latent_float * latent_float, axis=2)
    weights = weights + jnp.einsum("bisq,bi->sq", mixing, power, precision=lax.Precision.HIGHEST)
    return ((totals, weights), None)


def local(mean_volume, components, images, tilt, shift, frac, noise_var):
    peers = lax.axis_size("slab")
    rows_local = mean_volume.shape[0]
    planes_local = rows_local // GRID
    planes_up = planes_local + 1
    slot_count = 2 * planes_local
    block_count = GRID // slot_count
    image_count = images.shape[0]
    plane, depth_count = geometry(tilt)
    owner = plane // planes_local
    peer_ids = jnp.arange(peers, dtype=jnp.int32)
    hits = (owner.reshape(image_count, block_count, slot_count)[..., None] == peer_ids).astype(
        jnp.int32
    )
    block_ids = jnp.arange(block_count, dtype=jnp.int32)[None, :, None, None]
    filled = jnp.sum(hits, axis=1)
    chosen_block = jnp.sum(hits * block_ids, axis=1)
    chosen_plane = jnp.sum(
        hits * plane.reshape(image_count, block_count, slot_count)[..., None], axis=1
    )
    chosen_depth = jnp.sum(
        hits * depth_count.reshape(image_count, block_count, slot_count)[..., None], axis=1
    )
    plane_at = jnp.where(filled > 0, chosen_plane - peer_ids[None, None, :] * planes_local, -1)
    slot_ints = jnp.transpose(
        jnp.stack([plane_at, chosen_depth, chosen_block], axis=-1), (2, 0, 1, 3)
    )
    image_ints = jnp.broadcast_to(jnp.stack([shift, frac], axis=-1)[None], (peers, image_count, 2))
    served_slots, served_params = (
        lax.all_to_all(slot_ints, "slab", split_axis=0, concat_axis=0, tiled=True),
        lax.all_to_all(image_ints, "slab", split_axis=0, concat_axis=0, tiled=True),
    )
    pixel_rows = jnp.einsum(
        "itsj,itsx->jisx",
        hits.astype(jnp.bfloat16),
        images.reshape(image_count, block_count, slot_count, GRID),
        preferred_element_type=jnp.float32,
    ).astype(jnp.bfloat16)
    volume = jnp.concatenate([mean_volume[None], components], axis=0)
    upper_plane = shifted(volume[:, :GRID], "slab", -1)
    extended = jnp.concatenate([volume, upper_plane], axis=1)
    volume_table = jnp.transpose(
        extended.reshape(COMPS + 1, planes_up, block_count, slot_count, GRID), (3, 2, 1, 0, 4)
    ).reshape(slot_count, block_count * planes_up, (COMPS + 1) * GRID)
    slices = ungrouped(
        lax.map(
            lambda pieces: extract_block(
                volume_table, pieces[0], pieces[1], planes_up, block_count
            ),
            (grouped(served_slots), grouped(served_params)),
        )
    )
    returned = lax.all_to_all(slices, "slab", split_axis=0, concat_axis=0, tiled=True)
    gram = jnp.einsum("jiskx,jislx->ikl", returned, returned, preferred_element_type=jnp.float32)
    project = jnp.einsum("jiskx,jisx->ik", returned, pixel_rows, preferred_element_type=jnp.float32)
    latent = solve_latents(gram, project, noise_var)
    latent_weight = latent.astype(jnp.bfloat16)
    coefficient = jnp.concatenate([jnp.ones((image_count, 1), jnp.bfloat16), latent_weight], axis=1)
    residual = (
        pixel_rows.astype(jnp.float32)
        - jnp.einsum("jiskx,ik->jisx", returned, coefficient, preferred_element_type=jnp.float32)
    ).astype(jnp.bfloat16)
    latent_copies = jnp.broadcast_to(latent_weight[None], (peers, image_count, COMPS))
    back_rows, back_latent = (
        lax.all_to_all(residual, "slab", split_axis=0, concat_axis=0, tiled=True),
        lax.all_to_all(latent_copies, "slab", split_axis=0, concat_axis=0, tiled=True),
    )
    start = (
        jnp.zeros((slot_count, block_count * planes_up, COMPS, GRID), jnp.float32),
        jnp.zeros((slot_count, block_count * planes_up), jnp.float32),
    )
    blocks_in = (
        grouped(served_slots),
        grouped(served_params),
        grouped(back_rows),
        grouped(back_latent),
    )
    (table_sums, table_weights), unused = lax.scan(
        lambda carry, pieces: spread_block(carry, pieces, planes_up, block_count), start, blocks_in
    )
    totals = jnp.transpose(
        table_sums.reshape(slot_count, block_count, planes_up, COMPS, GRID), (3, 2, 1, 0, 4)
    ).reshape(COMPS, planes_up * GRID, GRID)
    weights = jnp.transpose(
        table_weights.reshape(slot_count, block_count, planes_up), (2, 1, 0)
    ).reshape(planes_up * GRID)
    spill, spill_weight = (
        shifted(totals[:, rows_local:].astype(jnp.bfloat16), "slab", 1).astype(jnp.float32),
        shifted(weights[rows_local:].astype(jnp.bfloat16), "slab", 1).astype(jnp.float32),
    )
    totals = totals[:, :rows_local].at[:, :GRID].add(spill)
    weights = weights[:rows_local].at[:GRID].add(spill_weight)
    new_components = (totals / (1.0 + weights)[None, :, None]).astype(jnp.bfloat16)
    return (new_components, latent)


def solution(mesh):
    placed = (
        P(("groups", "slab"), None),
        P(None, ("groups", "slab"), None),
        P(("groups", "slab"), None, None),
        P(("groups", "slab")),
        P(("groups", "slab")),
        P(("groups", "slab")),
        P(("groups", "slab")),
    )
    return jax.shard_map(
        local,
        mesh=mesh,
        in_specs=placed,
        out_specs=(P(None, ("groups", "slab"), None), P(("groups", "slab"), None)),
        check_vma=False,
    )
```

profile of v0, /device:TPU:0, one launch (start us, length us, event | category | flops | bytes accessed | tf_op | source)
XLA Modules:
  0.0 546.7 jit_solution(1241154305409257302)
XLA Ops:
  2.0 7.4 %all-to-all-start.1 = ((s32[16,4,2]{1,2,0:T(2,128)}), s32[16,4,2]{1,2,0:T(2,128)S(1)}, u32[]{:S(2)}, u32[]{:S(2)}) async-start(s32[16,4,2]{1,2,0:T(2,128)} %broadcast_in_dim.107), calls=%async_computation.1 | async-start | bytes 32768 | tf_op jit(solution)/shard_map/all_to_all | solution.py:148
  9.4 2.3 pad_maximum_fusion.1
  11.7 1.3 collective-permute-start
  15.0 0.9 all-to-all-done.1
  15.9 6.8 %all-to-all-start = ((s32[16,1,384]{2,1,0:T(1,128)}), s32[16,1,384]{2,1,0:T(1,128)S(1)}, u32[]{:S(2)}, u32[]{:S(2)}) async-start(s32[16,1,384]{2,1,0:T(1,128)} %reshape.602), calls=%async_computation | async-start | bytes 49152 | tf_op jit(solution)/shard_map/all_to_all | solution.py:147
  22.8 7.5 %all-to-all-done = s32[16,1,384]{2,1,0:T(1,128)S(1)} async-done(((s32[16,1,384]{2,1,0:T(1,128)}), s32[16,1,384]{2,1,0:T(1,128)S(1)}, u32[]{:S(2)}, u32[]{:S(2)}) %all-to-all-start) | async-done | bytes 24608 | tf_op jit(solution)/shard_map/all_to_all | solution.py:147
  32.0 9.9 %pad_maximum_fusion = bf16[7,4352,256]{2,1,0:T(8,128)(2,1)S(1)} fusion(bf16[7,256,256]{2,1,0:T(8,128)(2,1)} %collective-permute-done, bf16[6,4096,256]{2,1,0:T(8,128)(2,1)} %param.16, bf16[1,4096,256]{2,1,0:T(8,128)(2,1)S(1)} %bitcast.244), kind=kLoop, calls=%fused_computation.105 | loop fusion | flops 46792704 | bytes 31195136 | tf_op jit(solution)/shard_map/concatenate | solution.py:158
  41.8 21.7 %copy.470 = bf16[7,17,8,32,256]{4,0,1,2,3:T(8,128)(2,1)} copy(bf16[7,17,8,32,256]{4,3,2,1,0:T(8,128)(2,1)S(1)} %bitcast.242) | data formatting | bytes 31195136 | tf_op jit(solution)/shard_map/reshape | solution.py:160
  63.6 29.7 %reshape.573 = bf16[32,136,1792]{2,1,0:T(8,128)(2,1)} reshape(bf16[32,8,17,7,256]{4,3,2,1,0:T(8,128)(2,1)} %bitcast.241) | data formatting | bytes 31195136 | tf_op jit(solution)/shard_map/reshape | solution.py:161
  93.3 58.0 %while.29 = (s32[]{:T(128)}, bf16[2,8,4,32,7,256]{5,3,4,2,1,0:T(8,128)(2,1)}, s32[2,8,4,32,3]{1,2,3,4,0:T(4,128)S(1)}, bf16[32,136,1792]{2,1,0:T(8,128)(2,1)}, s32[2,8,4,2]{1,2,3,0:T(4,128)S(1)}, /*index=5*/s32[]{:T(128)}) while((s32[]{:T(128)}, bf16[2,8,4,32,7,256]{5,3,4,2,1,0:T(8,128)(2,1)}, s32[2,8,4,32,3]{1,2,3,4,0:T(4,128)S(1)}, ...), condition=%wide.region_5.6_spmd, body=%wide.region_4.5_spmd.sunk | while | flops 976781440 | bytes 48771544 | solution.py:163
  94.3 6.8 %fusion.105 = bf16[32,8,4,1792]{3,1,2,0:T(8,128)(2,1)S(1)} fusion(bf16[32,136,1792]{2,1,0:T(8,128)(2,1)} %get-tuple-element.470, f32[8,4,32]{0,1,2:T(4,128)S(1)} %get-tuple-element.436, s32[8,4,32]{0,1,2:T(4,128)S(1)} %get-tuple-element.437, f32[8,4,32]{0,1,2:T(4,128)S(1)} %get-tuple-element.438, s32[8,4,32]{0,1,2:T(4,128)S(1)} %get-tuple-element.439, ...), kind=kOutput, calls=%fused_computation.2.clone.1 | convolution fusion | flops 501932032 | bytes 19284992 | tf_op jit(solution)/shard_map/while/body/eval_jaxpr/bisq,sqm->bism/dot_general | solution.py:89
  101.1 4.4 fusion.107
  105.5 5.7 %copy.487 = bf16[8,4,32,7,2,128]{5,4,2,3,1,0:T(2,128)(2,1)} copy(bf16[8,4,32,7,2,128]{5,2,4,3,1,0:T(8,128)(2,1)S(1)} %fusion.107) | data formatting | bytes 7340032 | tf_op jit(solution)/shard_map/while/body/eval_jaxpr/convert_element_type | solution.py:96
  111.2 7.0 %convert_element_type.255 = bf16[1,8,4,32,7,256]{5,3,4,2,1,0:T(8,128)(2,1)} reshape(bf16[8,4,32,7,2,128]{5,4,2,3,1,0:T(2,128)(2,1)} %copy.487) | data formatting | bytes 7340032 | tf_op jit(solution)/shard_map/while/body/eval_jaxpr/convert_element_type | solution.py:96
  118.2 4.4 constant_dynamic-update-slice_fusion.2
  123.0 6.8 %fusion.105 = bf16[32,8,4,1792]{3,1,2,0:T(8,128)(2,1)S(1)} fusion(bf16[32,136,1792]{2,1,0:T(8,128)(2,1)} %get-tuple-element.470, f32[8,4,32]{0,1,2:T(4,128)S(1)} %get-tuple-element.436, s32[8,4,32]{0,1,2:T(4,128)S(1)} %get-tuple-element.437, f32[8,4,32]{0,1,2:T(4,128)S(1)} %get-tuple-element.438, s32[8,4,32]{0,1,2:T(4,128)S(1)} %get-tuple-element.439, ...), kind=kOutput, calls=%fused_computation.2.clone.1 | convolution fusion | flops 501932032 | bytes 19284992 | tf_op jit(solution)/shard_map/while/body/eval_jaxpr/bisq,sqm->bism/dot_general | solution.py:89
  129.9 4.4 fusion.107
  134.3 5.7 %copy.487 = bf16[8,4,32,7,2,128]{5,4,2,3,1,0:T(2,128)(2,1)} copy(bf16[8,4,32,7,2,128]{5,2,4,3,1,0:T(8,128)(2,1)S(1)} %fusion.107) | data formatting | bytes 7340032 | tf_op jit(solution)/shard_map/while/body/eval_jaxpr/convert_element_type | solution.py:96
  140.0 7.0 %convert_element_type.255 = bf16[1,8,4,32,7,256]{5,3,4,2,1,0:T(8,128)(2,1)} reshape(bf16[8,4,32,7,2,128]{5,4,2,3,1,0:T(2,128)(2,1)} %copy.487) | data formatting | bytes 7340032 | tf_op jit(solution)/shard_map/while/body/eval_jaxpr/convert_element_type | solution.py:96
  146.9 4.4 constant_dynamic-update-slice_fusion.2
  151.3 4.9 all-to-all-start.2
  156.3 1.0 convolution_convert_fusion
  157.3 131.2 %all-to-all-done.2 = bf16[16,4,32,7,256]{4,2,3,1,0:T(8,128)(2,1)} async-done(((bf16[16,4,32,7,256]{4,2,3,1,0:T(8,128)(2,1)}), bf16[16,4,32,7,256]{4,2,3,1,0:T(8,128)(2,1)}, u32[]{:S(2)}, u32[]{:S(2)}) %all-to-all-start.2) | async-done | bytes 7340064 | tf_op jit(solution)/shard_map/all_to_all | solution.py:170
  288.6 13.9 %fusion.66 = f32[4,7,7]{1,2,0:T(8,128)S(1)} fusion(bf16[16,4,32,7,256]{4,2,3,1,0:T(8,128)(2,1)} %all-to-all-done.2), kind=kOutput, calls=%fused_computation.119 | convolution fusion | flops 51380224 | bytes 7340816 | tf_op jit(solution)/shard_map/jiskx,jislx->ikl/dot_general | solution.py:171
  302.8 2.4 custom-call.4
  305.6 10.2 %fusion.59 = f32[4,1,7,1,1]{2,1,4,3,0:T(1,128)S(1)} fusion(bf16[16,4,32,7,256]{4,2,3,1,0:T(8,128)(2,1)} %all-to-all-done.2, bf16[16,4,32,256,1]{3,0,2,1,4:T(8,128)(2,1)S(1)} %bitcast.246), kind=kOutput, calls=%fused_computation.108 | convolution fusion | flops 7340032 | bytes 8388720 | tf_op jit(solution)/shard_map/jiskx,jisx->ik/dot_general | solution.py:172
  316.9 32.2 %all-to-all-start.3 = ((bf16[16,4,6]{2,1,0:T(4,128)(2,1)}), bf16[16,4,6]{2,1,0:T(4,128)(2,1)S(1)}, u32[]{:S(2)}, u32[]{:S(2)}) async-start(bf16[16,4,6]{2,1,0:T(4,128)(2,1)} %broadcast_in_dim.109), calls=%async_computation.3 | async-start | bytes 32768 | tf_op jit(solution)/shard_map/all_to_all | solution.py:183
  349.1 8.0 %fusion.57 = f32[4,1,16,32,256]{4,1,3,2,0:T(1,128)S(1)} fusion(bf16[16,4,32,7,256]{4,2,3,1,0:T(8,128)(2,1)} %all-to-all-done.2, bf16[4,7,1,1,1]{1,0,2,3,4:T(4,128)(2,1)S(1)} %pad_bitcast_fusion), kind=kOutput, calls=%fused_computation.106 | convolution fusion | flops 7340032 | bytes 9437240 | tf_op jit(solution)/shard_map/jiskx,ik->jisx/dot_general | solution.py:178
  357.1 1.4 fusion.63
  358.6 1.3 copy.418
  359.9 6.3 %all-to-all-start.4 = ((bf16[16,4,32,256]{3,2,1,0:T(8,128)(2,1)}), bf16[16,4,32,256]{3,2,1,0:T(8,128)(2,1)}, u32[]{:S(2)}, u32[]{:S(2)}) async-start(bf16[16,4,32,256]{3,2,1,0:T(8,128)(2,1)} %copy.418), calls=%async_computation.4 | async-start | bytes 2097152 | tf_op jit(solution)/shard_map/all_to_all | solution.py:182
  366.4 22.8 %all-to-all-done.4 = bf16[16,4,32,256]{3,2,1,0:T(8,128)(2,1)} async-done(((bf16[16,4,32,256]{3,2,1,0:T(8,128)(2,1)}), bf16[16,4,32,256]{3,2,1,0:T(8,128)(2,1)}, u32[]{:S(2)}, u32[]{:S(2)}) %all-to-all-start.4) | async-done | bytes 1048608 | tf_op jit(solution)/shard_map/all_to_all | solution.py:182
  389.2 72.7 %while.30 = (s32[]{:T(128)}, f32[32,136,6,256]{3,1,2,0:T(8,128)}, f32[32,136]{1,0:T(8,128)S(1)}, s32[2,8,4,32,3]{1,2,3,4,0:T(4,128)S(1)}, bf16[2,8,4,6]{1,2,3,0:...) while((s32[]{:T(128)}, f32[32,136,6,256]{3,1,2,0:T(8,128)}, ...), condition=%wide.region_10.11_spmd.clone, body=%wide.region_8.10_spmd.clone.sunk | while | flops 2654831872 | bytes 63737856 | solution.py:195
  389.7 1.5 fusion.116
  391.2 1.1 constant_dynamic-slice_fusion.2
  395.8 28.7 %bitcast_add_fusion.5 = f32[32,136,6,256]{3,1,2,0:T(8,128)} fusion(f32[32,136,6,256]{3,1,2,0:T(8,128)} %get-tuple-element.483, pred[]{:T(512)S(6)} %compare.47, f32[8,4,6]{0,1,2:T(4,128)S(1)} %bitcast_convert_fusion.2, f32[8,4,32,136]{3,0,1,2:T(8,128)S(1)} %add_select_fusion.14, f32[8,4,32,256,1]{3,0,1,2,4:T(8,128)S(1)} %reshape.607), kind=kOutput, calls=%fused_computation.52.clone.1 | convolution fusion | flops 2581118976 | bytes 55083776 | tf_op jit(solution)/shard_map/while/body/eval_jaxpr/bisqk,bisx->sqkx/dot_general | solution.py:110
  425.0 1.5 fusion.116
  426.5 1.1 constant_dynamic-slice_fusion.2
  427.7 0.9 fusion.115
  431.0 30.9 %bitcast_add_fusion.5 = f32[32,136,6,256]{3,1,2,0:T(8,128)} fusion(f32[32,136,6,256]{3,1,2,0:T(8,128)} %get-tuple-element.483, pred[]{:T(512)S(6)} %compare.47, f32[8,4,6]{0,1,2:T(4,128)S(1)} %bitcast_convert_fusion.2, f32[8,4,32,136]{3,0,1,2:T(8,128)S(1)} %add_select_fusion.14, f32[8,4,32,256,1]{3,0,1,2,4:T(8,128)S(1)} %reshape.607), kind=kOutput, calls=%fused_computation.52.clone.1 | convolution fusion | flops 2581118976 | bytes 55083776 | tf_op jit(solution)/shard_map/while/body/eval_jaxpr/bisqk,bisx->sqkx/dot_general | solution.py:110
  461.9 24.5 %copy.422 = f32[32,136,6,256]{3,0,2,1:T(8,128)} copy(f32[32,136,6,256]{3,1,2,0:T(8,128)} %get-tuple-element.184) | data formatting | bytes 53477376 | tf_op jit(solution)/shard_map/while | solution.py:195
  486.4 10.7 %copy.423 = f32[6,17,8,32,256]{4,3,2,1,0:T(8,128)S(1)} copy(f32[6,17,8,32,256]{4,3,0,1,2:T(8,128)} %bitcast.240) | data formatting | bytes 53477376 | tf_op jit(solution)/shard_map/transpose | solution.py:198
  497.1 8.8 %copy-done.2 = f32[6,17,8,32,256]{4,3,2,1,0:T(8,128)} copy-done((f32[6,17,8,32,256]{4,3,2,1,0:T(8,128)}, f32[6,17,8,32,256]{4,3,2,1,0:T(8,128)S(1)}, u32[]{:S(2)}) %copy-start.2) | copy-done | bytes 26738712
  506.0 2.6 collective-permute-start.1
  509.0 3.2 collective-permute-start.2
  512.2 16.8 %slice.315 = f32[6,4096,256]{2,1,0:T(8,128)} slice(f32[6,4352,256]{2,1,0:T(8,128)} %bitcast.238), slice={[0:6], [0:4096], [0:256]} | slice | bytes 50331648 | tf_op jit(solution)/shard_map/slice | solution.py:208
  529.5 2.7 fusion.65
  532.2 14.1 %divide_convert_fusion = bf16[6,4096,256]{2,1,0:T(8,128)(2,1)} fusion(f32[6,4096,256]{2,1,0:T(8,128)} %fusion.65, f32[4096]{0:T(1024)S(1)} %broadcast_add_fusion.1), kind=kLoop, calls=%fused_computation.103 | loop fusion | flops 12582912 | bytes 37765120 | tf_op jit(solution)/shard_map/convert_element_type | solution.py:210
  (131 shorter events, 15.8 us)
Async XLA Ops:
  0.6 155.7 %copy-start = (bf16[4,256,256]{2,1,0:T(8,128)(2,1)S(1)}, bf16[4,256,256]{2,1,0:T(8,128)(2,1)}, u32[]{:S(2)}) copy-start(bf16[4,256,256]{2,1,0:T(8,128)(2,1)} %param.17) | copy-start | bytes 1572868
  2.0 13.9 %all-to-all-start.1 = ((s32[16,4,2]{1,2,0:T(2,128)}), s32[16,4,2]{1,2,0:T(2,128)S(1)}, u32[]{:S(2)}, u32[]{:S(2)}) async-start(s32[16,4,2]{1,2,0:T(2,128)} %broadcast_in_dim.107), calls=%async_computation.1 | async-start | bytes 32768 | tf_op jit(solution)/shard_map/all_to_all | solution.py:148
  9.4 3.6 copy-start.6
  9.4 22.5 %copy-start.3 = (bf16[4096,256]{1,0:T(8,128)(2,1)S(1)}, bf16[4096,256]{1,0:T(8,128)(2,1)}, u32[]{:S(2)}) copy-start(bf16[4096,256]{1,0:T(8,128)(2,1)} %param.15) | copy-start | bytes 6291460
  11.7 20.2 %collective-permute-start = (bf16[7,256,256]{2,1,0:T(8,128)(2,1)}, bf16[7,256,256]{2,1,0:T(8,128)(2,1)}, u32[]{:S(2)}, u32[]{:S(2)}) collective-permute-start(bf16[7,256,256]{2,1,0:T(8,128)(2,1)} %pad_maximum_fusion.1), channel_id=1, source_target_pairs={{1,0},{2,1},{3,2},{4,3},{5,4},{6,5},{7,6},{8,7},{9,8},{10,9},{11,1... | collective-permute-start | bytes 2752520 | tf_op jit(solution)/shard_map/ppermute | solution.py:17
  15.9 14.4 %all-to-all-start = ((s32[16,1,384]{2,1,0:T(1,128)}), s32[16,1,384]{2,1,0:T(1,128)S(1)}, u32[]{:S(2)}, u32[]{:S(2)}) async-start(s32[16,1,384]{2,1,0:T(1,128)} %reshape.602), calls=%async_computation | async-start | bytes 49152 | tf_op jit(solution)/shard_map/all_to_all | solution.py:147
  151.3 137.2 %all-to-all-start.2 = ((bf16[16,4,32,7,256]{4,2,3,1,0:T(8,128)(2,1)}), bf16[16,4,32,7,256]{4,2,3,1,0:T(8,128)(2,1)}, u32[]{:S(2)}, u32[]{:S(2)}) async-start(bf16[16,4,32,7,256]{4,2,3,1,0:T(8,128)(2,1)} %bitcast.245), calls=%async_computation.2 | async-start | bytes 14680064 | tf_op jit(solution)/shard_map/all_to_all | solution.py:170
  156.2 146.4 %copy-start.5 = (f32[4]{0:T(128)S(1)}, f32[4]{0:T(128)}, u32[]{:S(2)}) copy-start(f32[4]{0:T(128)} %param.21) | copy-start | bytes 52
  316.2 0.7 copy-start.4
  316.9 43.0 %all-to-all-start.3 = ((bf16[16,4,6]{2,1,0:T(4,128)(2,1)}), bf16[16,4,6]{2,1,0:T(4,128)(2,1)S(1)}, u32[]{:S(2)}, u32[]{:S(2)}) async-start(bf16[16,4,6]{2,1,0:T(4,128)(2,1)} %broadcast_in_dim.109), calls=%async_computation.3 | async-start | bytes 32768 | tf_op jit(solution)/shard_map/all_to_all | solution.py:183
  359.9 29.3 %all-to-all-start.4 = ((bf16[16,4,32,256]{3,2,1,0:T(8,128)(2,1)}), bf16[16,4,32,256]{3,2,1,0:T(8,128)(2,1)}, u32[]{:S(2)}, u32[]{:S(2)}) async-start(bf16[16,4,32,256]{3,2,1,0:T(8,128)(2,1)} %copy.418), calls=%async_computation.4 | async-start | bytes 2097152 | tf_op jit(solution)/shard_map/all_to_all | solution.py:182
  497.1 8.8 %copy-start.2 = (f32[6,17,8,32,256]{4,3,2,1,0:T(8,128)}, f32[6,17,8,32,256]{4,3,2,1,0:T(8,128)S(1)}, u32[]{:S(2)}) copy-start(f32[6,17,8,32,256]{4,3,2,1,0:T(8,128)S(1)} %copy.423) | copy-start | bytes 80216064
  506.0 23.5 %collective-permute-start.1 = (bf16[6,256,256]{2,1,0:T(8,128)(2,1)S(1)}, bf16[6,256,256]{2,1,0:T(8,128)(2,1)S(1)}, u32[]{:S(2)}, u32[]{:S(2)}) collective-permute-start(bf16[6,256,256]{2,1,0:T(8,128)(2,1)S(1)} %slice.393), channel_id=1, source_target_pairs={{0,1},{1,2},{2,3},{3,4},{4,5},{5,6},{6,7},{7,8},{8,9},{9,10},{10,1... | collective-permute-start | bytes 2359304 | tf_op jit(solution)/shard_map/ppermute | solution.py:17
  509.0 20.4 %collective-permute-start.2 = (bf16[256]{0:T(256)(128)(2,1)S(1)}, bf16[256]{0:T(256)(128)(2,1)S(1)}, u32[]{:S(2)}, u32[]{:S(2)}) collective-permute-start(bf16[256]{0:T(256)(128)(2,1)S(1)} %convert_element_type.176), channel_id=1, source_target_pairs={{0,1},{1,2},{2,3},{3,4},{4,5},{5,6},{6,7},{7,8},{8,9},{9,10},{10,1... | collective-permute-start | bytes 1544 | tf_op jit(solution)/shard_map/ppermute | solution.py:17
  532.2 14.1 %copy-start.1 = (bf16[4,256,256]{2,1,0:T(8,128)(2,1)S(1)}, bf16[4,256,256]{2,1,0:T(8,128)(2,1)}, u32[]{:S(2)}) copy-start(bf16[4,256,256]{2,1,0:T(8,128)(2,1)} %param.17) | copy-start | bytes 1572868
where the time goes:
time: 554 us; the launch traced here: 547 us
  waiting for transfers between devices  162 us (29%)
  local copies, waits for them, and re-layouts  159 us (29%)
  matrix products  120 us (22%)
  starting transfers between devices  64.6 us (12%)
  other arithmetic  38.4 us (7%)
    all_to_all x1, waiting for transfers between devices, local(): lax.all_to_all(slices, 'slab', split_axis=0, concat_axis=0, tiled=True)  131 us
    dot_general x2, matrix products, spread_block(): jnp.einsum('bisqk,bisx->sqkx', scaled, spread, precision=lax.Precision.HI...  59.6 us
    all_to_all x1, starting transfers between devices, local(): lax.all_to_all(latent_copies, 'slab', split_axis=0, concat_axis=0, tiled=...  32.2 us
    reshape x1, local copies, waits for them, and re-layouts, local(): volume_table = jnp.transpose(extended.reshape(COMPS + 1, planes_up, block...  29.7 us
    convert_element_type x4, local copies, waits for them, and re-layouts, extract_block(): result.reshape(blocks, image_count, slot_count, COMPS + 1, GRID)  25.3 us
    while x1, local copies, waits for them, and re-layouts, local(): lax.scan(lambda carry, pieces: spread_block(carry, pieces, planes_up, blo...  24.5 us
    all_to_all x1, waiting for transfers between devices, local(): lax.all_to_all(residual, 'slab', split_axis=0, concat_axis=0, tiled=True)  22.8 us
    reshape x1, local copies, waits for them, and re-layouts, local(): extended.reshape(COMPS + 1, planes_up, block_count, slot_count, GRID)  21.7 us
  transfers between devices with their start and end apart: 8, of which 4 were waited for; matrix products, arithmetic and copies ran while one was open for 7% of the time, Pallas kernels for 0%

commit v1 on v0

v1 whole, which is shorter than its diff:
```python
import functools

import jax
import jax.numpy as jnp
from jax import lax
from jax.experimental import pallas as pl
from jax.experimental.pallas import tpu as pltpu
from jax.sharding import PartitionSpec as P

GRID = 256
HALF = GRID // 2
COMPS = 6
CHANS = COMPS + 1
TILE = 128
LANES = 128
PAIRS = [(k, l) for k in range(CHANS) for l in range(k, CHANS)]
PROJECT_AT = len(PAIRS)
VMEM = 56 * 1024 * 1024

f32 = jnp.float32
bf16 = jnp.bfloat16
i32 = jnp.int32


def iota(shape, dim):
    return lax.broadcasted_iota(i32, shape, dim)


def dot(a, b):
    return jnp.dot(a, b, preferred_element_type=f32)


def params():
    return pltpu.CompilerParams(vmem_limit_bytes=VMEM)


def plane_depth(position, tilt):
    numerator = (position - HALF) * tilt
    return jnp.right_shift(numerator, 7) + HALF, jnp.bitwise_and(numerator, HALF - 1)


def pack_kernel(sizes, tilt_ref, image_ref, out_ref):
    planes, slots, peers, count = sizes
    rows = count * slots + 2 * count
    lane = iota((1, count * GRID), 1)
    tilt = jnp.full((1, count * GRID), tilt_ref[0], i32)
    for image in range(1, count):
        tilt = jnp.where(lane >= image * GRID, tilt_ref[image], tilt)
    plane, _ = plane_depth(jnp.bitwise_and(lane, GRID - 1), tilt)
    main_shape = (count * slots, count * GRID)
    row, col = iota(main_shape, 0), iota(main_shape, 1)
    main_hit = (row // slots == col // GRID) & (row % slots == col % slots)
    extra_shape = (2 * count, count * GRID)
    row, col = iota(extra_shape, 0), iota(extra_shape, 1)
    extra_hit = (row // 2 == col // GRID) & (row % 2 == col % 2)
    main_plane = jnp.where(main_hit, plane, -1000)
    extra_plane = jnp.where(extra_hit, plane, -1000)
    picture = image_ref[...]
    for peer in range(peers):
        first = peer * planes
        main = jnp.where((main_plane >= first) & (main_plane < first + planes), 1.0, 0.0)
        extra = jnp.where(extra_plane == first - 1, 1.0, 0.0)
        hit = jnp.concatenate([main, extra], axis=0).astype(bf16)
        out_ref[peer] = dot(hit, picture).astype(bf16)


def slot_order(slots, blocks):
    row, col = iota((GRID, GRID), 0), iota((GRID, GRID), 1)
    return (col == (row % blocks) * slots + row // blocks).astype(f32).astype(bf16)


def table_kernel(sizes, mean_ref, comp_ref, out_ref, order_ref):
    planes, slots, blocks, chunk = sizes

    @pl.when(pl.program_id(0) == 0)
    def _():
        order_ref[...] = slot_order(slots, blocks)

    order = order_ref[...]
    for chan in range(CHANS):
        pieces = []
        for at in range(chunk):
            span = slice(at * GRID, (at + 1) * GRID)
            plane = mean_ref[span, :] if chan == 0 else comp_ref[chan - 1, span, :]
            pieces.append(dot(order, plane).reshape(slots, blocks, GRID))
        both = jnp.concatenate(pieces, axis=1).astype(bf16)
        out_ref[:, :, chan * GRID : (chan + 1) * GRID] = both


def interpolate(rows, index, weight):
    parts = []
    for at in range(GRID // TILE):
        part = rows[:, at * TILE : (at + 1) * TILE]
        mixed = (1.0 - weight) * part + weight * pltpu.roll(part, TILE - 1, 1)
        parts.append(jnp.take_along_axis(mixed, index, axis=1, mode="promise_in_bounds"))
    return parts


def extract_kernel(
    sizes, first_ref, tilt_ref, shift_ref, frac_ref, table_ref, up_ref, low_ref, mean_ref, comp_ref,
    out_ref, extra_ref, gram_ref, upper_ref, sums_ref,
):
    planes, slots, blocks, chunk, images = sizes
    step, first = pl.program_id(0), first_ref[0]
    tilt = tilt_ref[...]
    weight = frac_ref[...].astype(f32) / 16.0
    index = jnp.bitwise_and(iota((images, TILE), 1) + shift_ref[...], TILE - 1)
    upper_rows = upper_ref.shape[1]

    @pl.when(step == 0)
    def _():
        order = slot_order(slots, blocks)
        lane = iota((images, GRID), 1)
        plane, depth = plane_depth(lane, tilt)
        depth = depth.astype(f32) / HALF
        below = plane == first - 1
        parts = []
        for odd in range(2):
            hit = below & (jnp.bitwise_and(lane, 1) == odd)
            low, high = jnp.where(hit, 1.0 - depth, 0.0), jnp.where(hit, depth, 0.0)
            parts.append(jnp.concatenate([low, high], axis=1))
        mixing = jnp.concatenate(parts, axis=0).astype(bf16)
        index2 = jnp.concatenate([index, index], axis=0)
        weight2 = jnp.concatenate([weight, weight], axis=0)
        for chan in range(CHANS):
            at = slice(chan * GRID, (chan + 1) * GRID)
            upper = dot(order, up_ref[chan]).reshape(slots, blocks, GRID)
            if upper_rows > blocks:
                fill = jnp.zeros((slots, upper_rows - blocks, GRID), f32)
                upper = jnp.concatenate([upper, fill], axis=1)
            upper_ref[:, :, at] = upper.astype(bf16)
            own = mean_ref[...] if chan == 0 else comp_ref[chan - 1]
            blended = dot(mixing[:, :GRID], low_ref[chan]) + dot(mixing[:, GRID:], own)
            parts = interpolate(blended.astype(bf16).astype(f32), index2, weight2)
            extra_ref[:, at] = jnp.concatenate(parts, axis=1).astype(bf16)
        sums_ref[...] = jnp.zeros_like(sums_ref)

    lane = iota((images, planes * blocks), 1)
    block_at, plane_at = lane % blocks, lane // blocks
    lane_up = iota((images, upper_rows), 1)
    for at in range(chunk):
        slot = step * chunk + at
        plane, depth = plane_depth(block_at * slots + slot, tilt)
        plane = plane - first
        low = jnp.where(plane == plane_at, HALF - depth, 0)
        high = jnp.where((plane + 1 == plane_at) & (plane_at > 0), depth, 0)
        mixing = ((low + high).astype(f32) / HALF).astype(bf16)
        plane, depth = plane_depth(lane_up * slots + slot, tilt)
        hit = (plane - first == planes - 1) & (lane_up < blocks)
        mixing_up = (jnp.where(hit, depth, 0).astype(f32) / HALF).astype(bf16)
        for chan in range(CHANS):
            span = slice(chan * GRID, (chan + 1) * GRID)
            blended = dot(mixing, table_ref[at, :, span]) + dot(mixing_up, upper_ref[slot, :, span])
            parts = interpolate(blended.astype(bf16).astype(f32), index, weight)
            out_ref[at, :, span] = jnp.concatenate(parts, axis=1).astype(bf16)

    def accumulate(group, carry):
        rows = pl.ds(pl.multiple_of(group * 16, 16), 16)
        sums = [sums_ref[n, rows, :] for n in range(len(PAIRS))]
        for at in range(chunk):
            for tile in range(GRID // LANES):
                values = [
                    out_ref[at, rows, pl.ds(chan * GRID + tile * LANES, LANES)].astype(f32)
                    for chan in range(CHANS)
                ]
                for n, (k, l) in enumerate(PAIRS):
                    sums[n] = sums[n] + values[k] * values[l]
        for n in range(len(PAIRS)):
            sums_ref[n, rows, :] = sums[n]
        return carry

    lax.fori_loop(0, images // 16, accumulate, 0)

    @pl.when(step == pl.num_programs(0) - 1)
    def _():
        lane = iota((images, LANES), 1)
        total = jnp.zeros((images, LANES), f32)
        for n in range(len(PAIRS)):
            total = jnp.where(lane == n, jnp.sum(sums_ref[n], axis=1, keepdims=True), total)
        gram_ref[...] = total


def project_kernel(
    sizes, got_ref, slice_ref, gram_ref, rows_ref, extra_ref, total_ref, wide_ref, sums_ref
):
    slots, chunk, images, peers, count = sizes
    stride = count * slots + 2 * count
    step = pl.program_id(0)

    @pl.when(step == 0)
    def _():
        for tile in range(GRID // LANES):
            wide_ref[tile] = got_ref[:, tile * LANES : (tile + 1) * LANES].astype(f32)
        sums_ref[...] = jnp.zeros_like(sums_ref)
        for odd in range(2):
            for image in range(count):
                start = count * slots + image * 2 + odd
                at = (odd * count + image) * peers
                for tile in range(GRID // LANES):
                    part = wide_ref[tile, pl.ds(start, peers, stride=stride), :]
                    extra_ref[at : at + peers, tile * LANES : (tile + 1) * LANES] = part.astype(bf16)

    for image in range(count):
        span = slice(image * peers, (image + 1) * peers)
        sums = [sums_ref[chan, span, :] for chan in range(CHANS)]
        for at in range(chunk):
            slot = step * chunk + at
            for tile in range(GRID // LANES):
                part = wide_ref[tile, pl.ds(image * slots + slot, peers, stride=stride), :]
                rows_ref[at, span, tile * LANES : (tile + 1) * LANES] = part.astype(bf16)
                for chan in range(CHANS):
                    lanes = slice(chan * GRID + tile * LANES, chan * GRID + (tile + 1) * LANES)
                    sums[chan] = sums[chan] + part * slice_ref[at, span, lanes].astype(f32)
        for chan in range(CHANS):
            sums_ref[chan, span, :] = sums[chan]

    @pl.when(step == pl.num_programs(0) - 1)
    def _():
        lane = iota((images, LANES), 1)
        total = gram_ref[...]
        for chan in range(CHANS):
            value = jnp.sum(sums_ref[chan], axis=1, keepdims=True)
            total = jnp.where(lane == PROJECT_AT + chan, value, total)
        total_ref[...] = total


def solve_rows(table, noise):
    count = float(GRID * GRID)

    def gram(k, l):
        at = PAIRS.index((min(k, l), max(k, l)))
        return table[at : at + 1, :]

    factor = [[None] * COMPS for _ in range(COMPS)]
    inverse = [None] * COMPS
    for col in range(COMPS):
        for row in range(col, COMPS):
            total = gram(row + 1, col + 1) / count
            if row == col:
                total = total + noise
            for at in range(col):
                total = total - factor[row][at] * factor[col][at]
            if row == col:
                inverse[col] = 1.0 / jnp.sqrt(total)
            else:
                factor[row][col] = total * inverse[col]
    forward = []
    for row in range(COMPS):
        at = PROJECT_AT + row + 1
        total = (table[at : at + 1, :] - gram(row + 1, 0)) / count
        for col in range(row):
            total = total - factor[row][col] * forward[col]
        forward.append(total * inverse[row])
    latent = [None] * COMPS
    for row in reversed(range(COMPS)):
        total = forward[row]
        for col in range(row + 1, COMPS):
            total = total - factor[col][row] * latent[col]
        latent[row] = total * inverse[row]
    return latent


def back_kernel(
    sizes, first_ref, total_ref, noise_ref, tilt_row_ref, tilt_ref, shift_ref, frac_ref,
    slice_ref, rows_ref, slice_extra_ref, rows_extra_ref,
    out_ref, latent_ref, stack_ref, row_ref, col_ref, spill_ref, order_ref,
):
    planes, slots, blocks, chunk, images, steps, out_planes = sizes
    step, first = pl.program_id(0), first_ref[0]

    @pl.when(step == 0)
    def _():
        table = jnp.transpose(total_ref[...])
        latent = solve_rows(table, noise_ref[...])
        fill = [jnp.zeros((1, images), f32)] * (8 - COMPS)
        latent_ref[...] = jnp.concatenate(latent + fill, axis=0)
        rounded = [value.astype(bf16).astype(f32) for value in latent]
        power = rounded[0] * rounded[0]
        for value in rounded[1:]:
            power = power + value * value
        rows = jnp.concatenate(rounded + [power, fill[0]], axis=0)
        row_ref[...] = jnp.concatenate([rows, rows, rows], axis=1)
        wide = jnp.concatenate([rows, jnp.zeros((LANES - 8, images), f32)], axis=0)
        col_ref[...] = jnp.transpose(wide)
        row, col = iota((GRID, GRID), 0), iota((GRID, GRID), 1)
        order_ref[...] = (row == (col % blocks) * slots + col // blocks).astype(f32).astype(bf16)

    def spread(slices, rows, copies):
        weight = frac_ref[...].astype(f32) / 16.0
        index = jnp.bitwise_and(iota((images, TILE), 1) - shift_ref[...], TILE - 1)
        latent = col_ref[...]
        if copies > 1:
            weight = jnp.concatenate([weight] * copies, axis=0)
            index = jnp.concatenate([index] * copies, axis=0)
            latent = jnp.concatenate([latent] * copies, axis=0)
        residual = rows[...].astype(f32) - slices[:, :GRID].astype(f32)
        for k in range(COMPS):
            span = slice((k + 1) * GRID, (k + 2) * GRID)
            residual = residual - latent[:, k : k + 1] * slices[:, span].astype(f32)
        residual = residual.astype(bf16).astype(f32)
        parts = []
        for at in range(GRID // TILE):
            part = residual[:, at * TILE : (at + 1) * TILE]
            mixed = (1.0 - weight) * part + weight * pltpu.roll(part, 1, 1)
            parts.append(jnp.take_along_axis(mixed, index, axis=1, mode="promise_in_bounds"))
        return jnp.concatenate(parts, axis=1)

    @pl.when(step == 0)
    def _():
        value = spread(slice_extra_ref, rows_extra_ref, 2)
        plane, depth = plane_depth(iota((images, GRID), 1), tilt_ref[...])
        odd = jnp.bitwise_and(iota((images, GRID), 1), 1)
        parts = []
        for at in range(2):
            hit = (plane == first - 1) & (odd == at)
            parts.append(jnp.sum(jnp.where(hit, depth, 0).astype(f32), axis=1, keepdims=True) / HALF)
        spill_ref[...] = (jnp.concatenate(parts, axis=0) * value).astype(bf16)

    @pl.when(step < steps)
    def _():
        tilt = tilt_row_ref[...]
        shape = (planes * blocks, 3 * images)
        row, lane = iota(shape, 0), iota(shape, 1)
        plane_at, block_at = row // blocks, row % blocks
        own = lane < 2 * images
        low = lane < images
        wanted = jnp.where(low, plane_at, plane_at - 1)
        wanted = jnp.where(own & (wanted < 0), -1000, wanted)
        wanted = jnp.where(own | (wanted < 0), wanted, -1000)
        power = row_ref[COMPS : COMPS + 1, :]
        lane_slot = iota((images, LANES), 1)
        group = 2 if blocks % 16 else 1
        for start in range(0, chunk, group):
            pieces = [[] for _ in range(COMPS)]
            for at in range(start, start + group):
                slot = step * chunk + at
                value = spread(slice_ref.at[at], rows_ref.at[at], 1)
                plane, depth = plane_depth(lane_slot * slots + slot, tilt_ref[...])
                plane = plane - first
                live = (plane >= 0) & (plane < planes) & (lane_slot < blocks)
                depth = jnp.sum(jnp.where(live, depth, 0).astype(f32), axis=1, keepdims=True) / HALF
                odd = (slot % 2) * images
                spill = spill_ref[pl.ds(pl.multiple_of(odd, 16), images), :]
                right = jnp.concatenate(
                    [((1.0 - depth) * value).astype(bf16), (depth * value).astype(bf16), spill], axis=0
                )
                plane, depth = plane_depth(block_at * slots + slot, tilt)
                hit = plane - first == wanted
                part = jnp.where(low, HALF - depth, depth).astype(f32) / HALF
                weight = jnp.sum(jnp.where(hit, part * power, 0.0), axis=1, keepdims=True)
                scale = 1.0 / (1.0 + weight)
                for k in range(COMPS):
                    left = jnp.where(hit, row_ref[k : k + 1, :], 0.0).astype(bf16)
                    total = dot(left, right) * scale
                    pieces[k].append(total.reshape(planes, blocks, GRID))
            rows = pl.ds(pl.multiple_of((step * chunk + start) * blocks, 16), group * blocks)
            for k in range(COMPS):
                stack_ref[k, :, rows, :] = jnp.concatenate(pieces[k], axis=1).astype(bf16)

    @pl.when(step >= steps)
    def _():
        order = order_ref[...]
        for k in range(COMPS):
            for at in range(out_planes):
                plane = (step - steps) * out_planes + at
                out_ref[k, at * GRID : (at + 1) * GRID, :] = dot(order, stack_ref[k, plane]).astype(bf16)


def whole(shape):
    return pl.BlockSpec(shape, lambda *_: (0,) * len(shape))


def smem():
    return pl.BlockSpec(memory_space=pltpu.SMEM)


def local(mean_volume, components, images, tilt, shift, frac, noise_var):
    peers = lax.axis_size("slab")
    me = lax.axis_index("slab")
    planes = mean_volume.shape[0] // GRID
    slots = 2 * planes
    blocks = GRID // slots
    count = images.shape[0]
    total = peers * count
    width = CHANS * GRID
    chunk = max(1, 256 // total)
    steps = slots // chunk
    pack_rows = count * slots + 2 * count
    upper_rows = -(-blocks // 16) * 16
    first = (me * planes).astype(i32).reshape(1)

    packed = pl.pallas_call(
        functools.partial(pack_kernel, (planes, slots, peers, count)),
        out_shape=jax.ShapeDtypeStruct((peers, pack_rows, GRID), bf16),
        in_specs=[smem(), whole((count * GRID, GRID))],
        out_specs=whole((peers, pack_rows, GRID)),
        grid=(1,),
        compiler_params=params(),
        name="pack",
    )(tilt, images.reshape(count * GRID, GRID))
    got = lax.all_to_all(packed, "slab", split_axis=0, concat_axis=0, tiled=True)

    mine = jnp.stack([tilt.astype(f32), shift.astype(f32), frac.astype(f32), noise_var])
    slot_hit = (jnp.arange(peers) == me).astype(f32)
    every = mine[:, :, None] * slot_hit
    every = butterfly(every, peers).reshape(4, total)
    tilts, shifts, fracs = (every[n].astype(i32) for n in range(3))
    noises = every[3]
    tilt_col, shift_col, frac_col = (value[:, None] for value in (tilts, shifts, fracs))

    edge = GRID * (planes - 1)
    bottom = jnp.concatenate([mean_volume[None, :GRID], components[:, :GRID]], axis=0)
    top = jnp.concatenate([mean_volume[None, edge:], components[:, edge:]], axis=0)
    upper = lax.ppermute(bottom, "slab", [(n, n - 1) for n in range(1, peers)])
    lower = lax.ppermute(top, "slab", [(n, n + 1) for n in range(peers - 1)])

    pair = 2 if blocks % 16 else 1
    table = pl.pallas_call(
        functools.partial(table_kernel, (planes, slots, blocks, pair)),
        out_shape=jax.ShapeDtypeStruct((slots, planes * blocks, width), bf16),
        grid=(planes // pair,),
        in_specs=[
            pl.BlockSpec((pair * GRID, GRID), lambda n: (n, 0)),
            pl.BlockSpec((COMPS, pair * GRID, GRID), lambda n: (0, n, 0)),
        ],
        out_specs=pl.BlockSpec((slots, pair * blocks, width), lambda n: (0, n, 0)),
        scratch_shapes=[pltpu.VMEM((GRID, GRID), bf16)],
        compiler_params=params(),
        name="table",
    )(mean_volume, components)

    slices, slices_extra, gram = pl.pallas_call(
        functools.partial(extract_kernel, (planes, slots, blocks, chunk, total)),
        out_shape=[
            jax.ShapeDtypeStruct((slots, total, width), bf16),
            jax.ShapeDtypeStruct((2 * total, width), bf16),
            jax.ShapeDtypeStruct((total, LANES), f32),
        ],
        grid=(steps,),
        in_specs=[
            smem(),
            whole((total, 1)),
            whole((total, 1)),
            whole((total, 1)),
            pl.BlockSpec((chunk, planes * blocks, width), lambda n: (n, 0, 0)),
            whole((CHANS, GRID, GRID)),
            whole((CHANS, GRID, GRID)),
            whole((GRID, GRID)),
            whole((COMPS, GRID, GRID)),
        ],
        out_specs=[
            pl.BlockSpec((chunk, total, width), lambda n: (n, 0, 0)),
            whole((2 * total, width)),
            whole((total, LANES)),
        ],
        scratch_shapes=[
            pltpu.VMEM((slots, upper_rows, width), bf16),
            pltpu.VMEM((len(PAIRS), total, LANES), f32),
        ],
        compiler_params=params(),
        name="extract",
    )(first, tilt_col, shift_col, frac_col, table, upper, lower, mean_volume, components)

    rows, rows_extra, partial = pl.pallas_call(
        functools.partial(project_kernel, (slots, chunk, total, peers, count)),
        out_shape=[
            jax.ShapeDtypeStruct((slots, total, GRID), bf16),
            jax.ShapeDtypeStruct((2 * total, GRID), bf16),
            jax.ShapeDtypeStruct((total, LANES), f32),
        ],
        grid=(steps,),
        in_specs=[
            whole((peers * pack_rows, GRID)),
            pl.BlockSpec((chunk, total, width), lambda n: (n, 0, 0)),
            whole((total, LANES)),
        ],
        out_specs=[
            pl.BlockSpec((chunk, total, GRID), lambda n: (n, 0, 0)),
            whole((2 * total, GRID)),
            whole((total, LANES)),
        ],
        scratch_shapes=[
            pltpu.VMEM((GRID // LANES, peers * pack_rows, LANES), f32),
            pltpu.VMEM((CHANS, total, LANES), f32),
        ],
        compiler_params=params(),
        name="project",
    )(got.reshape(peers * pack_rows, GRID), slices, gram)

    sums = butterfly(partial, peers)

    out_planes = pair
    last = steps - 1
    new_components, latents = pl.pallas_call(
        functools.partial(back_kernel, (planes, slots, blocks, chunk, total, steps, out_planes)),
        out_shape=[
            jax.ShapeDtypeStruct((COMPS, planes * GRID, GRID), bf16),
            jax.ShapeDtypeStruct((8, total), f32),
        ],
        grid=(steps + planes // out_planes,),
        in_specs=[
            smem(),
            whole((total, LANES)),
            whole((1, total)),
            whole((1, 3 * total)),
            whole((total, 1)),
            whole((total, 1)),
            whole((total, 1)),
            pl.BlockSpec((chunk, total, width), lambda n: (jnp.minimum(n, last), 0, 0)),
            pl.BlockSpec((chunk, total, GRID), lambda n: (jnp.minimum(n, last), 0, 0)),
            whole((2 * total, width)),
            whole((2 * total, GRID)),
        ],
        out_specs=[
            pl.BlockSpec((COMPS, out_planes * GRID, GRID), lambda n: (0, jnp.maximum(n - steps, 0), 0)),
            whole((8, total)),
        ],
        scratch_shapes=[
            pltpu.VMEM((COMPS, planes, GRID, GRID), bf16),
            pltpu.VMEM((8, 3 * total), f32),
            pltpu.VMEM((total, LANES), f32),
            pltpu.VMEM((2 * total, GRID), bf16),
            pltpu.VMEM((GRID, GRID), bf16),
        ],
        compiler_params=params(),
        name="back",
    )(
        first, sums, noises[None], jnp.tile(tilts, 3)[None], tilt_col, shift_col, frac_col,
        slices, rows, slices_extra, rows_extra,
    )
    mine = lax.dynamic_index_in_dim(latents.reshape(8, count, peers), me, 2, keepdims=False)
    return new_components, jnp.transpose(mine[:COMPS])


def butterfly(value, peers):
    step = 1
    while step < peers:
        value = value + lax.ppermute(value, "slab", [(n, n ^ step) for n in range(peers)])
        step *= 2
    return value


def solution(mesh):
    placed = (
        P(("groups", "slab"), None),
        P(None, ("groups", "slab"), None),
        P(("groups", "slab"), None, None),
        P(("groups", "slab")),
        P(("groups", "slab")),
        P(("groups", "slab")),
        P(("groups", "slab")),
    )
    return jax.shard_map(
        local,
        mesh=mesh,
        in_specs=placed,
        out_specs=(P(None, ("groups", "slab"), None), P(("groups", "slab"), None)),
        check_vma=False,
    )
```

time: 554 us -> 153 us (0.28); the launches traced: 547 us -> 152 us
  local copies, waits for them, and re-layouts: 159 us -> 8.45 us
  waiting for transfers between devices: 162 us -> 22.8 us
  matrix products: 120 us -> 0 us
  Pallas kernels: 0 us -> 83.6 us
  other arithmetic: 38.4 us -> 1.8 us
  starting transfers between devices: 64.6 us -> 34.7 us
    all_to_all x5 -> x1, waiting for transfers between devices: 162 us -> 0.01 us  [local(): lax.all_to_all(packed, 'slab', split_axis=0, concat_axis=0, tiled=True)]
    dot_general x14 -> x0, matrix products: 120 us -> none  [the longest x2 59.6 us: spread_block(): jnp.einsum('bisqk,bisx->sqkx', scaled, spread, precision=lax.Precision.HI...]
    pallas_call x0 -> x5, Pallas kernels: none -> 83.6 us  [the longest x1 35.7 us: local(): pl.pallas_call(functools.partial(extract_kernel, (planes, slots, blocks,...]
    reshape x9 -> x1, local copies, waits for them, and re-layouts: 55.1 us -> 0.75 us  [local(): latents.reshape(8, count, peers)]
    all_to_all x5 -> x1, starting transfers between devices: 57.6 us -> 7.4 us  [local(): lax.all_to_all(packed, 'slab', split_axis=0, concat_axis=0, tiled=True)]
    while x2 -> x0, local copies, waits for them, and re-layouts: 24.6 us -> none  [the longest x1 24.5 us: local(): lax.scan(lambda carry, pieces: spread_block(carry, pieces, planes_up, blo...]
    convert_element_type x6 -> x4, local copies, waits for them, and re-layouts: 26.7 us -> 2.16 us  [local(): tilts, shifts, fracs = (every[n].astype(i32) for n in range(3))]
    ppermute x3 -> x10, waiting for transfers between devices: 0.01 us -> 22.8 us  [the longest x8 22.8 us: butterfly(): lax.ppermute(value, 'slab', [(n, n ^ step) for n in range(peers)])]
  transfers between devices with their start and end apart: 8 -> 11, of which waited for: 4 -> 7; matrix products, arithmetic and copies ran while one was open for 7% -> 4% of each run, Pallas kernels for 0% -> 33%
where the time goes in v1:
time: 153 us; the launch traced here: 152 us
  Pallas kernels  83.6 us (55%)
  starting transfers between devices  34.7 us (23%)
  waiting for transfers between devices  22.8 us (15%)
  local copies, waits for them, and re-layouts  8.45 us (6%)
  other arithmetic  1.8 us (1%)
    pallas_call x1, Pallas kernels, local(): pl.pallas_call(functools.partial(extract_kernel, (planes, slots, blocks,...  35.7 us
    ppermute x8, waiting for transfers between devices, butterfly(): lax.ppermute(value, 'slab', [(n, n ^ step) for n in range(peers)])  22.8 us
    ppermute x8, starting transfers between devices, butterfly(): lax.ppermute(value, 'slab', [(n, n ^ step) for n in range(peers)])  22.1 us
    pallas_call x1, Pallas kernels, local(): pl.pallas_call(functools.partial(back_kernel, (planes, slots, blocks, chu...  22 us
    pallas_call x1, Pallas kernels, local(): pl.pallas_call(functools.partial(table_kernel, (planes, slots, blocks, pa...  14.6 us
    pallas_call x1, Pallas kernels, local(): pl.pallas_call(functools.partial(project_kernel, (slots, chunk, total, pe...  7.87 us
    all_to_all x1, starting transfers between devices, local(): lax.all_to_all(packed, 'slab', split_axis=0, concat_axis=0, tiled=True)  7.4 us
    ppermute x1, starting transfers between devices, local(): lower = lax.ppermute(top, 'slab', [(n, n + 1) for n in range(peers - 1)])  3.99 us
  transfers between devices with their start and end apart: 11, of which 7 were waited for; matrix products, arithmetic and copies ran while one was open for 4% of the time, Pallas kernels for 33%

profile of v1, /device:TPU:0, one launch (start us, length us, event | category | flops | bytes accessed | tf_op | source)
XLA Modules:
  0.0 152.2 jit_solution(11845528134249050285)
XLA Ops:
  0.6 0.0 copy-start.1
  0.7 3.5 %pack.1 = bf16[16,136,256]{2,1,0:T(8,128)(2,1)} custom-call(s32[4]{0:T(128)} %tilt_ref.1, bf16[1024,256]{1,0:T(8,128)(2,1)} %bitcast.18), custom_call_target="tpu_custom_call" | custom-call | tf_op jit(solution)/shard_map/pack/pallas_call | solution.py:392
  4.1 7.4 %all-to-all-start = ((bf16[16,136,256]{2,1,0:T(8,128)(2,1)}), bf16[16,136,256]{2,1,0:T(8,128)(2,1)S(1)}, u32[]{:S(2)}, u32[]{:S(2)}) async-start(bf16[16,136,256]{2,1,0:T(8,128)(2,1)} %pack.1), calls=%async_computation | async-start | bytes 2228224 | tf_op jit(solution)/shard_map/all_to_all | solution.py:401
  11.5 1.5 fusion.1
  13.0 1.0 slice_bitcast_fusion
  14.0 0.1 pad_maximum_fusion
  14.1 1.3 collective-permute-start.4
  15.4 0.1 pad_maximum_fusion.1
  15.5 4.0 %collective-permute-start.5 = (bf16[7,256,256]{2,1,0:T(8,128)(2,1)S(1)}, bf16[7,256,256]{2,1,0:T(8,128)(2,1)}, u32[]{:S(2)}, u32[]{:S(2)}) collective-permute-start(bf16[7,256,256]{2,1,0:T(8,128)(2,1)S(1)} %pad_maximum_fusion.1), channel_id=1, source_target_pairs={{0,1},{1,2},{2,3},{3,4},{4,5},{5,6},{6,7},{7,8},{8,9},{9,10},{10,1... | collective-permute-start | bytes 2752520 | tf_op jit(solution)/shard_map/ppermute | solution.py:415
  19.6 0.1 broadcast_multiply_fusion
  19.6 0.7 collective-permute-start
  20.4 0.8 collective-permute-done
  21.2 0.1 fusion
  21.3 2.6 %collective-permute-start.1 = (f32[4,4,16]{2,1,0:T(4,128)S(1)}, f32[4,4,16]{2,1,0:T(4,128)S(1)}, u32[]{:S(2)}, u32[]{:S(2)}) collective-permute-start(f32[4,4,16]{2,1,0:T(4,128)S(1)} %fusion), channel_id=1, source_target_pairs={{0,2},{1,3},{2,0},{3,1},{4,6},{5,7},{6,4},{7,5},{8,10},{9,11},{10,... | collective-permute-start | bytes 3080 | tf_op jit(solution)/shard_map/ppermute | solution.py:538
  23.8 12.8 %collective-permute-done.1 = f32[4,4,16]{2,1,0:T(4,128)S(1)} collective-permute-done((f32[4,4,16]{2,1,0:T(4,128)S(1)}, f32[4,4,16]{2,1,0:T(4,128)S(1)}, u32[]{:S(2)}, u32[]{:S(2)}) %collective-permute-start.1) | collective-permute-done | bytes 1056 | tf_op jit(solution)/shard_map/ppermute | solution.py:538
  36.6 0.1 fusion.3
  36.7 12.1 %collective-permute-start.2 = (f32[4,4,16]{2,1,0:T(4,128)S(1)}, f32[4,4,16]{2,1,0:T(4,128)S(1)}, u32[]{:S(2)}, u32[]{:S(2)}) collective-permute-start(f32[4,4,16]{2,1,0:T(4,128)S(1)} %fusion.3), channel_id=1, source_target_pairs={{0,4},{1,5},{2,6},{3,7},{4,0},{5,1},{6,2},{7,3},{8,12},{9,13},{10,... | collective-permute-start | bytes 3080 | tf_op jit(solution)/shard_map/ppermute | solution.py:538
  48.8 1.6 %collective-permute-done.2 = f32[4,4,16]{2,1,0:T(4,128)S(1)} collective-permute-done((f32[4,4,16]{2,1,0:T(4,128)S(1)}, f32[4,4,16]{2,1,0:T(4,128)S(1)}, u32[]{:S(2)}, u32[]{:S(2)}) %collective-permute-start.2) | collective-permute-done | bytes 1056 | tf_op jit(solution)/shard_map/ppermute | solution.py:538
  50.4 1.6 %collective-permute-start.3 = (f32[4,4,16]{2,1,0:T(4,128)S(1)}, f32[4,4,16]{2,1,0:T(4,128)S(1)}, u32[]{:S(2)}, u32[]{:S(2)}) collective-permute-start(f32[4,4,16]{2,1,0:T(4,128)S(1)} %add.30), channel_id=1, source_target_pairs={{0,8},{1,9},{2,10},{3,11},{4,12},{5,13},{6,14},{7,15},{8,0},{9,1},... | collective-permute-start | bytes 3080 | tf_op jit(solution)/shard_map/ppermute | solution.py:538
  52.0 14.6 %table.1.table_ref = bf16[32,128,1792]{2,1,0:T(8,128)(2,1)} custom-call(bf16[4096,256]{1,0:T(8,128)(2,1)} %mean_ref.3, bf16[6,4096,256]{2,1,0:T(8,128)(2,1)} %comp_ref.3), custom_call_target="tpu_custom_call" | custom-call | tf_op jit(solution)/shard_map/table/pallas_call | solution.py:418
  66.6 0.0 collective-permute-done.3
  66.6 0.7 convert_element_type.73.tilt_ref
  67.3 0.7 convert_element_type.74.shift_ref
  68.0 0.7 convert_element_type.75.frac_ref
  68.7 0.0 collective-permute-done.4.up_ref
  68.7 0.0 collective-permute-done.5.low_ref
  68.7 35.7 %extract.1 = (bf16[32,64,1792]{2,1,0:T(8,128)(2,1)}, bf16[128,1792]{1,0:T(8,128)(2,1)}, f32[64,128]{1,0:T(8,128)}) custom-call(s32[1]{0:T(128)} %bitcast.first_ref, s32[64,1]{1,0:T(8,128)} %convert_element_type.73.tilt_ref, s32[64,1]{1,0:T(8,128)} %convert_element_type.74.shift_ref, s32[64,1]{1,0:T(8,128)} %convert_element_type.75.frac_ref, ...), custom_call_target="tpu_custom_call" | custom-call | tf_op jit(solution)/shard_map/extract/pallas_call | solution.py:432
  104.4 0.0 all-to-all-done
  104.4 0.0 copy-start
  104.4 1.0 copy-done
  105.4 7.9 %project.1 = (bf16[32,64,256]{2,1,0:T(8,128)(2,1)}, bf16[128,256]{1,0:T(8,128)(2,1)}, f32[64,128]{1,0:T(8,128)}) custom-call(bf16[2176,256]{1,0:T(8,128)(2,1)} %bitcast.17, bf16[32,64,1792]{2,1,0:T(8,128)(2,1)} %get-tuple-element.10.slice_ref, f32[64,128]{1,0:T(8,128)} %get-tuple-element.11.gram_ref), custom_call_target="tpu_custom_call" | custom-call | tf_op jit(solution)/shard_map/project/pallas_call | solution.py:464
  113.2 0.0 collective-permute-start.6
  113.2 1.4 collective-permute-done.6
  114.6 0.8 add.32
  115.4 1.7 %collective-permute-start.7 = (f32[64,128]{1,0:T(8,128)S(1)}, f32[64,128]{1,0:T(8,128)S(1)}, u32[]{:S(2)}, u32[]{:S(2)}) collective-permute-start(f32[64,128]{1,0:T(8,128)S(1)} %add.32), channel_id=1, source_target_pairs={{0,2},{1,3},{2,0},{3,1},{4,6},{5,7},{6,4},{7,5},{8,10},{9,11},{10,... | collective-permute-start | bytes 98312 | tf_op jit(solution)/shard_map/ppermute | solution.py:538
  117.2 2.2 %collective-permute-done.7 = f32[64,128]{1,0:T(8,128)S(1)} collective-permute-done((f32[64,128]{1,0:T(8,128)S(1)}, f32[64,128]{1,0:T(8,128)S(1)}, u32[]{:S(2)}, u32[]{:S(2)}) %collective-permute-start.7) | collective-permute-done | bytes 32800 | tf_op jit(solution)/shard_map/ppermute | solution.py:538
  119.3 2.0 %collective-permute-start.8 = (f32[64,128]{1,0:T(8,128)S(1)}, f32[64,128]{1,0:T(8,128)S(1)}, u32[]{:S(2)}, u32[]{:S(2)}) collective-permute-start(f32[64,128]{1,0:T(8,128)S(1)} %add.33), channel_id=1, source_target_pairs={{0,4},{1,5},{2,6},{3,7},{4,0},{5,1},{6,2},{7,3},{8,12},{9,13},{10,... | collective-permute-start | bytes 98312 | tf_op jit(solution)/shard_map/ppermute | solution.py:538
  121.3 1.9 %collective-permute-done.8 = f32[64,128]{1,0:T(8,128)S(1)} collective-permute-done((f32[64,128]{1,0:T(8,128)S(1)}, f32[64,128]{1,0:T(8,128)S(1)}, u32[]{:S(2)}, u32[]{:S(2)}) %collective-permute-start.8) | collective-permute-done | bytes 32800 | tf_op jit(solution)/shard_map/ppermute | solution.py:538
  123.3 1.3 collective-permute-start.9
  124.6 0.1 convert_element_type.72
  124.7 0.6 broadcast_in_dim_tile.3.tilt_row_ref
  125.3 0.7 slice.44.noise_ref
  126.0 2.1 %collective-permute-done.9 = f32[64,128]{1,0:T(8,128)S(1)} collective-permute-done((f32[64,128]{1,0:T(8,128)S(1)}, f32[64,128]{1,0:T(8,128)S(1)}, u32[]{:S(2)}, u32[]{:S(2)}) %collective-permute-start.9) | collective-permute-done | bytes 32800 | tf_op jit(solution)/shard_map/ppermute | solution.py:538
  128.1 0.6 add.35.total_ref
  128.7 22.0 %back.1 = (bf16[6,4096,256]{2,1,0:T(8,128)(2,1)}, f32[8,64]{1,0:T(8,128)}) custom-call(s32[1]{0:T(128)} %bitcast.first_ref, f32[64,128]{1,0:T(8,128)} %add.35.total_ref, f32[1,64]{1,0:T(1,128)} %slice.44.noise_ref, s32[1,192]{1,0:T(1,128)} %broadcast_in_dim_tile.3.tilt_row_ref, s32[64,1]{1,0:T(8,128)} %convert_element_type.73.tilt_ref, ...), custom_call_target="tpu_custom_call" | custom-call | tf_op jit(solution)/shard_map/back/pallas_call | solution.py:494
  150.7 0.8 reshape.73
  151.4 0.1 constant_dynamic-slice_fusion
  151.5 0.7 copy.17
  (17 shorter events, 0.1 us)
Async XLA Ops:
  0.6 18.9 %copy-start.1 = (s32[4]{0:T(128)S(1)}, s32[4]{0:T(128)}, u32[]{:S(2)}) copy-start(s32[4]{0:T(128)} %tilt_ref.1) | copy-start | bytes 52
  0.6 18.9 %copy-start.3 = (s32[4]{0:T(128)S(1)}, s32[4]{0:T(128)}, u32[]{:S(2)}) copy-start(s32[4]{0:T(128)} %param.11) | copy-start | bytes 52
  0.7 18.9 %copy-start.2 = (s32[4]{0:T(128)S(1)}, s32[4]{0:T(128)}, u32[]{:S(2)}) copy-start(s32[4]{0:T(128)} %param.12) | copy-start | bytes 52
  0.7 18.9 %copy-start.4 = (f32[4]{0:T(128)S(1)}, f32[4]{0:T(128)}, u32[]{:S(2)}) copy-start(f32[4]{0:T(128)} %param.13) | copy-start | bytes 52
  4.1 100.2 %all-to-all-start = ((bf16[16,136,256]{2,1,0:T(8,128)(2,1)}), bf16[16,136,256]{2,1,0:T(8,128)(2,1)S(1)}, u32[]{:S(2)}, u32[]{:S(2)}) async-start(bf16[16,136,256]{2,1,0:T(8,128)(2,1)} %pack.1), calls=%async_computation | async-start | bytes 2228224 | tf_op jit(solution)/shard_map/all_to_all | solution.py:401
  14.1 54.6 %collective-permute-start.4 = (bf16[7,256,256]{2,1,0:T(8,128)(2,1)S(1)}, bf16[7,256,256]{2,1,0:T(8,128)(2,1)}, u32[]{:S(2)}, u32[]{:S(2)}) collective-permute-start(bf16[7,256,256]{2,1,0:T(8,128)(2,1)S(1)} %pad_maximum_fusion), channel_id=1, source_target_pairs={{1,0},{2,1},{3,2},{4,3},{5,4},{6,5},{7,6},{8,7},{9,8},{10,9},{11,1... | collective-permute-start | bytes 2752520 | tf_op jit(solution)/shard_map/ppermute | solution.py:414
  15.5 53.2 %collective-permute-start.5 = (bf16[7,256,256]{2,1,0:T(8,128)(2,1)S(1)}, bf16[7,256,256]{2,1,0:T(8,128)(2,1)}, u32[]{:S(2)}, u32[]{:S(2)}) collective-permute-start(bf16[7,256,256]{2,1,0:T(8,128)(2,1)S(1)} %pad_maximum_fusion.1), channel_id=1, source_target_pairs={{0,1},{1,2},{2,3},{3,4},{4,5},{5,6},{6,7},{7,8},{8,9},{9,10},{10,1... | collective-permute-start | bytes 2752520 | tf_op jit(solution)/shard_map/ppermute | solution.py:415
  19.6 1.6 %collective-permute-start = (f32[4,4,16]{2,1,0:T(4,128)S(1)}, f32[4,4,16]{2,1,0:T(4,128)S(1)}, u32[]{:S(2)}, u32[]{:S(2)}) collective-permute-start(f32[4,4,16]{2,1,0:T(4,128)S(1)} %broadcast_multiply_fusion), channel_id=1, source_target_pairs={{0,1},{1,0},{2,3},{3,2},{4,5},{5,4},{6,7},{7,6},{8,9},{9,8},{10,11... | collective-permute-start | bytes 3080 | tf_op jit(solution)/shard_map/ppermute | solution.py:538
  21.3 15.4 %collective-permute-start.1 = (f32[4,4,16]{2,1,0:T(4,128)S(1)}, f32[4,4,16]{2,1,0:T(4,128)S(1)}, u32[]{:S(2)}, u32[]{:S(2)}) collective-permute-start(f32[4,4,16]{2,1,0:T(4,128)S(1)} %fusion), channel_id=1, source_target_pairs={{0,2},{1,3},{2,0},{3,1},{4,6},{5,7},{6,4},{7,5},{8,10},{9,11},{10,... | collective-permute-start | bytes 3080 | tf_op jit(solution)/shard_map/ppermute | solution.py:538
  36.7 13.7 %collective-permute-start.2 = (f32[4,4,16]{2,1,0:T(4,128)S(1)}, f32[4,4,16]{2,1,0:T(4,128)S(1)}, u32[]{:S(2)}, u32[]{:S(2)}) collective-permute-start(f32[4,4,16]{2,1,0:T(4,128)S(1)} %fusion.3), channel_id=1, source_target_pairs={{0,4},{1,5},{2,6},{3,7},{4,0},{5,1},{6,2},{7,3},{8,12},{9,13},{10,... | collective-permute-start | bytes 3080 | tf_op jit(solution)/shard_map/ppermute | solution.py:538
  50.4 16.1 %collective-permute-start.3 = (f32[4,4,16]{2,1,0:T(4,128)S(1)}, f32[4,4,16]{2,1,0:T(4,128)S(1)}, u32[]{:S(2)}, u32[]{:S(2)}) collective-permute-start(f32[4,4,16]{2,1,0:T(4,128)S(1)} %add.30), channel_id=1, source_target_pairs={{0,8},{1,9},{2,10},{3,11},{4,12},{5,13},{6,14},{7,15},{8,0},{9,1},... | collective-permute-start | bytes 3080 | tf_op jit(solution)/shard_map/ppermute | solution.py:538
  104.4 1.0 copy-start
  113.2 1.4 collective-permute-start.6
  115.4 3.9 %collective-permute-start.7 = (f32[64,128]{1,0:T(8,128)S(1)}, f32[64,128]{1,0:T(8,128)S(1)}, u32[]{:S(2)}, u32[]{:S(2)}) collective-permute-start(f32[64,128]{1,0:T(8,128)S(1)} %add.32), channel_id=1, source_target_pairs={{0,2},{1,3},{2,0},{3,1},{4,6},{5,7},{6,4},{7,5},{8,10},{9,11},{10,... | collective-permute-start | bytes 98312 | tf_op jit(solution)/shard_map/ppermute | solution.py:538
  119.3 3.9 %collective-permute-start.8 = (f32[64,128]{1,0:T(8,128)S(1)}, f32[64,128]{1,0:T(8,128)S(1)}, u32[]{:S(2)}, u32[]{:S(2)}) collective-permute-start(f32[64,128]{1,0:T(8,128)S(1)} %add.33), channel_id=1, source_target_pairs={{0,4},{1,5},{2,6},{3,7},{4,0},{5,1},{6,2},{7,3},{8,12},{9,13},{10,... | collective-permute-start | bytes 98312 | tf_op jit(solution)/shard_map/ppermute | solution.py:538
  123.3 4.8 %collective-permute-start.9 = (f32[64,128]{1,0:T(8,128)S(1)}, f32[64,128]{1,0:T(8,128)S(1)}, u32[]{:S(2)}, u32[]{:S(2)}) collective-permute-start(f32[64,128]{1,0:T(8,128)S(1)} %add.34), channel_id=1, source_target_pairs={{0,8},{1,9},{2,10},{3,11},{4,12},{5,13},{6,14},{7,15},{8,0},{9,1},... | collective-permute-start | bytes 98312 | tf_op jit(solution)/shard_map/ppermute | solution.py:538

commit v2 on v1

v2 whole, which is shorter than its diff:
```python
import functools

import jax
import jax.numpy as jnp
from jax import lax
from jax.experimental import pallas as pl
from jax.experimental.pallas import tpu as pltpu
from jax.sharding import PartitionSpec as P

GRID = 256
HALF = GRID // 2
COMPS = 6
CHANS = COMPS + 1
TILE = 128
LANES = 128
PAIRS = [(k, l) for k in range(CHANS) for l in range(k, CHANS)]
PROJECT_AT = len(PAIRS)

f32 = jnp.float32
bf16 = jnp.bfloat16
i32 = jnp.int32


def iota(shape, dim):
    return lax.broadcasted_iota(i32, shape, dim)


def dot(a, b):
    return jnp.dot(a, b, preferred_element_type=f32)


def params(mebibytes):
    return pltpu.CompilerParams(vmem_limit_bytes=mebibytes * 1024 * 1024)


def plane_depth(position, tilt):
    numerator = (position - HALF) * tilt
    return jnp.right_shift(numerator, 7) + HALF, jnp.bitwise_and(numerator, HALF - 1)


def pack_kernel(sizes, tilt_ref, shift_ref, mine_ref, image_ref, out_ref, turned_ref):
    planes, slots, peers, count = sizes
    main_rows = count * slots
    shape = (peers * slots, GRID)
    row, col = iota(shape, 0), iota(shape, 1)
    slot_hit = row % slots == col % slots
    first = row // slots * planes
    for image in range(count):
        rows = slice(image * GRID, (image + 1) * GRID)
        for at in range(GRID // TILE):
            span = slice(at * TILE, (at + 1) * TILE)
            part = image_ref[rows, span].astype(f32)
            turned_ref[rows, span] = pltpu.roll(part, shift_ref[image], 1).astype(bf16)
        plane, _ = plane_depth(iota((1, GRID), 1), tilt_ref[image])
        ahead = plane - first
        hit = slot_hit & (ahead >= 0) & (ahead < planes)
        found = dot(jnp.where(hit, 1.0, 0.0).astype(bf16), turned_ref[rows, :])
        found = found.reshape(peers, slots, GRID).astype(bf16)
        out_ref[:, image * slots : (image + 1) * slots, :] = found
    lane = iota((1, count * GRID), 1)
    tilt = jnp.full((1, count * GRID), tilt_ref[0], i32)
    for image in range(1, count):
        tilt = jnp.where(lane >= image * GRID, tilt_ref[image], tilt)
    plane, _ = plane_depth(jnp.bitwise_and(lane, GRID - 1), tilt)
    shape = (peers * 2 * count, count * GRID)
    row, col = iota(shape, 0), iota(shape, 1)
    hit = (row // 2 % count == col // GRID) & (row % 2 == col % 2)
    hit = hit & (plane == row // (2 * count) * planes - 1)
    found = dot(jnp.where(hit, 1.0, 0.0).astype(bf16), turned_ref[...])
    out_ref[:, main_rows:, :] = found.reshape(peers, 2 * count, GRID).astype(bf16)


def slot_order(slots, blocks):
    row, col = iota((GRID, GRID), 0), iota((GRID, GRID), 1)
    return (col == (row % blocks) * slots + row // blocks).astype(f32).astype(bf16)


WINDOW = 80
MIDDLE = 32


def window_starts(boundary):
    away = jnp.abs(boundary)
    nearest = jnp.where(boundary > 0, away - 1, away)
    furthest = jnp.minimum(jnp.where(boundary > 0, 2 * away - 1, 2 * away + 2), HALF)
    low = (HALF - furthest) // 16 * 16
    high = jnp.minimum((HALF + nearest) // 16 * 16, GRID - WINDOW)
    return low, high


def window_rows(boundary):
    low, high = window_starts(boundary)
    lane = iota((1, 2 * WINDOW + MIDDLE), 1)
    far = boundary != 0
    below = jnp.where(far & (low + lane < HALF), low + lane, -1)
    above = high + lane - WINDOW
    above = jnp.where(far & (above >= HALF), above, -1)
    middle = jnp.where(far, -1, HALF - MIDDLE // 2 + lane - 2 * WINDOW)
    return jnp.where(lane < WINDOW, below, jnp.where(lane < 2 * WINDOW, above, middle))


def edges_kernel(
    planes, place_ref, tilt_ref, frac_ref, noise_ref, mean_ref, comp_ref, mean_top_ref, comp_top_ref,
    down_ref, up_ref, middle_ref, mine_ref,
):
    first = place_ref[0]
    here = iota((1, mine_ref.shape[1]), 1) == place_ref[1]
    count = mine_ref.shape[0] // 3
    for image in range(count):
        values = (tilt_ref[image].astype(f32), frac_ref[image].astype(f32), noise_ref[image])
        for n, value in enumerate(values):
            mine_ref[pl.ds(n * count + image, 1), :] = jnp.where(here, value, 0.0)
    bottom = first - HALF
    middle = pl.ds(HALF - MIDDLE // 2, MIDDLE)
    sides = (
        (bottom, mean_ref, comp_ref, down_ref),
        (bottom + planes, mean_top_ref, comp_top_ref, up_ref),
    )
    for chan in range(CHANS):
        middles = []
        for boundary, mean, comp, out in sides:
            plane = mean if chan == 0 else comp.at[chan - 1]
            low, high = window_starts(boundary)
            out[chan, :WINDOW, :] = plane[pl.ds(pl.multiple_of(low, 16), WINDOW), :]
            out[chan, WINDOW:, :] = plane[pl.ds(pl.multiple_of(high, 16), WINDOW), :]
            middles.append(plane[middle, :])
        middle_ref[chan] = jnp.where(bottom == 0, middles[0], middles[1])


def stream(step, parts, copies):
    @pl.when(step == 0)
    def _():
        for part in range(parts):
            for copy in copies(part):
                copy.start()

    @pl.when(step < parts)
    def _():
        for copy in copies(step):
            copy.wait()


def parameter_rows(every_ref):
    count = every_ref.shape[0] // 3
    rows = []
    for n in range(3):
        parts = [every_ref[n * count + at : n * count + at + 1, :] for at in range(count)]
        rows.append(jnp.concatenate(parts, axis=1))
    return rows


def columns(rows):
    fill = jnp.zeros((LANES - len(rows), rows[0].shape[1]), f32)
    return jnp.transpose(jnp.concatenate(rows + [fill], axis=0))


def interpolate(rows, weight, turn):
    parts = []
    for at in range(GRID // TILE):
        part = rows[:, at * TILE : (at + 1) * TILE]
        parts.append((1.0 - weight) * part + weight * pltpu.roll(part, turn, 1))
    return jnp.concatenate(parts, axis=1)


def extract_kernel(
    sizes, place_ref, every_ref, mean_hbm, comp_hbm, up_ref, low_ref, middle_ref,
    out_ref, extra_ref, gram_ref,
    mean_ref, comp_ref, mean_sem, comp_sem, table_ref, order_ref, sums_ref, column_ref,
):
    planes, slots, blocks, chunk, images, pair = sizes
    step, first = pl.program_id(0), place_ref[0]
    tables = planes // pair

    def copies(part):
        rows = pl.ds(pl.multiple_of(part * pair * GRID, GRID), pair * GRID)
        return (
            pltpu.make_async_copy(mean_hbm.at[rows], mean_ref.at[rows], mean_sem.at[part]),
            pltpu.make_async_copy(comp_hbm.at[:, rows], comp_ref.at[:, rows], comp_sem.at[part]),
        )

    stream(step, tables, copies)

    @pl.when(step == 0)
    def _():
        column_ref[...] = columns(parameter_rows(every_ref))

    tilt = column_ref[:, 0:1].astype(i32)
    weight = column_ref[:, 1:2] / 16.0
    own_rows = planes * blocks

    @pl.when(step == 0)
    def _():
        order_ref[...] = slot_order(slots, blocks)
        at_up, at_low = window_rows(first + planes - HALF), window_rows(first - HALF)
        row = iota((GRID, at_up.shape[1]), 0)
        order = (at_up == (row % blocks) * slots + row // blocks).astype(f32).astype(bf16)
        parts = []
        for odd in range(2):
            pieces = []
            for lane, part in ((at_low, 0), (iota((1, GRID), 1), 1)):
                plane, depth = plane_depth(lane, tilt)
                hit = (plane == first - 1) & (lane >= 0) & (jnp.bitwise_and(lane, 1) == odd)
                depth = depth if part else HALF - depth
                pieces.append(jnp.where(hit, depth, 0).astype(f32) / HALF)
            parts.append(pieces)
        mixing_low = jnp.concatenate([parts[0][0], parts[1][0]], axis=0).astype(bf16)
        mixing_own = jnp.concatenate([parts[0][1], parts[1][1]], axis=0).astype(bf16)
        weight2 = jnp.concatenate([weight, weight], axis=0)
        fill = table_ref.shape[1] - own_rows - blocks
        for chan in range(CHANS):
            at = slice(chan * GRID, (chan + 1) * GRID)
            upper = jnp.concatenate([up_ref[chan], middle_ref[chan]], axis=0)
            upper = dot(order, upper).reshape(slots, blocks, GRID)
            if fill:
                upper = jnp.concatenate([upper, jnp.zeros((slots, fill, GRID), f32)], axis=1)
            table_ref[:, own_rows:, at] = upper.astype(bf16)
            lower = jnp.concatenate([low_ref[chan], middle_ref[chan]], axis=0)
            own = mean_ref[:GRID, :] if chan == 0 else comp_ref[chan - 1, :GRID, :]
            blended = dot(mixing_low, lower) + dot(mixing_own, own)
            blended = blended.astype(bf16).astype(f32)
            extra_ref[:, at] = interpolate(blended, weight2, TILE - 1).astype(bf16)
        sums_ref[...] = jnp.zeros_like(sums_ref)

    @pl.when(step < tables)
    def _():
        order = order_ref[...]
        rows = pl.ds(pl.multiple_of(step * pair * blocks, 16), pair * blocks)
        for chan in range(CHANS):
            pieces = []
            for at in range(pair):
                span = pl.ds(pl.multiple_of((step * pair + at) * GRID, GRID), GRID)
                plane = mean_ref[span, :] if chan == 0 else comp_ref[chan - 1, span, :]
                pieces.append(dot(order, plane).reshape(slots, blocks, GRID))
            both = jnp.concatenate(pieces, axis=1).astype(bf16)
            table_ref[:, rows, chan * GRID : (chan + 1) * GRID] = both

    @pl.when(step >= tables)
    def _():
        lane = iota((images, table_ref.shape[1]), 1)
        block_at, plane_at = lane % blocks, lane // blocks
        plane_at = jnp.where(plane_at > planes, -1000, plane_at) + first
        low_at = jnp.where(plane_at < first + planes, plane_at, -1000)
        high_at = jnp.where(plane_at > first, plane_at - 1, -1000)
        base = (block_at * slots - HALF) * tilt
        for at in range(chunk):
            slot = (step - tables) * chunk + at
            numerator = base + slot * tilt
            plane, depth = jnp.right_shift(numerator, 7) + HALF, jnp.bitwise_and(numerator, HALF - 1)
            mixing = jnp.where(plane == low_at, HALF - depth, jnp.where(plane == high_at, depth, 0))
            mixing = (mixing.astype(f32) * (1.0 / HALF)).astype(bf16)
            blended = dot(mixing, table_ref[slot])
            for chan in range(CHANS):
                span = slice(chan * GRID, (chan + 1) * GRID)
                part = blended[:, span].astype(bf16).astype(f32)
                out_ref[at, :, span] = interpolate(part, weight, TILE - 1).astype(bf16)
        gram_sums(chunk, images, out_ref, sums_ref)

    @pl.when(step == pl.num_programs(0) - 1)
    def _():
        lane = iota((images, LANES), 1)
        total = jnp.zeros((images, LANES), f32)
        for n in range(len(PAIRS)):
            total = jnp.where(lane == n, jnp.sum(sums_ref[n], axis=1, keepdims=True), total)
        gram_ref[...] = total


def gram_sums(chunk, images, out_ref, sums_ref):
    def accumulate(group, carry):
        rows = pl.ds(pl.multiple_of(group * 16, 16), 16)
        sums = [sums_ref[n, rows, :] for n in range(len(PAIRS))]
        for at in range(chunk):
            for tile in range(GRID // LANES):
                values = [
                    out_ref[at, rows, pl.ds(chan * GRID + tile * LANES, LANES)].astype(f32)
                    for chan in range(CHANS)
                ]
                for n, (k, l) in enumerate(PAIRS):
                    sums[n] = sums[n] + values[k] * values[l]
        for n in range(len(PAIRS)):
            sums_ref[n, rows, :] = sums[n]
        return carry

    lax.fori_loop(0, images // 16, accumulate, 0)


def project_kernel(
    sizes, got_ref, slice_hbm, gram_ref, rows_ref, extra_ref, total_ref,
    slice_ref, slice_sem, wide_ref, sums_ref,
):
    slots, chunk, images, peers, count = sizes
    stride = count * slots + 2 * count
    step = pl.program_id(0)

    def copies(part):
        at = pl.ds(part * chunk, chunk)
        return (pltpu.make_async_copy(slice_hbm.at[at], slice_ref.at[at], slice_sem.at[part]),)

    stream(step, slots // chunk, copies)

    @pl.when(step == 0)
    def _():
        for tile in range(GRID // LANES):
            wide_ref[tile] = got_ref[:, tile * LANES : (tile + 1) * LANES].astype(f32)
        sums_ref[...] = jnp.zeros_like(sums_ref)
        for odd in range(2):
            for image in range(count):
                start = count * slots + image * 2 + odd
                at = (odd * count + image) * peers
                for tile in range(GRID // LANES):
                    part = wide_ref[tile, pl.ds(start, peers, stride=stride), :]
                    extra_ref[at : at + peers, tile * LANES : (tile + 1) * LANES] = part.astype(bf16)

    for image in range(count):
        span = slice(image * peers, (image + 1) * peers)
        sums = [sums_ref[chan, span, :] for chan in range(CHANS)]
        for at in range(chunk):
            slot = step * chunk + at
            for tile in range(GRID // LANES):
                part = wide_ref[tile, pl.ds(image * slots + slot, peers, stride=stride), :]
                rows_ref[at, span, tile * LANES : (tile + 1) * LANES] = part.astype(bf16)
                for chan in range(CHANS):
                    lanes = slice(chan * GRID + tile * LANES, chan * GRID + (tile + 1) * LANES)
                    sums[chan] = sums[chan] + part * slice_ref[slot, span, lanes].astype(f32)
        for chan in range(CHANS):
            sums_ref[chan, span, :] = sums[chan]

    @pl.when(step == pl.num_programs(0) - 1)
    def _():
        lane = iota((images, LANES), 1)
        total = gram_ref[...]
        for chan in range(CHANS):
            value = jnp.sum(sums_ref[chan], axis=1, keepdims=True)
            total = jnp.where(lane == PROJECT_AT + chan, value, total)
        total_ref[...] = total


def solve_rows(table, noise):
    count = float(GRID * GRID)

    def gram(k, l):
        at = PAIRS.index((min(k, l), max(k, l)))
        return table[at : at + 1, :]

    factor = [[None] * COMPS for _ in range(COMPS)]
    inverse = [None] * COMPS
    for col in range(COMPS):
        for row in range(col, COMPS):
            total = gram(row + 1, col + 1) / count
            if row == col:
                total = total + noise
            for at in range(col):
                total = total - factor[row][at] * factor[col][at]
            if row == col:
                inverse[col] = 1.0 / jnp.sqrt(total)
            else:
                factor[row][col] = total * inverse[col]
    forward = []
    for row in range(COMPS):
        at = PROJECT_AT + row + 1
        total = (table[at : at + 1, :] - gram(row + 1, 0)) / count
        for col in range(row):
            total = total - factor[row][col] * forward[col]
        forward.append(total * inverse[row])
    latent = [None] * COMPS
    for row in reversed(range(COMPS)):
        total = forward[row]
        for col in range(row + 1, COMPS):
            total = total - factor[col][row] * latent[col]
        latent[row] = total * inverse[row]
    return latent


def back_kernel(
    sizes, place_ref, total_ref, every_ref,
    slice_hbm, rows_ref, slice_extra_ref, rows_extra_ref,
    out_ref, latent_ref, slice_ref, slice_sem, stack_ref, row_ref, tilt_ref, col_ref, free_ref, spill_ref, spill_power_ref, order_ref,
):
    planes, slots, blocks, chunk, images, steps, out_planes = sizes
    step, first = pl.program_id(0), place_ref[0]
    group = 2 if blocks % 16 else 1

    def copies(part):
        at = pl.ds(part * chunk, chunk)
        return (pltpu.make_async_copy(slice_hbm.at[at], slice_ref.at[at], slice_sem.at[part]),)

    stream(step, steps, copies)

    @pl.when(step == 0)
    def _():
        table = jnp.transpose(total_ref[...])
        tilt, frac, noise = parameter_rows(every_ref)
        latent = solve_rows(table, noise)
        free_ref[...] = columns(latent)
        count = latent_ref.shape[0]
        for image in range(count):
            at = image * (images // count) + place_ref[1]
            latent_ref[image : image + 1, :] = free_ref[pl.ds(at, 1), :COMPS]
        rounded = [value.astype(bf16).astype(f32) for value in latent]
        power = rounded[0] * rounded[0]
        for value in rounded[1:]:
            power = power + value * value
        rows = jnp.concatenate(rounded + [power, power], axis=0)
        row_ref[...] = jnp.concatenate([rows, rows, rows], axis=1).astype(bf16)
        tilt_ref[...] = jnp.concatenate([tilt, tilt, tilt], axis=1).astype(i32)
        col_ref[...] = columns(rounded + [power, tilt, frac])
        row, col = iota((GRID, GRID), 0), iota((GRID, GRID), 1)
        order_ref[...] = (row == (col % blocks) * slots + col // blocks).astype(f32).astype(bf16)

    def spread(slices, rows, copies):
        weight = col_ref[:, COMPS + 2 : COMPS + 3] / 16.0
        latent = col_ref[...]
        if copies > 1:
            weight = jnp.concatenate([weight] * copies, axis=0)
            latent = jnp.concatenate([latent] * copies, axis=0)
        residual = rows[...].astype(f32) - slices[:, :GRID].astype(f32)
        for k in range(COMPS):
            span = slice((k + 1) * GRID, (k + 2) * GRID)
            residual = residual - latent[:, k : k + 1] * slices[:, span].astype(f32)
        return interpolate(residual.astype(bf16).astype(f32), weight, 1)

    def factors(parts):
        high = [part.astype(bf16) for part in parts]
        low = [(part - top.astype(f32)).astype(bf16) for part, top in zip(parts, high)]
        shape = (images, LANES)
        high = jnp.concatenate([jnp.broadcast_to(part, shape) for part in high], axis=0)
        low = jnp.concatenate([jnp.broadcast_to(part, shape) for part in low], axis=0)
        return jnp.concatenate([high, low], axis=1)

    @pl.when(step == 0)
    def _():
        value = spread(slice_extra_ref, rows_extra_ref, 2)
        power = col_ref[:, COMPS : COMPS + 1]
        plane, depth = plane_depth(iota((images, GRID), 1), col_ref[:, COMPS + 1 : COMPS + 2].astype(i32))
        odd = jnp.bitwise_and(iota((images, GRID), 1), 1)
        for at in range(2):
            hit = (plane == first - 1) & (odd == at)
            part = jnp.sum(jnp.where(hit, depth, 0).astype(f32), axis=1, keepdims=True) / HALF
            span = slice(at * images, (at + 1) * images)
            spill_ref[span, :] = (part * value[span]).astype(bf16)
            spill_power_ref[span, :] = factors([part * power])

    @pl.when(step < steps)
    def _():
        power = col_ref[:, COMPS : COMPS + 1]
        lane_slot = iota((images, LANES), 1)
        tilt = tilt_ref[...]
        tilt_col = col_ref[:, COMPS + 1 : COMPS + 2].astype(i32)
        row = iota((blocks, 3 * images), 0)
        base = (row * slots - HALF) * tilt
        shape = (planes, blocks, 3 * images)
        plane_at, lane = iota(shape, 0), iota(shape, 2)
        wanted = jnp.where(lane < images, plane_at, plane_at - 1)
        wanted = jnp.where((lane < 2 * images) == (wanted < 0), -1000, wanted) + (first - HALF)
        for start in range(0, chunk, group):
            pieces = [[] for _ in range(COMPS)]
            for at in range(start, start + group):
                slot = step * chunk + at
                value = spread(slice_ref.at[slot], rows_ref.at[at], 1)
                plane, depth = plane_depth(lane_slot * slots + slot, tilt_col)
                plane = plane - first
                live = (plane >= 0) & (plane < planes) & (lane_slot < blocks)
                depth = jnp.sum(jnp.where(live, depth, 0).astype(f32), axis=1, keepdims=True) / HALF
                odd = pl.ds(pl.multiple_of((slot % 2) * images, 16), images)
                right = jnp.concatenate(
                    [
                        ((1.0 - depth) * value).astype(bf16),
                        (depth * value).astype(bf16),
                        spill_ref[odd, :],
                    ],
                    axis=0,
                )
                powers = jnp.concatenate(
                    [factors([(1.0 - depth) * power, depth * power]), spill_power_ref[odd, :]], axis=0
                )
                plane = jnp.right_shift(base + slot * tilt, 7)
                hit = jnp.where(plane[None] == wanted, 1.0, 0.0)
                hit = hit.reshape(planes * blocks, 3 * images).astype(bf16)
                weight = dot(hit, powers)
                scale = 1.0 / (1.0 + (weight[:, :LANES] + weight[:, LANES:]))
                scale = jnp.concatenate([scale, scale], axis=1)
                left = jnp.concatenate([hit * row_ref[k : k + 1, :] for k in range(COMPS)], axis=0)
                totals = dot(left, right)
                for k in range(COMPS):
                    total = totals[k * planes * blocks : (k + 1) * planes * blocks] * scale
                    pieces[k].append(total.reshape(planes, blocks, GRID))
            rows = pl.ds(pl.multiple_of((step * chunk + start) * blocks, 16), group * blocks)
            for k in range(COMPS):
                stack_ref[k, :, rows, :] = jnp.concatenate(pieces[k], axis=1).astype(bf16)

    @pl.when(step >= steps)
    def _():
        order = order_ref[...]
        for k in range(COMPS):
            for at in range(out_planes):
                plane = (step - steps) * out_planes + at
                out_ref[k, at * GRID : (at + 1) * GRID, :] = dot(order, stack_ref[k, plane]).astype(bf16)


def whole(shape):
    return pl.BlockSpec(shape, lambda *_: (0,) * len(shape))


def smem():
    return pl.BlockSpec(memory_space=pltpu.SMEM)


def local(mean_volume, components, images, tilt, shift, frac, noise_var):
    peers = lax.axis_size("slab")
    me = lax.axis_index("slab")
    planes = mean_volume.shape[0] // GRID
    slots = 2 * planes
    blocks = GRID // slots
    count = images.shape[0]
    total = peers * count
    width = CHANS * GRID
    chunk = max(1, 256 // total)
    steps = slots // chunk
    pack_rows = count * slots + 2 * count
    upper_rows = -(-blocks // 16) * 16
    place = jnp.stack([me * planes, me]).astype(i32)

    top = planes - 1
    wide = 2 * WINDOW
    down_rows, up_rows, middle_rows, mine = pl.pallas_call(
        functools.partial(edges_kernel, planes),
        out_shape=[
            jax.ShapeDtypeStruct((CHANS, rows, GRID), bf16) for rows in (wide, wide, MIDDLE)
        ] + [jax.ShapeDtypeStruct((3 * count, peers), f32)],
        grid=(1,),
        in_specs=[
            smem(),
            smem(),
            smem(),
            smem(),
            pl.BlockSpec((GRID, GRID), lambda n: (0, 0)),
            pl.BlockSpec((COMPS, GRID, GRID), lambda n: (0, 0, 0)),
            pl.BlockSpec((GRID, GRID), lambda n: (top, 0)),
            pl.BlockSpec((COMPS, GRID, GRID), lambda n: (0, top, 0)),
        ],
        out_specs=[whole((CHANS, rows, GRID)) for rows in (wide, wide, MIDDLE)]
        + [whole((3 * count, peers))],
        compiler_params=params(56),
        name="edges",
    )(place, tilt, frac, noise_var, mean_volume, components, mean_volume, components)
    half = peers // 2
    upper = lax.ppermute(down_rows, "slab", [(n, n - 1) for n in range(1, peers) if n != half])
    lower = lax.ppermute(up_rows, "slab", [(n, n + 1) for n in range(peers - 1) if n + 1 != half])
    middle = lax.ppermute(middle_rows, "slab", [(half, half - 1), (half - 1, half)])

    every = gather_places(mine, peers)

    packed = pl.pallas_call(
        functools.partial(pack_kernel, (planes, slots, peers, count)),
        out_shape=jax.ShapeDtypeStruct((peers, pack_rows, GRID), bf16),
        in_specs=[smem(), smem(), pl.BlockSpec(memory_space=pl.ANY), whole((count * GRID, GRID))],
        out_specs=whole((peers, pack_rows, GRID)),
        scratch_shapes=[pltpu.VMEM((count * GRID, GRID), bf16)],
        grid=(1,),
        compiler_params=params(56),
        name="pack",
    )(tilt, shift, mine, images.reshape(count * GRID, GRID))
    got = lax.all_to_all(packed, "slab", split_axis=0, concat_axis=0, tiled=True)

    pair = 2 if blocks % 16 else 1
    tables = planes // pair
    table_rows = -(-(planes + 1) * blocks // 16) * 16
    slices, slices_extra, gram = pl.pallas_call(
        functools.partial(extract_kernel, (planes, slots, blocks, chunk, total, pair)),
        out_shape=[
            jax.ShapeDtypeStruct((slots, total, width), bf16),
            jax.ShapeDtypeStruct((2 * total, width), bf16),
            jax.ShapeDtypeStruct((total, LANES), f32),
        ],
        grid=(tables + steps,),
        in_specs=[
            smem(),
            whole((3 * count, peers)),
            pl.BlockSpec(memory_space=pl.ANY),
            pl.BlockSpec(memory_space=pl.ANY),
            whole((CHANS, wide, GRID)),
            whole((CHANS, wide, GRID)),
            whole((CHANS, MIDDLE, GRID)),
        ],
        out_specs=[
            pl.BlockSpec((chunk, total, width), lambda n: (jnp.maximum(n - tables, 0), 0, 0)),
            whole((2 * total, width)),
            whole((total, LANES)),
        ],
        scratch_shapes=[
            pltpu.VMEM((planes * GRID, GRID), bf16),
            pltpu.VMEM((COMPS, planes * GRID, GRID), bf16),
            pltpu.SemaphoreType.DMA((tables,)),
            pltpu.SemaphoreType.DMA((tables,)),
            pltpu.VMEM((slots, table_rows, width), bf16),
            pltpu.VMEM((GRID, GRID), bf16),
            pltpu.VMEM((len(PAIRS), total, LANES), f32),
            pltpu.VMEM((total, LANES), f32),
        ],
        compiler_params=params(56),
        name="extract",
    )(place, every, mean_volume, components, upper, lower, middle)

    rows, rows_extra, partial = pl.pallas_call(
        functools.partial(project_kernel, (slots, chunk, total, peers, count)),
        out_shape=[
            jax.ShapeDtypeStruct((slots, total, GRID), bf16),
            jax.ShapeDtypeStruct((2 * total, GRID), bf16),
            jax.ShapeDtypeStruct((total, LANES), f32),
        ],
        grid=(steps,),
        in_specs=[
            whole((peers * pack_rows, GRID)),
            pl.BlockSpec(memory_space=pl.ANY),
            whole((total, LANES)),
        ],
        out_specs=[
            pl.BlockSpec((chunk, total, GRID), lambda n: (n, 0, 0)),
            whole((2 * total, GRID)),
            whole((total, LANES)),
        ],
        scratch_shapes=[
            pltpu.VMEM((slots, total, width), bf16),
            pltpu.SemaphoreType.DMA((steps,)),
            pltpu.VMEM((GRID // LANES, peers * pack_rows, LANES), f32),
            pltpu.VMEM((CHANS, total, LANES), f32),
        ],
        compiler_params=params(56),
        name="project",
    )(got.reshape(peers * pack_rows, GRID), slices, gram)

    sums = butterfly(partial, peers)

    out_planes = 2
    last = steps - 1
    new_components, latents = pl.pallas_call(
        functools.partial(back_kernel, (planes, slots, blocks, chunk, total, steps, out_planes)),
        out_shape=[
            jax.ShapeDtypeStruct((COMPS, planes * GRID, GRID), bf16),
            jax.ShapeDtypeStruct((count, COMPS), f32),
        ],
        grid=(steps + planes // out_planes,),
        in_specs=[
            smem(),
            whole((total, LANES)),
            whole((3 * count, peers)),
            pl.BlockSpec(memory_space=pl.ANY),
            pl.BlockSpec((chunk, total, GRID), lambda n: (jnp.minimum(n, last), 0, 0)),
            whole((2 * total, width)),
            whole((2 * total, GRID)),
        ],
        out_specs=[
            pl.BlockSpec((COMPS, out_planes * GRID, GRID), lambda n: (0, jnp.maximum(n - steps, 0), 0)),
            whole((count, COMPS)),
        ],
        scratch_shapes=[
            pltpu.VMEM((slots, total, width), bf16),
            pltpu.SemaphoreType.DMA((steps,)),
            pltpu.VMEM((COMPS, planes, GRID, GRID), bf16),
            pltpu.VMEM((8, 3 * total), bf16),
            pltpu.VMEM((1, 3 * total), i32),
            pltpu.VMEM((total, LANES), f32),
            pltpu.VMEM((total, LANES), f32),
            pltpu.VMEM((2 * total, GRID), bf16),
            pltpu.VMEM((2 * total, 2 * LANES), bf16),
            pltpu.VMEM((GRID, GRID), bf16),
        ],
        compiler_params=params(56),
        name="back",
    )(place, sums, every, slices, rows, slices_extra, rows_extra)
    return new_components, latents


def exchange(value, step):
    peers = lax.axis_size("slab")
    return value + lax.ppermute(value, "slab", [(n, n ^ step) for n in range(peers)])


def gather_places(value, peers):
    fours = [value] + [
        lax.ppermute(value, "slab", [(n, n ^ (part * peers // 4)) for n in range(peers)])
        for part in (2, 3, 1)
    ]
    value = (fours[0] + fours[1]) + (fours[2] + fours[3])
    step = peers // 8
    while step:
        value = exchange(value, step)
        step //= 2
    return value


def butterfly(value, peers):
    step = 1
    while step < peers:
        value = exchange(value, step)
        step *= 2
    return value


def solution(mesh):
    placed = (
        P(("groups", "slab"), None),
        P(None, ("groups", "slab"), None),
        P(("groups", "slab"), None, None),
        P(("groups", "slab")),
        P(("groups", "slab")),
        P(("groups", "slab")),
        P(("groups", "slab")),
    )
    return jax.shard_map(
        local,
        mesh=mesh,
        in_specs=placed,
        out_specs=(P(None, ("groups", "slab"), None), P(("groups", "slab"), None)),
        check_vma=False,
    )
```

time: 153 us -> 120 us (0.78)
  Pallas kernels: 83.6 us -> 54.3 us
  waiting for transfers between devices: 22.8 us -> 35.7 us
  starting transfers between devices: 34.7 us -> 22.6 us
  local copies, waits for them, and re-layouts: 8.45 us -> 2.7 us
  other arithmetic: 1.8 us -> 3.35 us
    pallas_call x1, Pallas kernels: 35.7 us -> 22.7 us  [local(): pl.pallas_call(functools.partial(extract_kernel, (planes, slots, blocks,...]
    ppermute x10 -> x12, waiting for transfers between devices: 22.8 us -> 35.7 us  [the longest x3 20.9 us: gather_places(): lax.ppermute(value, 'slab', [(n, n ^ part * peers // 4) for n in range(pe...]
    ppermute x10 -> x12, starting transfers between devices: 27.4 us -> 15.2 us  [the longest x6 5.1 us: exchange(): lax.ppermute(value, 'slab', [(n, n ^ step) for n in range(peers)])]
    pallas_call x1, Pallas kernels: 14.6 us -> 2.67 us  [local(): pl.pallas_call(functools.partial(edges_kernel, planes), out_shape=[jax.Sh...]
    pallas_call x1, Pallas kernels: 22 us -> 19.4 us  [local(): pl.pallas_call(functools.partial(back_kernel, (planes, slots, blocks, chu...]
    slice x3 -> x0, local copies, waits for them, and re-layouts: 2.21 us -> none  [the longest x1 1.48 us: local(): components[:, edge:]]
    convert_element_type x4 -> x0, local copies, waits for them, and re-layouts: 2.16 us -> none  [local(): tilts, shifts, fracs = (every[n].astype(i32) for n in range(3))]
  transfers between devices with their start and end apart: 11 -> 13, of which waited for: 7 -> 8; matrix products, arithmetic and copies ran while one was open for 4% -> 1% of each run, Pallas kernels for 33% -> 19%
where the time goes in v2:
time: 120 us; the launch traced here: 119 us
  Pallas kernels  54.3 us (45%)
  waiting for transfers between devices  35.7 us (30%)
  starting transfers between devices  22.6 us (19%)
  other arithmetic  3.35 us (3%)
  local copies, waits for them, and re-layouts  2.7 us (2%)
    pallas_call x1, Pallas kernels, local(): pl.pallas_call(functools.partial(extract_kernel, (planes, slots, blocks,...  22.7 us
    ppermute x3, waiting for transfers between devices, gather_places(): lax.ppermute(value, 'slab', [(n, n ^ part * peers // 4) for n in range(pe...  20.9 us
    pallas_call x1, Pallas kernels, local(): pl.pallas_call(functools.partial(back_kernel, (planes, slots, blocks, chu...  19.4 us
    ppermute x6, waiting for transfers between devices, exchange(): lax.ppermute(value, 'slab', [(n, n ^ step) for n in range(peers)])  14.8 us
    all_to_all x1, starting transfers between devices, local(): lax.all_to_all(packed, 'slab', split_axis=0, concat_axis=0, tiled=True)  7.38 us
    pallas_call x1, Pallas kernels, local(): pl.pallas_call(functools.partial(project_kernel, (slots, chunk, total, pe...  6.58 us
    ppermute x6, starting transfers between devices, exchange(): lax.ppermute(value, 'slab', [(n, n ^ step) for n in range(peers)])  5.1 us
    ppermute x3, starting transfers between devices, gather_places(): lax.ppermute(value, 'slab', [(n, n ^ part * peers // 4) for n in range(pe...  5.06 us
  transfers between devices with their start and end apart: 13, of which 8 were waited for; matrix products, arithmetic and copies ran while one was open for 1% of the time, Pallas kernels for 19%

profile of v2, /device:TPU:0, one launch (start us, length us, event | category | flops | bytes accessed | tf_op | source)
XLA Modules:
  0.0 119.4 jit_solution(4474911557288187779)
XLA Ops:
  0.6 0.7 pad_add_fusion.place_ref
  1.3 2.7 %edges.1 = (bf16[7,160,256]{2,1,0:T(8,128)(2,1)}, bf16[7,160,256]{2,1,0:T(8,128)(2,1)}, bf16[7,32,256]{2,1,0:T(8,128)(2,1)}, f32[12,16]{1,0:T(8,128)}) custom-call(s32[2]{0:T(128)} %pad_add_fusion.place_ref, s32[4]{0:T(128)} %tilt_ref.3, s32[4]{0:T(128)} %frac_ref.1, f32[4]{0:T(128)} %noise_ref.1, bf16[4096,256]{1,0:T(8,128)(2,1)} %mean_hbm.1, ...), custom_call_target="tpu_custom_call" | custom-call | tf_op jit(solution)/shard_map/edges/pallas_call | solution.py:524
  4.0 3.0 %pack.1 = bf16[16,136,256]{2,1,0:T(8,128)(2,1)} custom-call(s32[4]{0:T(128)} %tilt_ref.3, s32[4]{0:T(128)} %shift_ref.1, f32[12,16]{1,0:T(8,128)} %get-tuple-element.12.mine_ref, bf16[1024,256]{1,0:T(8,128)(2,1)} %bitcast.5), custom_call_target="tpu_custom_call" | custom-call | tf_op jit(solution)/shard_map/pack/pallas_call | solution.py:552
  7.0 7.4 %all-to-all-start = ((bf16[16,136,256]{2,1,0:T(8,128)(2,1)}), bf16[16,136,256]{2,1,0:T(8,128)(2,1)S(1)}, u32[]{:S(2)}, u32[]{:S(2)}) async-start(bf16[16,136,256]{2,1,0:T(8,128)(2,1)} %pack.1), calls=%async_computation | async-start | bytes 2228224 | tf_op jit(solution)/shard_map/all_to_all | solution.py:562
  14.4 1.3 %collective-permute-start.5 = (bf16[7,160,256]{2,1,0:T(8,128)(2,1)}, bf16[7,160,256]{2,1,0:T(8,128)(2,1)S(1)}, u32[]{:S(2)}, u32[]{:S(2)}) collective-permute-start(bf16[7,160,256]{2,1,0:T(8,128)(2,1)} %get-tuple-element.13), channel_id=1, source_target_pairs={{1,0},{2,1},{3,2},{4,3},{5,4},{6,5},{7,6},{9,8},{10,9},{11,10},{12... | collective-permute-start | bytes 1720328 | tf_op jit(solution)/shard_map/ppermute | solution.py:546
  15.7 3.1 %collective-permute-start.6 = (bf16[7,160,256]{2,1,0:T(8,128)(2,1)}, bf16[7,160,256]{2,1,0:T(8,128)(2,1)S(1)}, u32[]{:S(2)}, u32[]{:S(2)}) collective-permute-start(bf16[7,160,256]{2,1,0:T(8,128)(2,1)} %get-tuple-element.14), channel_id=1, source_target_pairs={{0,1},{1,2},{2,3},{3,4},{4,5},{5,6},{6,7},{8,9},{9,10},{10,11},{11... | collective-permute-start | bytes 1720328 | tf_op jit(solution)/shard_map/ppermute | solution.py:547
  18.8 2.7 %collective-permute-start.2 = (f32[12,16]{1,0:T(8,128)}, f32[12,16]{1,0:T(8,128)S(1)}, u32[]{:S(2)}, u32[]{:S(2)}) collective-permute-start(f32[12,16]{1,0:T(8,128)} %get-tuple-element.12.mine_ref), channel_id=1, source_target_pairs={{0,4},{1,5},{2,6},{3,7},{4,0},{5,1},{6,2},{7,3},{8,12},{9,13},{10,... | collective-permute-start | bytes 2312 | tf_op jit(solution)/shard_map/ppermute | solution.py:680
  21.4 1.9 %collective-permute-start.1 = (f32[12,16]{1,0:T(8,128)}, f32[12,16]{1,0:T(8,128)S(1)}, u32[]{:S(2)}, u32[]{:S(2)}) collective-permute-start(f32[12,16]{1,0:T(8,128)} %get-tuple-element.12.mine_ref), channel_id=1, source_target_pairs={{0,12},{1,13},{2,14},{3,15},{4,8},{5,9},{6,10},{7,11},{8,4},{9,5},... | collective-permute-start | bytes 2312 | tf_op jit(solution)/shard_map/ppermute | solution.py:680
  23.3 0.5 collective-permute-start
  23.8 18.1 %collective-permute-done.2 = f32[12,16]{1,0:T(8,128)S(1)} collective-permute-done((f32[12,16]{1,0:T(8,128)}, f32[12,16]{1,0:T(8,128)S(1)}, u32[]{:S(2)}, u32[]{:S(2)}) %collective-permute-start.2) | collective-permute-done | bytes 800 | tf_op jit(solution)/shard_map/ppermute | solution.py:680
  41.9 0.7 collective-permute-start.7
  42.6 2.8 %collective-permute-done.1 = f32[12,16]{1,0:T(8,128)S(1)} collective-permute-done((f32[12,16]{1,0:T(8,128)}, f32[12,16]{1,0:T(8,128)S(1)}, u32[]{:S(2)}, u32[]{:S(2)}) %collective-permute-start.1) | collective-permute-done | bytes 800 | tf_op jit(solution)/shard_map/ppermute | solution.py:680
  45.4 0.0 collective-permute-done
  45.4 0.7 add_add_fusion
  46.1 0.0 collective-permute-start.3
  46.1 3.6 %collective-permute-done.3 = f32[12,16]{1,0:T(8,128)S(1)} collective-permute-done((f32[12,16]{1,0:T(8,128)S(1)}, f32[12,16]{1,0:T(8,128)S(1)}, u32[]{:S(2)}, u32[]{:S(2)}) %collective-permute-start.3) | collective-permute-done | bytes 800 | tf_op jit(solution)/shard_map/ppermute | solution.py:675
  49.7 0.0 collective-permute-start.4
  49.8 1.2 collective-permute-done.4
  50.9 0.6 add.31.every_ref
  51.5 0.0 collective-permute-done.7.middle_ref
  51.5 0.0 copy-start.3
  51.5 0.0 collective-permute-done.5.up_ref
  51.5 0.0 copy-start.1
  51.5 0.0 collective-permute-done.6.low_ref
  51.6 0.6 copy-done.3
  52.2 0.2 copy-done.1
  52.4 0.0 copy-start.2
  52.4 0.9 copy-done.2
  53.3 22.7 %extract.1 = (bf16[32,64,1792]{2,1,0:T(8,128)(2,1)}, bf16[128,1792]{1,0:T(8,128)(2,1)}, f32[64,128]{1,0:T(8,128)}) custom-call(s32[2]{0:T(128)} %pad_add_fusion.place_ref, f32[12,16]{1,0:T(8,128)} %add.31.every_ref, bf16[4096,256]{1,0:T(8,128)(2,1)} %mean_hbm.1, bf16[6,4096,256]{2,1,0:T(8,128)(2,1)} %comp_hbm.1, bf16[7,160,256]{2,1,0:T(8,128)(2,1)} %copy-done.1, ...), custom_call_target="tpu_custom_call" | custom-call | tf_op jit(solution)/shard_map/extract/pallas_call | solution.py:567
  75.9 0.0 all-to-all-done
  76.0 0.0 copy-start
  76.0 1.0 copy-done
  76.9 6.6 %project.1 = (bf16[32,64,256]{2,1,0:T(8,128)(2,1)}, bf16[128,256]{1,0:T(8,128)(2,1)}, f32[64,128]{1,0:T(8,128)}) custom-call(bf16[2176,256]{1,0:T(8,128)(2,1)} %bitcast.4, bf16[32,64,1792]{2,1,0:T(8,128)(2,1)} %get-tuple-element.16.slice_hbm, f32[64,128]{1,0:T(8,128)} %get-tuple-element.17.gram_ref), custom_call_target="tpu_custom_call" | custom-call | tf_op jit(solution)/shard_map/project/pallas_call | solution.py:603
  83.5 0.2 collective-permute-start.8
  83.8 1.3 %collective-permute-done.8 = f32[64,128]{1,0:T(8,128)S(1)} collective-permute-done((f32[64,128]{1,0:T(8,128)}, f32[64,128]{1,0:T(8,128)S(1)}, u32[]{:S(2)}, u32[]{:S(2)}) %collective-permute-start.8) | collective-permute-done | bytes 32800 | tf_op jit(solution)/shard_map/ppermute | solution.py:675
  85.0 0.8 add.32
  85.8 0.0 collective-permute-start.9
  85.8 3.9 %collective-permute-done.9 = f32[64,128]{1,0:T(8,128)S(1)} collective-permute-done((f32[64,128]{1,0:T(8,128)S(1)}, f32[64,128]{1,0:T(8,128)S(1)}, u32[]{:S(2)}, u32[]{:S(2)}) %collective-permute-start.9) | collective-permute-done | bytes 32800 | tf_op jit(solution)/shard_map/ppermute | solution.py:675
  89.7 1.3 %collective-permute-start.10 = (f32[64,128]{1,0:T(8,128)S(1)}, f32[64,128]{1,0:T(8,128)S(1)}, u32[]{:S(2)}, u32[]{:S(2)}) collective-permute-start(f32[64,128]{1,0:T(8,128)S(1)} %add.33), channel_id=1, source_target_pairs={{0,4},{1,5},{2,6},{3,7},{4,0},{5,1},{6,2},{7,3},{8,12},{9,13},{10,... | collective-permute-start | bytes 98312 | tf_op jit(solution)/shard_map/ppermute | solution.py:675
  91.0 2.6 %collective-permute-done.10 = f32[64,128]{1,0:T(8,128)S(1)} collective-permute-done((f32[64,128]{1,0:T(8,128)S(1)}, f32[64,128]{1,0:T(8,128)S(1)}, u32[]{:S(2)}, u32[]{:S(2)}) %collective-permute-start.10) | collective-permute-done | bytes 32800 | tf_op jit(solution)/shard_map/ppermute | solution.py:675
  93.6 3.6 %collective-permute-start.11 = (f32[64,128]{1,0:T(8,128)S(1)}, f32[64,128]{1,0:T(8,128)S(1)}, u32[]{:S(2)}, u32[]{:S(2)}) collective-permute-start(f32[64,128]{1,0:T(8,128)S(1)} %add.34), channel_id=1, source_target_pairs={{0,8},{1,9},{2,10},{3,11},{4,12},{5,13},{6,14},{7,15},{8,0},{9,1},... | collective-permute-start | bytes 98312 | tf_op jit(solution)/shard_map/ppermute | solution.py:675
  97.2 2.2 %collective-permute-done.11 = f32[64,128]{1,0:T(8,128)S(1)} collective-permute-done((f32[64,128]{1,0:T(8,128)S(1)}, f32[64,128]{1,0:T(8,128)S(1)}, u32[]{:S(2)}, u32[]{:S(2)}) %collective-permute-start.11) | collective-permute-done | bytes 32800 | tf_op jit(solution)/shard_map/ppermute | solution.py:675
  99.4 0.6 add.35.total_ref
  100.0 19.4 %back.1 = (bf16[6,4096,256]{2,1,0:T(8,128)(2,1)}, f32[4,6]{1,0:T(4,128)}) custom-call(s32[2]{0:T(128)} %pad_add_fusion.place_ref, f32[64,128]{1,0:T(8,128)} %add.35.total_ref, f32[12,16]{1,0:T(8,128)} %add.31.every_ref, bf16[32,64,1792]{2,1,0:T(8,128)(2,1)} %get-tuple-element.16.slice_hbm, bf16[32,64,256]{2,1,0:T(8,128)(2,1)} %get-tuple-element.19.rows_ref, ...), custom_call_target="tpu_custom_call" | custom-call | tf_op jit(solution)/shard_map/back/pallas_call | solution.py:635
  (3 shorter events, 0.0 us)
Async XLA Ops:
  7.0 68.9 %all-to-all-start = ((bf16[16,136,256]{2,1,0:T(8,128)(2,1)}), bf16[16,136,256]{2,1,0:T(8,128)(2,1)S(1)}, u32[]{:S(2)}, u32[]{:S(2)}) async-start(bf16[16,136,256]{2,1,0:T(8,128)(2,1)} %pack.1), calls=%async_computation | async-start | bytes 2228224 | tf_op jit(solution)/shard_map/all_to_all | solution.py:562
  14.4 37.1 %collective-permute-start.5 = (bf16[7,160,256]{2,1,0:T(8,128)(2,1)}, bf16[7,160,256]{2,1,0:T(8,128)(2,1)S(1)}, u32[]{:S(2)}, u32[]{:S(2)}) collective-permute-start(bf16[7,160,256]{2,1,0:T(8,128)(2,1)} %get-tuple-element.13), channel_id=1, source_target_pairs={{1,0},{2,1},{3,2},{4,3},{5,4},{6,5},{7,6},{9,8},{10,9},{11,10},{12... | collective-permute-start | bytes 1720328 | tf_op jit(solution)/shard_map/ppermute | solution.py:546
  15.7 35.9 %collective-permute-start.6 = (bf16[7,160,256]{2,1,0:T(8,128)(2,1)}, bf16[7,160,256]{2,1,0:T(8,128)(2,1)S(1)}, u32[]{:S(2)}, u32[]{:S(2)}) collective-permute-start(bf16[7,160,256]{2,1,0:T(8,128)(2,1)} %get-tuple-element.14), channel_id=1, source_target_pairs={{0,1},{1,2},{2,3},{3,4},{4,5},{5,6},{6,7},{8,9},{9,10},{10,11},{11... | collective-permute-start | bytes 1720328 | tf_op jit(solution)/shard_map/ppermute | solution.py:547
  18.8 23.2 %collective-permute-start.2 = (f32[12,16]{1,0:T(8,128)}, f32[12,16]{1,0:T(8,128)S(1)}, u32[]{:S(2)}, u32[]{:S(2)}) collective-permute-start(f32[12,16]{1,0:T(8,128)} %get-tuple-element.12.mine_ref), channel_id=1, source_target_pairs={{0,4},{1,5},{2,6},{3,7},{4,0},{5,1},{6,2},{7,3},{8,12},{9,13},{10,... | collective-permute-start | bytes 2312 | tf_op jit(solution)/shard_map/ppermute | solution.py:680
  21.4 24.0 %collective-permute-start.1 = (f32[12,16]{1,0:T(8,128)}, f32[12,16]{1,0:T(8,128)S(1)}, u32[]{:S(2)}, u32[]{:S(2)}) collective-permute-start(f32[12,16]{1,0:T(8,128)} %get-tuple-element.12.mine_ref), channel_id=1, source_target_pairs={{0,12},{1,13},{2,14},{3,15},{4,8},{5,9},{6,10},{7,11},{8,4},{9,5},... | collective-permute-start | bytes 2312 | tf_op jit(solution)/shard_map/ppermute | solution.py:680
  23.3 22.1 %collective-permute-start = (f32[12,16]{1,0:T(8,128)}, f32[12,16]{1,0:T(8,128)S(1)}, u32[]{:S(2)}, u32[]{:S(2)}) collective-permute-start(f32[12,16]{1,0:T(8,128)} %get-tuple-element.12.mine_ref), channel_id=1, source_target_pairs={{0,8},{1,9},{2,10},{3,11},{4,12},{5,13},{6,14},{7,15},{8,0},{9,1},... | collective-permute-start | bytes 2312 | tf_op jit(solution)/shard_map/ppermute | solution.py:680
  41.9 9.6 %collective-permute-start.7 = (bf16[7,32,256]{2,1,0:T(8,128)(2,1)}, bf16[7,32,256]{2,1,0:T(8,128)(2,1)S(1)}, u32[]{:S(2)}, u32[]{:S(2)}) collective-permute-start(bf16[7,32,256]{2,1,0:T(8,128)(2,1)} %get-tuple-element.15), channel_id=1, source_target_pairs={{8,7},{7,8},{24,23},{23,24}} | collective-permute-start | bytes 344072 | tf_op jit(solution)/shard_map/ppermute | solution.py:548
  46.1 3.7 %collective-permute-start.3 = (f32[12,16]{1,0:T(8,128)S(1)}, f32[12,16]{1,0:T(8,128)S(1)}, u32[]{:S(2)}, u32[]{:S(2)}) collective-permute-start(f32[12,16]{1,0:T(8,128)S(1)} %add_add_fusion), channel_id=1, source_target_pairs={{0,2},{1,3},{2,0},{3,1},{4,6},{5,7},{6,4},{7,5},{8,10},{9,11},{10,... | collective-permute-start | bytes 2312 | tf_op jit(solution)/shard_map/ppermute | solution.py:675
  49.7 1.2 collective-permute-start.4
  51.5 0.7 copy-start.3
  51.5 0.8 copy-start.1
  52.4 0.9 copy-start.2
  76.0 1.0 copy-start
  83.5 1.5 %collective-permute-start.8 = (f32[64,128]{1,0:T(8,128)}, f32[64,128]{1,0:T(8,128)S(1)}, u32[]{:S(2)}, u32[]{:S(2)}) collective-permute-start(f32[64,128]{1,0:T(8,128)} %get-tuple-element.18), channel_id=1, source_target_pairs={{0,1},{1,0},{2,3},{3,2},{4,5},{5,4},{6,7},{7,6},{8,9},{9,8},{10,11... | collective-permute-start | bytes 98312 | tf_op jit(solution)/shard_map/ppermute | solution.py:675
  85.8 3.9 %collective-permute-start.9 = (f32[64,128]{1,0:T(8,128)S(1)}, f32[64,128]{1,0:T(8,128)S(1)}, u32[]{:S(2)}, u32[]{:S(2)}) collective-permute-start(f32[64,128]{1,0:T(8,128)S(1)} %add.32), channel_id=1, source_target_pairs={{0,2},{1,3},{2,0},{3,1},{4,6},{5,7},{6,4},{7,5},{8,10},{9,11},{10,... | collective-permute-start | bytes 98312 | tf_op jit(solution)/shard_map/ppermute | solution.py:675
  89.7 3.9 %collective-permute-start.10 = (f32[64,128]{1,0:T(8,128)S(1)}, f32[64,128]{1,0:T(8,128)S(1)}, u32[]{:S(2)}, u32[]{:S(2)}) collective-permute-start(f32[64,128]{1,0:T(8,128)S(1)} %add.33), channel_id=1, source_target_pairs={{0,4},{1,5},{2,6},{3,7},{4,0},{5,1},{6,2},{7,3},{8,12},{9,13},{10,... | collective-permute-start | bytes 98312 | tf_op jit(solution)/shard_map/ppermute | solution.py:675
  93.6 5.8 %collective-permute-start.11 = (f32[64,128]{1,0:T(8,128)S(1)}, f32[64,128]{1,0:T(8,128)S(1)}, u32[]{:S(2)}, u32[]{:S(2)}) collective-permute-start(f32[64,128]{1,0:T(8,128)S(1)} %add.34), channel_id=1, source_target_pairs={{0,8},{1,9},{2,10},{3,11},{4,12},{5,13},{6,14},{7,15},{8,0},{9,1},... | collective-permute-start | bytes 98312 | tf_op jit(solution)/shard_map/ppermute | solution.py:675

commit v3 on v2

v3 whole, which is shorter than its diff:
```python
import functools

import jax
import jax.numpy as jnp
from jax import lax
from jax.experimental import pallas as pl
from jax.experimental.pallas import tpu as pltpu
from jax.sharding import PartitionSpec as P

GRID = 256
HALF = GRID // 2
COMPS = 6
CHANS = COMPS + 1
TILE = 128
LANES = 128
PAIRS = [(k, l) for k in range(CHANS) for l in range(k, CHANS)]
PROJECT_AT = len(PAIRS)

f32 = jnp.float32
bf16 = jnp.bfloat16
i32 = jnp.int32


def iota(shape, dim):
    return lax.broadcasted_iota(i32, shape, dim)


def dot(a, b):
    return jnp.dot(a, b, preferred_element_type=f32)


def params(mebibytes):
    return pltpu.CompilerParams(vmem_limit_bytes=mebibytes * 1024 * 1024)


def plane_depth(position, tilt):
    numerator = (position - HALF) * tilt
    return jnp.right_shift(numerator, 7) + HALF, jnp.bitwise_and(numerator, HALF - 1)


def pack_kernel(sizes, tilt_ref, shift_ref, image_ref, out_ref, turned_ref):
    planes, slots, peers, count = sizes
    main_rows = count * slots
    shape = (peers * slots, GRID)
    row, col = iota(shape, 0), iota(shape, 1)
    slot_hit = jnp.bitwise_and(row - col, slots - 1) == 0
    first_hit = jnp.where(slot_hit, row // slots * planes, -1)
    for image in range(count):
        rows = slice(image * GRID, (image + 1) * GRID)
        for at in range(GRID // TILE):
            span = slice(at * TILE, (at + 1) * TILE)
            part = image_ref[rows, span].astype(f32)
            turned_ref[rows, span] = pltpu.roll(part, shift_ref[image], 1).astype(bf16)
        plane, _ = plane_depth(iota((1, GRID), 1), tilt_ref[image])
        hit = jnp.bitwise_and(plane, -planes) == first_hit
        found = dot(jnp.where(hit, 1.0, 0.0).astype(bf16), turned_ref[rows, :])
        found = found.reshape(peers, slots, GRID).astype(bf16)
        out_ref[:, image * slots : (image + 1) * slots, :] = found
    lane = iota((1, count * GRID), 1)
    tilt = jnp.full((1, count * GRID), tilt_ref[0], i32)
    for image in range(1, count):
        tilt = jnp.where(lane >= image * GRID, tilt_ref[image], tilt)
    plane, _ = plane_depth(jnp.bitwise_and(lane, GRID - 1), tilt)
    shape = (peers * 2 * count, count * GRID)
    row, col = iota(shape, 0), iota(shape, 1)
    hit = (row // 2 % count == col // GRID) & (row % 2 == col % 2)
    hit = hit & (plane == row // (2 * count) * planes - 1)
    found = dot(jnp.where(hit, 1.0, 0.0).astype(bf16), turned_ref[...])
    out_ref[:, main_rows:, :] = found.reshape(peers, 2 * count, GRID).astype(bf16)


def after_kernel(*refs):
    pass


def slot_order(slots, blocks):
    row, col = iota((GRID, GRID), 0), iota((GRID, GRID), 1)
    return (col == (row % blocks) * slots + row // blocks).astype(f32).astype(bf16)


WINDOW = 80


def window_starts(boundary):
    away = jnp.abs(boundary)
    nearest = jnp.where(boundary > 0, away - 1, away)
    furthest = jnp.minimum(jnp.where(boundary > 0, 2 * away - 1, 2 * away + 2), HALF)
    low = (HALF - furthest) // 16 * 16
    high = jnp.minimum((HALF + nearest) // 16 * 16, GRID - WINDOW)
    return low, high


def window_rows(boundary):
    low, high = window_starts(boundary)
    lane = iota((1, 2 * WINDOW), 1)
    below = jnp.where(low + lane < HALF, low + lane, -1)
    above = high + lane - WINDOW
    above = jnp.where(above >= HALF, above, -1)
    return jnp.where(lane < WINDOW, below, above)


def reached_starts(distance):
    away = jnp.abs(distance)
    nearest = jnp.where(away > 1, away, 0)
    furthest = jnp.minimum(2 * away + 2, HALF)
    low = jnp.minimum((HALF - furthest) // 16 * 16, HALF - 32)
    high = jnp.minimum(jnp.maximum((HALF + nearest) // 16 * 16, low + WINDOW), GRID - WINDOW)
    return low, high


def edges_kernel(planes, place_ref, mean_ref, comp_ref, mean_top_ref, comp_top_ref, near_ref, far_ref):
    bottom = place_ref[0] - HALF
    even = place_ref[1] % 2 == 0

    def fill(boundary, mean, comp, out):
        for chan in range(CHANS):
            plane = mean if chan == 0 else comp.at[chan - 1]
            for n, start in enumerate(window_starts(boundary)):
                rows = pl.ds(pl.multiple_of(start, 16), WINDOW)
                out[chan, n * WINDOW : (n + 1) * WINDOW, :] = plane[rows, :]

    @pl.when(even)
    def _():
        fill(bottom + planes, mean_top_ref, comp_top_ref, near_ref)
        fill(bottom, mean_ref, comp_ref, far_ref)

    @pl.when(jnp.logical_not(even))
    def _():
        fill(bottom, mean_ref, comp_ref, near_ref)
        fill(bottom + planes, mean_top_ref, comp_top_ref, far_ref)


def stream(step, parts, copies):
    @pl.when(step == 0)
    def _():
        for part in range(parts):
            for copy in copies(part):
                copy.start()

    @pl.when(step < parts)
    def _():
        for copy in copies(step):
            copy.wait()


def parameter_rows(every_ref, images):
    table = jnp.transpose(every_ref[:, 0, :])
    count = images // every_ref.shape[0]
    rows = []
    for n in range(3):
        parts = [table[n * count + at : n * count + at + 1, :] for at in range(count)]
        rows.append(jnp.concatenate(parts, axis=1))
    return rows


def columns(rows):
    fill = jnp.zeros((LANES - len(rows), rows[0].shape[1]), f32)
    return jnp.transpose(jnp.concatenate(rows + [fill], axis=0))


def interpolate(rows, weight, turn):
    parts = []
    for at in range(GRID // TILE):
        part = rows[:, at * TILE : (at + 1) * TILE]
        parts.append((1.0 - weight) * part + weight * pltpu.roll(part, turn, 1))
    return jnp.concatenate(parts, axis=1)


def extract_kernel(
    sizes, place_ref, every_ref, mean_hbm, comp_hbm, near_hbm, far_hbm,
    out_ref, extra_ref, gram_ref, blank_ref,
    near_ref, far_ref, edge_sem, zero_ref, zero_sem, mean_ref, comp_ref, mean_sem, comp_sem, table_ref, order_ref, sums_ref, column_ref,
):
    planes, slots, blocks, chunk, images, pair = sizes
    step, first = pl.program_id(0), place_ref[0]
    tables = planes // pair

    def copies(part):
        rows = pl.ds(pl.multiple_of(part * pair * GRID, GRID), pair * GRID)
        return (
            pltpu.make_async_copy(mean_hbm.at[rows], mean_ref.at[rows], mean_sem.at[part]),
            pltpu.make_async_copy(comp_hbm.at[:, rows], comp_ref.at[:, rows], comp_sem.at[part]),
        )

    stream(step, tables, copies)

    def blanks(part):
        rows = pl.ds(pl.multiple_of(part * GRID, GRID), GRID)
        return pltpu.make_async_copy(zero_ref, blank_ref.at[:, rows], zero_sem.at[part])

    @pl.when(step == 0)
    def _():
        zero_ref[...] = jnp.zeros_like(zero_ref)

    @pl.when(step == tables)
    def _():
        for part in range(planes):
            blanks(part).start()

    @pl.when(step == pl.num_programs(0) - 1)
    def _():
        for part in range(planes):
            blanks(part).wait()

    @pl.when(step == 0)
    def _():
        column_ref[...] = columns(parameter_rows(every_ref, images))

    tilt = column_ref[:, 0:1].astype(i32)
    weight = column_ref[:, 1:2] / 16.0
    own_rows = planes * blocks

    edges = (
        pltpu.make_async_copy(near_hbm, near_ref, edge_sem.at[0]),
        pltpu.make_async_copy(far_hbm, far_ref, edge_sem.at[1]),
    )

    @pl.when(step == 0)
    def _():
        for copy in edges:
            copy.start()
        order_ref[...] = slot_order(slots, blocks)
        sums_ref[...] = jnp.zeros_like(sums_ref)

    @pl.when(step == tables - 1)
    def _():
        for copy in edges:
            copy.wait()
        at_up, at_low = window_rows(first + planes - HALF), window_rows(first - HALF)
        row = iota((GRID, at_up.shape[1]), 0)
        order = (at_up == (row % blocks) * slots + row // blocks).astype(f32).astype(bf16)
        parts = []
        for odd in range(2):
            pieces = []
            for lane, part in ((at_low, 0), (iota((1, GRID), 1), 1)):
                plane, depth = plane_depth(lane, tilt)
                hit = (plane == first - 1) & (lane >= 0) & (jnp.bitwise_and(lane, 1) == odd)
                depth = depth if part else HALF - depth
                pieces.append(jnp.where(hit, depth, 0).astype(f32) / HALF)
            parts.append(pieces)
        mixing_low = jnp.concatenate([parts[0][0], parts[1][0]], axis=0).astype(bf16)
        mixing_own = jnp.concatenate([parts[0][1], parts[1][1]], axis=0).astype(bf16)
        weight2 = jnp.concatenate([weight, weight], axis=0)
        fill = table_ref.shape[1] - own_rows - blocks
        even = place_ref[1] % 2 == 0
        for chan in range(CHANS):
            at = slice(chan * GRID, (chan + 1) * GRID)
            near, far = near_ref[chan], far_ref[chan]
            upper = dot(order, jnp.where(even, near, far)).reshape(slots, blocks, GRID)
            if fill:
                upper = jnp.concatenate([upper, jnp.zeros((slots, fill, GRID), f32)], axis=1)
            table_ref[:, own_rows:, at] = upper.astype(bf16)
            own = mean_ref[:GRID, :] if chan == 0 else comp_ref[chan - 1, :GRID, :]
            blended = dot(mixing_low, jnp.where(even, far, near)) + dot(mixing_own, own)
            blended = blended.astype(bf16).astype(f32)
            extra_ref[:, at] = interpolate(blended, weight2, TILE - 1).astype(bf16)

    @pl.when(step < tables)
    def _():
        order = order_ref[...]
        rows = pl.ds(pl.multiple_of(step * pair * blocks, 16), pair * blocks)
        for chan in range(CHANS):
            pieces = []
            for at in range(pair):
                span = pl.ds(pl.multiple_of((step * pair + at) * GRID, GRID), GRID)
                plane = mean_ref[span, :] if chan == 0 else comp_ref[chan - 1, span, :]
                pieces.append(dot(order, plane).reshape(slots, blocks, GRID))
            both = jnp.concatenate(pieces, axis=1).astype(bf16)
            table_ref[:, rows, chan * GRID : (chan + 1) * GRID] = both

    @pl.when(step >= tables)
    def _():
        lane = iota((images, table_ref.shape[1]), 1)
        block_at, plane_at = lane % blocks, lane // blocks
        plane_at = jnp.where(plane_at > planes, -1000, plane_at) + first
        low_at = jnp.where(plane_at < first + planes, plane_at, -1000)
        high_at = jnp.where(plane_at > first, plane_at - 1, -1000)
        base = (block_at * slots - HALF) * tilt
        for at in range(chunk):
            slot = (step - tables) * chunk + at
            numerator = base + slot * tilt
            plane, depth = jnp.right_shift(numerator, 7) + HALF, jnp.bitwise_and(numerator, HALF - 1)
            mixing = jnp.where(plane == low_at, HALF - depth, jnp.where(plane == high_at, depth, 0))
            mixing = (mixing.astype(f32) * (1.0 / HALF)).astype(bf16)
            blended = dot(mixing, table_ref[slot])
            for chan in range(CHANS):
                span = slice(chan * GRID, (chan + 1) * GRID)
                part = blended[:, span].astype(bf16).astype(f32)
                part = interpolate(part, weight, TILE - 1).astype(bf16)
                out_ref[at, chan * images : (chan + 1) * images, :] = part
        gram_sums(chunk, images, out_ref, sums_ref)

    @pl.when(step == pl.num_programs(0) - 1)
    def _():
        lane = iota((images, LANES), 1)
        total = jnp.zeros((images, LANES), f32)
        for n in range(len(PAIRS)):
            total = jnp.where(lane == n, jnp.sum(sums_ref[n], axis=1, keepdims=True), total)
        gram_ref[...] = total


def gram_sums(chunk, images, out_ref, sums_ref):
    def accumulate(group, carry):
        start = pl.multiple_of(group * 16, 16)
        rows = pl.ds(start, 16)
        sums = [sums_ref[n, rows, :] for n in range(len(PAIRS))]
        for at in range(chunk):
            for tile in range(GRID // LANES):
                values = [
                    out_ref[at, pl.ds(chan * images + start, 16), pl.ds(tile * LANES, LANES)].astype(f32)
                    for chan in range(CHANS)
                ]
                for n, (k, l) in enumerate(PAIRS):
                    sums[n] = sums[n] + values[k] * values[l]
        for n in range(len(PAIRS)):
            sums_ref[n, rows, :] = sums[n]
        return carry

    lax.fori_loop(0, images // 16, accumulate, 0)


def project_kernel(
    sizes, got_ref, slice_ref, gram_ref, rows_ref, extra_ref, total_ref, wide_ref, sums_ref
):
    slots, chunk, images, peers, count = sizes
    stride = count * slots + 2 * count
    step = pl.program_id(0)

    @pl.when(step == 0)
    def _():
        for tile in range(GRID // LANES):
            wide_ref[tile] = got_ref[:, tile * LANES : (tile + 1) * LANES].astype(f32)
        sums_ref[...] = jnp.zeros_like(sums_ref)
        for odd in range(2):
            for image in range(count):
                start = count * slots + image * 2 + odd
                at = (odd * count + image) * peers
                for tile in range(GRID // LANES):
                    part = wide_ref[tile, pl.ds(start, peers, stride=stride), :]
                    extra_ref[at : at + peers, tile * LANES : (tile + 1) * LANES] = part.astype(bf16)

    for image in range(count):
        span = slice(image * peers, (image + 1) * peers)
        sums = [sums_ref[chan, span, :] for chan in range(CHANS)]
        for at in range(chunk):
            slot = step * chunk + at
            for tile in range(GRID // LANES):
                part = wide_ref[tile, pl.ds(image * slots + slot, peers, stride=stride), :]
                rows_ref[at, span, tile * LANES : (tile + 1) * LANES] = part.astype(bf16)
                for chan in range(CHANS):
                    at_rows = slice(chan * images + image * peers, chan * images + (image + 1) * peers)
                    lanes = slice(tile * LANES, (tile + 1) * LANES)
                    sums[chan] = sums[chan] + part * slice_ref[slot, at_rows, lanes].astype(f32)
        for chan in range(CHANS):
            sums_ref[chan, span, :] = sums[chan]

    @pl.when(step == pl.num_programs(0) - 1)
    def _():
        lane = iota((images, LANES), 1)
        total = gram_ref[...]
        for chan in range(CHANS):
            value = jnp.sum(sums_ref[chan], axis=1, keepdims=True)
            total = jnp.where(lane == PROJECT_AT + chan, value, total)
        total_ref[...] = total


def solve_rows(table, noise):
    count = float(GRID * GRID)

    def gram(k, l):
        at = PAIRS.index((min(k, l), max(k, l)))
        return table[at : at + 1, :]

    factor = [[None] * COMPS for _ in range(COMPS)]
    inverse = [None] * COMPS
    for col in range(COMPS):
        for row in range(col, COMPS):
            total = gram(row + 1, col + 1) / count
            if row == col:
                total = total + noise
            for at in range(col):
                total = total - factor[row][at] * factor[col][at]
            if row == col:
                inverse[col] = 1.0 / jnp.sqrt(total)
            else:
                factor[row][col] = total * inverse[col]
    forward = []
    for row in range(COMPS):
        at = PROJECT_AT + row + 1
        total = (table[at : at + 1, :] - gram(row + 1, 0)) / count
        for col in range(row):
            total = total - factor[row][col] * forward[col]
        forward.append(total * inverse[row])
    latent = [None] * COMPS
    for row in reversed(range(COMPS)):
        total = forward[row]
        for col in range(row + 1, COMPS):
            total = total - factor[col][row] * latent[col]
        latent[row] = total * inverse[row]
    return latent


def back_kernel(
    sizes, place_ref, part_ref, other_ref, every_ref,
    slice_ref, rows_ref, slice_extra_ref, rows_extra_ref, _,
    out_ref, latent_ref, reached_ref, reached_sem, stack_ref, row_ref, power_ref, tilt_ref, col_ref, free_ref, spill_ref, order_ref,
    depth_ref, share_at_ref, share_ref, combine_ref,
):
    planes, slots, blocks, chunk, images, steps, out_planes = sizes
    step, first = pl.program_id(0), place_ref[0]
    group = 2 if blocks % 16 else 1

    @pl.when(step == 0)
    def _():
        table = jnp.transpose(part_ref[...] + other_ref[...])
        tilt, frac, noise = parameter_rows(every_ref, images)
        latent = solve_rows(table, noise)
        free_ref[...] = columns(latent)
        count = latent_ref.shape[0]
        for image in range(count):
            at = image * (images // count) + place_ref[1]
            latent_ref[image : image + 1, :] = free_ref[pl.ds(at, 1), :COMPS]
        rounded = [value.astype(bf16).astype(f32) for value in latent]
        power = rounded[0] * rounded[0]
        for value in rounded[1:]:
            power = power + value * value
        rows = jnp.concatenate(rounded + [power, power], axis=0)
        row_ref[...] = jnp.concatenate([rows, rows, rows], axis=1).astype(bf16)
        power_ref[...] = jnp.concatenate([power, power], axis=1)
        tilt_ref[...] = jnp.concatenate([tilt, tilt, tilt], axis=1).astype(i32)
        col_ref[...] = columns(rounded + [power, tilt, frac])
        one = jnp.ones((1, images), f32)
        same = iota((images, images), 0) == iota((images, images), 1)
        parts = [jnp.where(same, value, 0.0) for value in [one] + rounded]
        combine_ref[...] = jnp.concatenate(parts, axis=1).astype(bf16)
        col = iota((WINDOW, GRID), 1)
        order_ref[...] = (col % blocks) * slots + col // blocks - iota((WINDOW, GRID), 0)

    def spread(total, rows, weight):
        residual = rows.astype(f32) - total
        return interpolate(residual.astype(bf16).astype(f32), weight, 1)

    weight = col_ref[:, COMPS + 2 : COMPS + 3] / 16.0

    @pl.when(step == 0)
    def _():
        latent = jnp.concatenate([col_ref[...]] * 2, axis=0)
        total = slice_extra_ref[:, :GRID].astype(f32)
        for k in range(COMPS):
            span = slice((k + 1) * GRID, (k + 2) * GRID)
            total = total + latent[:, k : k + 1] * slice_extra_ref[:, span].astype(f32)
        value = spread(total, rows_extra_ref[...], jnp.concatenate([weight, weight], axis=0))
        tilt = col_ref[:, COMPS + 1 : COMPS + 2].astype(i32)
        plane, depth = plane_depth(iota((images, GRID), 1), tilt)
        odd = jnp.bitwise_and(iota((images, GRID), 1), 1)
        for at in range(2):
            hit = (plane == first - 1) & (odd == at)
            part = jnp.sum(jnp.where(hit, depth, 0).astype(f32), axis=1, keepdims=True) / HALF
            span = slice(at * images, (at + 1) * images)
            spill_ref[span, :] = (part * value[span]).astype(bf16)
        slot_at = iota((images, LANES), 1)
        depths = jnp.zeros((images, LANES), f32)
        for block in range(blocks):
            plane, depth = plane_depth(block * slots + slot_at, tilt)
            live = (plane >= first) & (plane < first + planes)
            depths = depths + jnp.where(live, depth, 0).astype(f32)
        depth_ref[...] = depths / HALF
        shape = (GRID, 2 * images)
        low = iota(shape, 1) < images
        plane, depth = plane_depth(iota(shape, 0), tilt_ref[:, : 2 * images])
        share_at_ref[...] = jnp.where(low, plane, plane + 1)
        share_ref[...] = jnp.where(low, HALF - depth, depth).astype(f32) / HALF * power_ref[:, : 2 * images]

    @pl.when(step < steps)
    def _():
        tilt = tilt_ref[...]
        row = iota((blocks, 3 * images), 0)
        base = (row * slots - HALF) * tilt
        shape = (planes, blocks, 3 * images)
        plane_at, lane = iota(shape, 0), iota(shape, 2)
        wanted = jnp.where(lane < images, plane_at, plane_at - 1)
        wanted = jnp.where((lane < 2 * images) == (wanted < 0), -1000, wanted) + (first - HALF)
        depths = pltpu.roll(depth_ref[...], (LANES - step * chunk) % LANES, 1)
        rights, hits = [], []
        for at in range(chunk):
            slot = step * chunk + at
            value = spread(dot(combine_ref[...], slice_ref[slot]), rows_ref[at], weight)
            depth = depths[:, at : at + 1]
            odd = pl.ds(pl.multiple_of((slot % 2) * images, 16), images)
            low, high = ((1.0 - depth) * value).astype(bf16), (depth * value).astype(bf16)
            rights.append(jnp.concatenate([low, high, spill_ref[odd, :]], axis=0))
            plane = jnp.right_shift(base + slot * tilt, 7)
            hit = jnp.where(plane[None] == wanted, 1.0, 0.0)
            hits.append(hit.reshape(planes * blocks, 3 * images).astype(bf16))
        for start in range(0, chunk, group):
            pieces = [[] for _ in range(COMPS)]
            for at in range(start, start + group):
                left = jnp.concatenate([hits[at] * row_ref[k : k + 1, :] for k in range(COMPS)], axis=0)
                totals = dot(left, rights[at])
                for k in range(COMPS):
                    total = totals[k * planes * blocks : (k + 1) * planes * blocks]
                    pieces[k].append(total.reshape(planes, blocks, GRID))
            rows = pl.ds(pl.multiple_of((step * chunk + start) * blocks, 16), group * blocks)
            for k in range(COMPS):
                stack_ref[k, :, rows, :] = jnp.concatenate(pieces[k], axis=1).astype(bf16)

    def stores(plane):
        copies = []
        for n, start in enumerate(reached_starts(first + plane - HALF)):
            rows = pl.ds(pl.multiple_of(plane * GRID + start, 16), WINDOW)
            part = reached_ref.at[plane, :, pl.ds(n * WINDOW, WINDOW)]
            copies.append(pltpu.make_async_copy(part, out_ref.at[:, rows], reached_sem.at[2 * plane + n]))
        return copies

    @pl.when(step >= steps)
    def _():
        for at in range(out_planes):
            plane = (step - steps) * out_planes + at
            orders, shares = [], []
            for start in reached_starts(first + plane - HALF):
                rows = pl.ds(pl.multiple_of(start, 16), WINDOW)
                orders.append(jnp.where(order_ref[...] == start, 1.0, 0.0))
                shares.append(jnp.where(share_at_ref[rows, :] == first + plane, share_ref[rows, :], 0.0))
            order = jnp.concatenate(orders, axis=0).astype(bf16)
            share = jnp.concatenate(shares, axis=0)
            scale = 1.0 / (1.0 + jnp.sum(share, axis=1, keepdims=True))
            for k in range(COMPS):
                reached_ref[plane, k] = (dot(order, stack_ref[k, plane]) * scale).astype(bf16)
            for copy in stores(plane):
                copy.start()

    @pl.when(step == pl.num_programs(0) - 1)
    def _():
        for plane in range(planes):
            for copy in stores(plane):
                copy.wait()


def whole(shape):
    return pl.BlockSpec(shape, lambda *_: (0,) * len(shape))


def anywhere():
    return pl.BlockSpec(memory_space=pl.ANY)


def in_hbm(value):
    return pltpu.with_memory_space_constraint(value, pltpu.HBM)


def hbm():
    return pl.BlockSpec(memory_space=pltpu.HBM)


def smem():
    return pl.BlockSpec(memory_space=pltpu.SMEM)


def local(mean_volume, components, images, tilt, shift, frac, noise_var):
    peers = lax.axis_size("slab")
    me = lax.axis_index("slab")
    planes = mean_volume.shape[0] // GRID
    slots = 2 * planes
    blocks = GRID // slots
    count = images.shape[0]
    total = peers * count
    width = CHANS * GRID
    chunk = max(1, 256 // total)
    steps = slots // chunk
    pack_rows = count * slots + 2 * count
    upper_rows = -(-blocks // 16) * 16
    place = jnp.stack([me * planes, me]).astype(i32)

    mine = jnp.concatenate([tilt.astype(f32), frac.astype(f32), noise_var])
    mine = jnp.broadcast_to(jnp.pad(mine, (0, LANES - 3 * count)), (peers, 8, LANES))
    every = lax.all_to_all(mine, "slab", split_axis=0, concat_axis=0, tiled=True)

    wide = 2 * WINDOW
    top = planes - 1
    near, far = pl.pallas_call(
        functools.partial(edges_kernel, planes),
        out_shape=[jax.ShapeDtypeStruct((CHANS, wide, GRID), bf16)] * 2,
        grid=(1,),
        in_specs=[
            smem(),
            pl.BlockSpec((GRID, GRID), lambda n: (0, 0)),
            pl.BlockSpec((COMPS, GRID, GRID), lambda n: (0, 0, 0)),
            pl.BlockSpec((GRID, GRID), lambda n: (top, 0)),
            pl.BlockSpec((COMPS, GRID, GRID), lambda n: (0, top, 0)),
        ],
        out_specs=[whole((CHANS, wide, GRID))] * 2,
        compiler_params=params(56),
        cost_estimate=pl.CostEstimate(flops=0, bytes_accessed=6 * CHANS * wide * GRID, transcendentals=0),
        name="edges",
    )(place, mean_volume, components, mean_volume, components)
    near = lax.ppermute(near, "slab", [(n, n ^ 1) for n in range(peers)])
    far = lax.ppermute(far, "slab", [(n, n + 1 if n % 2 else n - 1) for n in range(1, peers - 1)])

    packed = pl.pallas_call(
        functools.partial(pack_kernel, (planes, slots, peers, count)),
        out_shape=jax.ShapeDtypeStruct((peers, pack_rows, GRID), bf16),
        in_specs=[smem(), smem(), whole((count * GRID, GRID))],
        out_specs=whole((peers, pack_rows, GRID)),
        scratch_shapes=[pltpu.VMEM((count * GRID, GRID), bf16)],
        grid=(1,),
        compiler_params=params(56),
        cost_estimate=pl.CostEstimate(
            flops=0, bytes_accessed=2 * (count * GRID + peers * pack_rows) * GRID, transcendentals=0
        ),
        name="pack",
    )(tilt, shift, images.reshape(count * GRID, GRID))
    packed = pl.pallas_call(
        after_kernel,
        out_shape=pltpu.HBM(packed.shape, bf16),
        in_specs=[hbm()] + [pl.BlockSpec(memory_space=pltpu.VMEM)] * 3,
        out_specs=hbm(),
        input_output_aliases={0: 0},
        compiler_params=params(4),
        name="after",
    )(in_hbm(packed), *(pltpu.with_memory_space_constraint(value, pltpu.VMEM) for value in (every, near, far)))
    got = lax.all_to_all(packed, "slab", split_axis=0, concat_axis=0, tiled=True)

    pair = 2 if blocks % 16 else 1
    tables = planes // pair
    table_rows = -(-(planes + 1) * blocks // 16) * 16
    slices, slices_extra, gram, blank = pl.pallas_call(
        functools.partial(extract_kernel, (planes, slots, blocks, chunk, total, pair)),
        out_shape=[
            pltpu.HBM((slots, CHANS * total, GRID), bf16),
            jax.ShapeDtypeStruct((2 * total, width), bf16),
            jax.ShapeDtypeStruct((total, LANES), f32),
            jax.ShapeDtypeStruct((COMPS, planes * GRID, GRID), bf16),
        ],
        grid=(tables + steps,),
        in_specs=[
            smem(),
            whole((peers, 8, LANES)),
            anywhere(),
            anywhere(),
            hbm(),
            hbm(),
        ],
        out_specs=[
            pl.BlockSpec((chunk, CHANS * total, GRID), lambda n: (jnp.maximum(n - tables, 0), 0, 0)),
            whole((2 * total, width)),
            whole((total, LANES)),
            anywhere(),
        ],
        scratch_shapes=[
            pltpu.VMEM((CHANS, wide, GRID), bf16),
            pltpu.VMEM((CHANS, wide, GRID), bf16),
            pltpu.SemaphoreType.DMA((2,)),
            pltpu.VMEM((COMPS, GRID, GRID), bf16),
            pltpu.SemaphoreType.DMA((planes,)),
            pltpu.VMEM((planes * GRID, GRID), bf16),
            pltpu.VMEM((COMPS, planes * GRID, GRID), bf16),
            pltpu.SemaphoreType.DMA((tables,)),
            pltpu.SemaphoreType.DMA((tables,)),
            pltpu.VMEM((slots, table_rows, width), bf16),
            pltpu.VMEM((GRID, GRID), bf16),
            pltpu.VMEM((len(PAIRS), total, LANES), f32),
            pltpu.VMEM((total, LANES), f32),
        ],
        compiler_params=params(44),
        name="extract",
    )(place, every, mean_volume, components, in_hbm(near), in_hbm(far))

    rows, rows_extra, partial = pl.pallas_call(
        functools.partial(project_kernel, (slots, chunk, total, peers, count)),
        out_shape=[
            jax.ShapeDtypeStruct((slots, total, GRID), bf16),
            jax.ShapeDtypeStruct((2 * total, GRID), bf16),
            jax.ShapeDtypeStruct((total, LANES), f32),
        ],
        grid=(steps,),
        in_specs=[
            whole((peers * pack_rows, GRID)),
            pl.BlockSpec(memory_space=pltpu.VMEM),
            whole((total, LANES)),
        ],
        out_specs=[
            pl.BlockSpec((chunk, total, GRID), lambda n: (n, 0, 0)),
            whole((2 * total, GRID)),
            whole((total, LANES)),
        ],
        scratch_shapes=[
            pltpu.VMEM((GRID // LANES, peers * pack_rows, LANES), f32),
            pltpu.VMEM((CHANS, total, LANES), f32),
        ],
        compiler_params=params(24),
        name="project",
    )(
        got.reshape(peers * pack_rows, GRID),
        pltpu.with_memory_space_constraint(slices, pltpu.VMEM),
        gram,
    )

    step = 1
    while step < peers // 2:
        partial = partial + lax.ppermute(partial, "slab", [(n, n ^ step) for n in range(peers)])
        step *= 2
    halves = partial, lax.ppermute(partial, "slab", [(n, n ^ step) for n in range(peers)])

    out_planes = 2
    last = steps - 1
    new_components, latents = pl.pallas_call(
        functools.partial(back_kernel, (planes, slots, blocks, chunk, total, steps, out_planes)),
        out_shape=[
            jax.ShapeDtypeStruct((COMPS, planes * GRID, GRID), bf16),
            jax.ShapeDtypeStruct((count, COMPS), f32),
        ],
        grid=(steps + planes // out_planes,),
        in_specs=[
            smem(),
            whole((total, LANES)),
            whole((total, LANES)),
            whole((peers, 8, LANES)),
            pl.BlockSpec(memory_space=pltpu.VMEM),
            pl.BlockSpec((chunk, total, GRID), lambda n: (jnp.minimum(n, last), 0, 0)),
            whole((2 * total, width)),
            whole((2 * total, GRID)),
            anywhere(),
        ],
        out_specs=[
            anywhere(),
            whole((count, COMPS)),
        ],
        scratch_shapes=[
            pltpu.VMEM((planes, COMPS, 2 * WINDOW, GRID), bf16),
            pltpu.SemaphoreType.DMA((2 * planes,)),
            pltpu.VMEM((COMPS, planes, GRID, GRID), bf16),
            pltpu.VMEM((8, 3 * total), bf16),
            pltpu.VMEM((1, 2 * total), f32),
            pltpu.VMEM((1, 3 * total), i32),
            pltpu.VMEM((total, LANES), f32),
            pltpu.VMEM((total, LANES), f32),
            pltpu.VMEM((2 * total, GRID), bf16),
            pltpu.VMEM((WINDOW, GRID), i32),
            pltpu.VMEM((total, LANES), f32),
            pltpu.VMEM((GRID, 2 * total), i32),
            pltpu.VMEM((GRID, 2 * total), f32),
            pltpu.VMEM((total, CHANS * total), bf16),
        ],
        input_output_aliases={8: 0},
        compiler_params=params(29),
        name="back",
    )(place, *halves, every, pltpu.with_memory_space_constraint(slices, pltpu.VMEM), rows, slices_extra, rows_extra, blank)
    return new_components, latents


def solution(mesh):
    placed = (
        P(("groups", "slab"), None),
        P(None, ("groups", "slab"), None),
        P(("groups", "slab"), None, None),
        P(("groups", "slab")),
        P(("groups", "slab")),
        P(("groups", "slab")),
        P(("groups", "slab")),
    )
    return jax.shard_map(
        local,
        mesh=mesh,
        in_specs=placed,
        out_specs=(P(None, ("groups", "slab"), None), P(("groups", "slab"), None)),
        check_vma=False,
    )
```

time: 120 us -> 90.9 us (0.76)
  waiting for transfers between devices: 35.7 us -> 10.7 us
  Pallas kernels: 54.3 us -> 46.7 us
  starting transfers between devices: 22.6 us -> 26 us
  local copies, waits for them, and re-layouts: 2.7 us -> 5.64 us
  other arithmetic: 3.35 us -> 0.76 us
    ppermute x12 -> x6, waiting for transfers between devices: 35.7 us -> 6.69 us  [the longest x4 6.69 us: local(): lax.ppermute(partial, 'slab', [(n, n ^ step) for n in range(peers)])]
    all_to_all x0 -> x1, starting transfers between devices: none -> 8.63 us  [local(): lax.all_to_all(mine, 'slab', split_axis=0, concat_axis=0, tiled=True)]
    ppermute x12 -> x6, starting transfers between devices: 15.2 us -> 9.8 us  [the longest x4 8.53 us: local(): lax.ppermute(partial, 'slab', [(n, n ^ step) for n in range(peers)])]
    pallas_call x1, Pallas kernels: 19.4 us -> 14.7 us  [local(): pl.pallas_call(functools.partial(back_kernel, (planes, slots, blocks, chu...]
    pallas_call x1, Pallas kernels: 6.58 us -> 2.16 us  [local(): pl.pallas_call(functools.partial(project_kernel, (slots, chunk, total, pe...]
    all_to_all x0 -> x1, waiting for transfers between devices: none -> 4.03 us  [local(): lax.all_to_all(mine, 'slab', split_axis=0, concat_axis=0, tiled=True)]
    add x7 -> x3, other arithmetic: 2.69 us -> 0.02 us  [local(): partial + lax.ppermute(partial, 'slab', [(n, n ^ step) for n in range(pee...]
    unnamed x8 -> x22, local copies, waits for them, and re-layouts: 2.7 us -> 5 us
  transfers between devices with their start and end apart: 13 -> 8, of which waited for: 8 -> 5; matrix products, arithmetic and copies ran while one was open for 1% -> 1% of each run, Pallas kernels for 19% -> 30%
where the time goes in v3:
time: 90.9 us; the launch traced here: 90.5 us
  Pallas kernels  46.7 us (51%)
  starting transfers between devices  26 us (29%)
  waiting for transfers between devices  10.7 us (12%)
  local copies, waits for them, and re-layouts  5.64 us (6%)
    pallas_call x1, Pallas kernels, local(): pl.pallas_call(functools.partial(extract_kernel, (planes, slots, blocks,...  24.3 us
    pallas_call x1, Pallas kernels, local(): pl.pallas_call(functools.partial(back_kernel, (planes, slots, blocks, chu...  14.7 us
    all_to_all x1, starting transfers between devices, local(): lax.all_to_all(mine, 'slab', split_axis=0, concat_axis=0, tiled=True)  8.63 us
    ppermute x4, starting transfers between devices, local(): lax.ppermute(partial, 'slab', [(n, n ^ step) for n in range(peers)])  8.53 us
    all_to_all x1, starting transfers between devices, local(): lax.all_to_all(packed, 'slab', split_axis=0, concat_axis=0, tiled=True)  7.56 us
    ppermute x4, waiting for transfers between devices, local(): lax.ppermute(partial, 'slab', [(n, n ^ step) for n in range(peers)])  6.69 us
    unnamed x22, local copies, waits for them, and re-layouts  5 us
    all_to_all x1, waiting for transfers between devices, local(): lax.all_to_all(mine, 'slab', split_axis=0, concat_axis=0, tiled=True)  4.03 us
  transfers between devices with their start and end apart: 8, of which 5 were waited for; matrix products, arithmetic and copies ran while one was open for 1% of the time, Pallas kernels for 30%

profile of v3, /device:TPU:0, one launch (start us, length us, event | category | flops | bytes accessed | tf_op | source)
XLA Modules:
  0.0 90.5 jit_solution(5914161445638418057)
XLA Ops:
  0.6 0.7 pad_add_fusion.place_ref
  1.3 0.0 copy-start.10
  1.3 0.0 copy-start.8
  1.3 0.0 copy-start.9
  1.3 2.6 %edges.1 = (bf16[7,160,256]{2,1,0:T(8,128)(2,1)}, bf16[7,160,256]{2,1,0:T(8,128)(2,1)}) custom-call(s32[2]{0:T(128)} %pad_add_fusion.place_ref, bf16[4096,256]{1,0:T(8,128)(2,1)} %mean_hbm.1, bf16[6,4096,256]{2,1,0:T(8,128)(2,1)} %comp_hbm.1, bf16[4096,256]{1,0:T(8,128)(2,1)} %mean_hbm.1, bf16[6,4096,256]{2,1,0:T(8,128)(2,1)} %comp_hbm.1), custom_call_target="tpu_custom_call" | custom-call | bytes 1720320 | tf_op jit(solution)/shard_map/edges/pallas_call | solution.py:580
  3.9 0.0 copy-start.2
  3.9 0.0 copy-start.7
  3.9 0.5 collective-permute-start
  4.4 0.8 collective-permute-start.1
  5.2 0.0 copy-done.10
  5.2 0.0 copy-done.8
  5.3 0.0 copy-done.9
  5.3 0.1 select_maximum_fusion
  5.3 0.6 broadcast_in_dim.3
  6.0 8.6 %all-to-all-start = ((f32[16,8,128]{2,1,0:T(8,128)}), f32[16,8,128]{2,1,0:T(8,128)S(1)}, u32[]{:S(2)}, u32[]{:S(2)}) async-start(f32[16,8,128]{2,1,0:T(8,128)} %broadcast_in_dim.3), calls=%async_computation | async-start | bytes 131072 | tf_op jit(solution)/shard_map/all_to_all | solution.py:576
  14.6 2.9 %pack.1.refs_0_ = bf16[16,136,256]{2,1,0:T(8,128)(2,1)} custom-call(s32[4]{0:T(128)} %tilt_ref.1, s32[4]{0:T(128)} %shift_ref.1, bf16[1024,256]{1,0:T(8,128)(2,1)} %bitcast.5), custom_call_target="tpu_custom_call" | custom-call | bytes 1638400 | tf_op jit(solution)/shard_map/pack/pallas_call | solution.py:599
  17.5 4.0 %all-to-all-done.refs_1_.every_ref = f32[16,8,128]{2,1,0:T(8,128)S(1)} async-done(((f32[16,8,128]{2,1,0:T(8,128)}), f32[16,8,128]{2,1,0:T(8,128)S(1)}, u32[]{:S(2)}, u32[]{:S(2)}) %all-to-all-start) | async-done | bytes 65568 | tf_op jit(solution)/shard_map/all_to_all | solution.py:576
  21.5 0.0 collective-permute-done.refs_2_.near_hbm
  21.5 0.0 copy-start.3
  21.5 0.0 collective-permute-done.1.refs_3_.far_hbm
  21.5 0.0 copy-start.4
  21.6 0.9 copy-done.3
  22.4 0.2 copy-done.4
  22.6 7.6 %all-to-all-start.1 = ((bf16[16,136,256]{2,1,0:T(8,128)(2,1)}), bf16[16,136,256]{2,1,0:T(8,128)(2,1)S(1)}, u32[]{:S(2)}, u32[]{:S(2)}) async-start(bf16[16,136,256]{2,1,0:T(8,128)(2,1)} %after.1), calls=%async_computation.1 | async-start | bytes 2228224 | tf_op jit(solution)/shard_map/all_to_all | solution.py:621
  30.2 0.0 copy-done.2
  30.2 0.0 copy-done.7
  30.2 24.3 %extract.1 = (bf16[32,448,256]{2,1,0:T(8,128)(2,1)}, bf16[128,1792]{1,0:T(8,128)(2,1)S(1)}, f32[64,128]{1,0:T(8,128)S(1)}, bf16[6,4096,256]{2,1,0:T(8,128)(2,1)}) custom-call(s32[2]{0:T(128)S(1)} %copy-done.7, f32[16,8,128]{2,1,0:T(8,128)S(1)} %all-to-all-done.refs_1_.every_ref, bf16[4096,256]{1,0:T(8,128)(2,1)S(1)} %copy-done.2, ...), custom_call_target="tpu_custom_call" | custom-call | tf_op jit(solution)/shard_map/extract/pallas_call | solution.py:626
  54.5 0.0 copy-start.5
  54.5 0.8 copy-done.5
  55.4 0.0 all-to-all-done.1
  55.4 0.0 copy-start
  55.4 3.1 %copy-done = bf16[32,448,256]{2,1,0:T(8,128)(2,1)S(1)} copy-done((bf16[32,448,256]{2,1,0:T(8,128)(2,1)S(1)}, bf16[32,448,256]{2,1,0:T(8,128)(2,1)}, u32[]{:S(2)}) %copy-start) | copy-done | bytes 7340056
  58.5 0.0 copy-start.1
  58.5 0.0 copy-start.6
  58.5 2.2 %project.1 = (bf16[32,64,256]{2,1,0:T(8,128)(2,1)S(1)}, bf16[128,256]{1,0:T(8,128)(2,1)S(1)}, f32[64,128]{1,0:T(8,128)S(1)}) custom-call(bf16[2176,256]{1,0:T(8,128)(2,1)S(1)} %bitcast.4, bf16[32,448,256]{2,1,0:T(8,128)(2,1)S(1)} %copy-done, f32[64,128]{1,0:T(8,128)S(1)} %get-tuple-element.14.gram_ref), custom_call_target="tpu_custom_call" | custom-call | tf_op jit(solution)/shard_map/project/pallas_call | solution.py:668
  60.6 0.5 collective-permute-start.2
  61.1 0.9 collective-permute-done.2
  62.0 1.9 %collective-permute-start.3 = (f32[64,128]{1,0:T(8,128)S(1)}, f32[64,128]{1,0:T(8,128)S(1)}, u32[]{:S(2)}, u32[]{:S(2)}) collective-permute-start(f32[64,128]{1,0:T(8,128)S(1)} %add.11), channel_id=1, source_target_pairs={{0,2},{1,3},{2,0},{3,1},{4,6},{5,7},{6,4},{7,5},{8,10},{9,11},{10,... | collective-permute-start | bytes 98312 | tf_op jit(solution)/shard_map/ppermute | solution.py:700
  63.8 2.0 %collective-permute-done.3 = f32[64,128]{1,0:T(8,128)S(1)} collective-permute-done((f32[64,128]{1,0:T(8,128)S(1)}, f32[64,128]{1,0:T(8,128)S(1)}, u32[]{:S(2)}, u32[]{:S(2)}) %collective-permute-start.3) | collective-permute-done | bytes 32800 | tf_op jit(solution)/shard_map/ppermute | solution.py:700
  65.9 2.7 %collective-permute-start.4 = (f32[64,128]{1,0:T(8,128)S(1)}, f32[64,128]{1,0:T(8,128)S(1)}, u32[]{:S(2)}, u32[]{:S(2)}) collective-permute-start(f32[64,128]{1,0:T(8,128)S(1)} %add.12), channel_id=1, source_target_pairs={{0,4},{1,5},{2,6},{3,7},{4,0},{5,1},{6,2},{7,3},{8,12},{9,13},{10,... | collective-permute-start | bytes 98312 | tf_op jit(solution)/shard_map/ppermute | solution.py:700
  68.6 1.9 %collective-permute-done.4 = f32[64,128]{1,0:T(8,128)S(1)} collective-permute-done((f32[64,128]{1,0:T(8,128)S(1)}, f32[64,128]{1,0:T(8,128)S(1)}, u32[]{:S(2)}, u32[]{:S(2)}) %collective-permute-start.4) | collective-permute-done | bytes 32800 | tf_op jit(solution)/shard_map/ppermute | solution.py:700
  70.5 3.5 %collective-permute-start.5 = (f32[64,128]{1,0:T(8,128)S(1)}, f32[64,128]{1,0:T(8,128)S(1)}, u32[]{:S(2)}, u32[]{:S(2)}) collective-permute-start(f32[64,128]{1,0:T(8,128)S(1)} %add.13.part_ref), channel_id=1, source_target_pairs={{0,8},{1,9},{2,10},{3,11},{4,12},{5,13},{6,14},{7,15},{8,0},{9,1},... | collective-permute-start | bytes 98312 | tf_op jit(solution)/shard_map/ppermute | solution.py:702
  74.0 1.9 %collective-permute-done.5.other_ref = f32[64,128]{1,0:T(8,128)S(1)} collective-permute-done((f32[64,128]{1,0:T(8,128)S(1)}, f32[64,128]{1,0:T(8,128)S(1)}, u32[]{:S(2)}, u32[]{:S(2)}) %collective-permute-start.5) | collective-permute-done | bytes 32800 | tf_op jit(solution)/shard_map/ppermute | solution.py:702
  75.9 0.0 copy-done.1
  75.9 0.0 copy-done.6
  75.9 14.7 %back.1 = (bf16[6,4096,256]{2,1,0:T(8,128)(2,1)}, f32[4,6]{1,0:T(4,128)}) custom-call(s32[2]{0:T(128)S(1)} %copy-done.7, f32[64,128]{1,0:T(8,128)S(1)} %add.13.part_ref, f32[64,128]{1,0:T(8,128)S(1)} %collective-permute-done.5.other_ref, f32[16,8,128]{2,1,0:T(8,128)S(1)} %all-to-all-done.refs_1_.every_ref, ...), custom_call_target="tpu_custom_call", output_to_operand_aliasing={{0}: (8, {})} | custom-call | tf_op jit(solution)/shard_map/back/pallas_call | solution.py:706
  (6 shorter events, 0.0 us)
Async XLA Ops:
  1.3 3.9 %copy-start.10 = (s32[4]{0:T(128)S(1)}, s32[4]{0:T(128)}, u32[]{:S(2)}) copy-start(s32[4]{0:T(128)} %param.12) | copy-start | bytes 52
  1.3 3.9 %copy-start.8 = (s32[4]{0:T(128)S(1)}, s32[4]{0:T(128)}, u32[]{:S(2)}) copy-start(s32[4]{0:T(128)} %tilt_ref.1) | copy-start | bytes 52
  1.3 4.0 %copy-start.9 = (f32[4]{0:T(128)S(1)}, f32[4]{0:T(128)}, u32[]{:S(2)}) copy-start(f32[4]{0:T(128)} %param.13) | copy-start | bytes 52
  3.9 26.3 %copy-start.2 = (bf16[4096,256]{1,0:T(8,128)(2,1)S(1)}, bf16[4096,256]{1,0:T(8,128)(2,1)}, u32[]{:S(2)}) copy-start(bf16[4096,256]{1,0:T(8,128)(2,1)} %mean_hbm.1) | copy-start | bytes 6291460
  3.9 26.3 %copy-start.7 = (s32[2]{0:T(128)S(1)}, s32[2]{0:T(128)}, u32[]{:S(2)}) copy-start(s32[2]{0:T(128)} %pad_add_fusion.place_ref) | copy-start | bytes 28
  3.9 17.6 %collective-permute-start = (bf16[7,160,256]{2,1,0:T(8,128)(2,1)}, bf16[7,160,256]{2,1,0:T(8,128)(2,1)S(1)}, u32[]{:S(2)}, u32[]{:S(2)}) collective-permute-start(bf16[7,160,256]{2,1,0:T(8,128)(2,1)} %get-tuple-element.11), channel_id=1, source_target_pairs={{0,1},{1,0},{2,3},{3,2},{4,5},{5,4},{6,7},{7,6},{8,9},{9,8},{10,11... | collective-permute-start | bytes 1720328 | tf_op jit(solution)/shard_map/ppermute | solution.py:596
  4.4 17.1 %collective-permute-start.1 = (bf16[7,160,256]{2,1,0:T(8,128)(2,1)}, bf16[7,160,256]{2,1,0:T(8,128)(2,1)S(1)}, u32[]{:S(2)}, u32[]{:S(2)}) collective-permute-start(bf16[7,160,256]{2,1,0:T(8,128)(2,1)} %get-tuple-element.12), channel_id=1, source_target_pairs={{1,2},{2,1},{3,4},{4,3},{5,6},{6,5},{7,8},{8,7},{9,10},{10,9},{11,... | collective-permute-start | bytes 1720328 | tf_op jit(solution)/shard_map/ppermute | solution.py:597
  6.0 15.5 %all-to-all-start = ((f32[16,8,128]{2,1,0:T(8,128)}), f32[16,8,128]{2,1,0:T(8,128)S(1)}, u32[]{:S(2)}, u32[]{:S(2)}) async-start(f32[16,8,128]{2,1,0:T(8,128)} %broadcast_in_dim.3), calls=%async_computation | async-start | bytes 131072 | tf_op jit(solution)/shard_map/all_to_all | solution.py:576
  21.5 0.9 %copy-start.3 = (bf16[7,160,256]{2,1,0:T(8,128)(2,1)}, bf16[7,160,256]{2,1,0:T(8,128)(2,1)S(1)}, u32[]{:S(2)}) copy-start(bf16[7,160,256]{2,1,0:T(8,128)(2,1)S(1)} %collective-permute-done.refs_2_.near_hbm) | copy-start | bytes 1720324
  21.5 1.1 %copy-start.4 = (bf16[7,160,256]{2,1,0:T(8,128)(2,1)}, bf16[7,160,256]{2,1,0:T(8,128)(2,1)S(1)}, u32[]{:S(2)}) copy-start(bf16[7,160,256]{2,1,0:T(8,128)(2,1)S(1)} %collective-permute-done.1.refs_3_.far_hbm) | copy-start | bytes 1720324
  22.6 32.7 %all-to-all-start.1 = ((bf16[16,136,256]{2,1,0:T(8,128)(2,1)}), bf16[16,136,256]{2,1,0:T(8,128)(2,1)S(1)}, u32[]{:S(2)}, u32[]{:S(2)}) async-start(bf16[16,136,256]{2,1,0:T(8,128)(2,1)} %after.1), calls=%async_computation.1 | async-start | bytes 2228224 | tf_op jit(solution)/shard_map/all_to_all | solution.py:621
  54.5 0.8 copy-start.5
  55.4 3.1 %copy-start = (bf16[32,448,256]{2,1,0:T(8,128)(2,1)S(1)}, bf16[32,448,256]{2,1,0:T(8,128)(2,1)}, u32[]{:S(2)}) copy-start(bf16[32,448,256]{2,1,0:T(8,128)(2,1)} %get-tuple-element.13.slice_ref) | copy-start | bytes 22020100
  58.5 17.4 %copy-start.1 = (bf16[32,448,256]{2,1,0:T(8,128)(2,1)S(1)}, bf16[32,448,256]{2,1,0:T(8,128)(2,1)}, u32[]{:S(2)}) copy-start(bf16[32,448,256]{2,1,0:T(8,128)(2,1)} %get-tuple-element.13.slice_ref) | copy-start | bytes 22020100
  58.5 17.4 %copy-start.6 = (bf16[128,1792]{1,0:T(8,128)(2,1)S(1)}, bf16[128,1792]{1,0:T(8,128)(2,1)}, u32[]{:S(2)}) copy-start(bf16[128,1792]{1,0:T(8,128)(2,1)} %copy-done.5) | copy-start | bytes 1376260
  60.6 1.3 %collective-permute-start.2 = (f32[64,128]{1,0:T(8,128)S(1)}, f32[64,128]{1,0:T(8,128)S(1)}, u32[]{:S(2)}, u32[]{:S(2)}) collective-permute-start(f32[64,128]{1,0:T(8,128)S(1)} %get-tuple-element.15), channel_id=1, source_target_pairs={{0,1},{1,0},{2,3},{3,2},{4,5},{5,4},{6,7},{7,6},{8,9},{9,8},{10,11... | collective-permute-start | bytes 98312 | tf_op jit(solution)/shard_map/ppermute | solution.py:700
  62.0 3.9 %collective-permute-start.3 = (f32[64,128]{1,0:T(8,128)S(1)}, f32[64,128]{1,0:T(8,128)S(1)}, u32[]{:S(2)}, u32[]{:S(2)}) collective-permute-start(f32[64,128]{1,0:T(8,128)S(1)} %add.11), channel_id=1, source_target_pairs={{0,2},{1,3},{2,0},{3,1},{4,6},{5,7},{6,4},{7,5},{8,10},{9,11},{10,... | collective-permute-start | bytes 98312 | tf_op jit(solution)/shard_map/ppermute | solution.py:700
  65.9 4.6 %collective-permute-start.4 = (f32[64,128]{1,0:T(8,128)S(1)}, f32[64,128]{1,0:T(8,128)S(1)}, u32[]{:S(2)}, u32[]{:S(2)}) collective-permute-start(f32[64,128]{1,0:T(8,128)S(1)} %add.12), channel_id=1, source_target_pairs={{0,4},{1,5},{2,6},{3,7},{4,0},{5,1},{6,2},{7,3},{8,12},{9,13},{10,... | collective-permute-start | bytes 98312 | tf_op jit(solution)/shard_map/ppermute | solution.py:700
  70.5 5.4 %collective-permute-start.5 = (f32[64,128]{1,0:T(8,128)S(1)}, f32[64,128]{1,0:T(8,128)S(1)}, u32[]{:S(2)}, u32[]{:S(2)}) collective-permute-start(f32[64,128]{1,0:T(8,128)S(1)} %add.13.part_ref), channel_id=1, source_target_pairs={{0,8},{1,9},{2,10},{3,11},{4,12},{5,13},{6,14},{7,15},{8,0},{9,1},... | collective-permute-start | bytes 98312 | tf_op jit(solution)/shard_map/ppermute | solution.py:702

commit v4 on v3

--- a/solution.py
+++ b/solution.py
@@ -13,8 +13,8 @@
 CHANS = COMPS + 1
 TILE = 128
 LANES = 128
-PAIRS = [(k, l) for k in range(CHANS) for l in range(k, CHANS)]
-PROJECT_AT = len(PAIRS)
+PAIRS = [(k, l) for k in range(CHANS) for l in range(k, CHANS + 1)]
+NOISE_AT = len(PAIRS)
 
 f32 = jnp.float32
 bf16 = jnp.bfloat16
@@ -38,7 +38,10 @@
     return jnp.right_shift(numerator, 7) + HALF, jnp.bitwise_and(numerator, HALF - 1)
 
 
-def pack_kernel(sizes, tilt_ref, shift_ref, image_ref, out_ref, turned_ref):
+PARAMETERS = 8
+
+
+def pack_kernel(sizes, tilt_ref, shift_ref, frac_ref, image_ref, out_ref, turned_ref):
     planes, slots, peers, count = sizes
     main_rows = count * slots
     shape = (peers * slots, GRID)
@@ -66,11 +69,14 @@
     hit = (row // 2 % count == col // GRID) & (row % 2 == col % 2)
     hit = hit & (plane == row // (2 * count) * planes - 1)
     found = dot(jnp.where(hit, 1.0, 0.0).astype(bf16), turned_ref[...])
-    out_ref[:, main_rows:, :] = found.reshape(peers, 2 * count, GRID).astype(bf16)
-
-
-def after_kernel(*refs):
-    pass
+    found = found.reshape(peers, 2 * count, GRID)
+    row, lane = iota((PARAMETERS, GRID), 0), iota((PARAMETERS, GRID), 1)
+    values = jnp.zeros((PARAMETERS, GRID), f32)
+    for image in range(count):
+        value = jnp.where(lane == 0, tilt_ref[image], jnp.where(lane == 1, frac_ref[image], 0))
+        values = jnp.where(row == image, value.astype(f32), values)
+    values = jnp.broadcast_to(values[None], (peers, PARAMETERS, GRID))
+    out_ref[:, main_rows:, :] = jnp.concatenate([found, values], axis=1).astype(bf16)
 
 
 def slot_order(slots, blocks):
@@ -79,6 +85,7 @@
 
 
 WINDOW = 80
+MIDDLE = 32
 
 
 def window_starts(boundary):
@@ -92,11 +99,13 @@
 
 def window_rows(boundary):
     low, high = window_starts(boundary)
-    lane = iota((1, 2 * WINDOW), 1)
-    below = jnp.where(low + lane < HALF, low + lane, -1)
+    lane = iota((1, 2 * WINDOW + MIDDLE), 1)
+    off_middle = boundary != 0
+    below = jnp.where(off_middle & (low + lane < HALF), low + lane, -1)
     above = high + lane - WINDOW
-    above = jnp.where(above >= HALF, above, -1)
-    return jnp.where(lane < WINDOW, below, above)
+    above = jnp.where(off_middle & (above >= HALF), above, -1)
+    middle = jnp.where(off_middle, -1, HALF - MIDDLE // 2 + lane - 2 * WINDOW)
+    return jnp.where(lane < WINDOW, below, jnp.where(lane < 2 * WINDOW, above, middle))
 
 
 def reached_starts(distance):
@@ -108,7 +117,9 @@
     return low, high
 
 
-def edges_kernel(planes, place_ref, mean_ref, comp_ref, mean_top_ref, comp_top_ref, near_ref, far_ref):
+def edges_kernel(
+    planes, place_ref, mean_ref, comp_ref, mean_top_ref, comp_top_ref, near_ref, far_ref, middle_ref
+):
     bottom = place_ref[0] - HALF
     even = place_ref[1] % 2 == 0
 
@@ -118,6 +129,8 @@
             for n, start in enumerate(window_starts(boundary)):
                 rows = pl.ds(pl.multiple_of(start, 16), WINDOW)
                 out[chan, n * WINDOW : (n + 1) * WINDOW, :] = plane[rows, :]
+            if out is far_ref:
+                middle_ref[chan] = plane[HALF - MIDDLE // 2 : HALF + MIDDLE // 2, :]
 
     @pl.when(even)
     def _():
@@ -141,16 +154,6 @@
     def _():
         for copy in copies(step):
             copy.wait()
-
-
-def parameter_rows(every_ref, images):
-    table = jnp.transpose(every_ref[:, 0, :])
-    count = images // every_ref.shape[0]
-    rows = []
-    for n in range(3):
-        parts = [table[n * count + at : n * count + at + 1, :] for at in range(count)]
-        rows.append(jnp.concatenate(parts, axis=1))
-    return rows
 
 
 def columns(rows):
@@ -166,12 +169,11 @@
     return jnp.concatenate(parts, axis=1)
 
 
-def extract_kernel(
-    sizes, place_ref, every_ref, mean_hbm, comp_hbm, near_hbm, far_hbm,
-    out_ref, extra_ref, gram_ref, blank_ref,
-    near_ref, far_ref, edge_sem, zero_ref, zero_sem, mean_ref, comp_ref, mean_sem, comp_sem, table_ref, order_ref, sums_ref, column_ref,
+def table_kernel(
+    sizes, place_ref, mean_hbm, comp_hbm, out_ref, blank_ref,
+    mean_ref, comp_ref, mean_sem, comp_sem, order_ref, zero_ref, zero_sem,
 ):
-    planes, slots, blocks, chunk, images, pair = sizes
+    planes, slots, blocks, pair = sizes
     step, first = pl.program_id(0), place_ref[0]
     tables = planes // pair
 
@@ -182,50 +184,100 @@
             pltpu.make_async_copy(comp_hbm.at[:, rows], comp_ref.at[:, rows], comp_sem.at[part]),
         )
 
+    def blanks(plane):
+        low, high = reached_starts(first + plane - HALF)
+        parts = []
+        for n in range((GRID - 2 * WINDOW) // 16):
+            start = jnp.where(n * 16 >= low, n * 16 + WINDOW, n * 16)
+            start = jnp.where(start >= high, start + WINDOW, start)
+            rows = pl.ds(pl.multiple_of(plane * GRID + start, 16), 16)
+            parts.append(pltpu.make_async_copy(zero_ref, blank_ref.at[:, rows], zero_sem.at[plane, n]))
+        return parts
+
+    @pl.when(step == 0)
+    def _():
+        zero_ref[...] = jnp.zeros_like(zero_ref)
+        order_ref[...] = slot_order(slots, blocks)
+
     stream(step, tables, copies)
-
-    def blanks(part):
-        rows = pl.ds(pl.multiple_of(part * GRID, GRID), GRID)
-        return pltpu.make_async_copy(zero_ref, blank_ref.at[:, rows], zero_sem.at[part])
+    for at in range(pair):
+        for copy in blanks(step * pair + at):
+            copy.start()
+    order = order_ref[...]
+    for chan in range(CHANS):
+        pieces = []
+        for at in range(pair):
+            span = pl.ds(pl.multiple_of((step * pair + at) * GRID, GRID), GRID)
+            plane = mean_ref[span, :] if chan == 0 else comp_ref[chan - 1, span, :]
+            pieces.append(dot(order, plane).reshape(slots, blocks, GRID))
+        out_ref[:, :, chan * GRID : (chan + 1) * GRID] = jnp.concatenate(pieces, axis=1).astype(bf16)
+
+    @pl.when(step == tables - 1)
+    def _():
+        for plane in range(planes):
+            for copy in blanks(plane):
+                copy.wait()
+
+
+def extract_kernel(
+    sizes, place_ref, noise_ref, got_hbm, near_hbm, far_hbm, middle_hbm, mean_hbm, comp_hbm, table_hbm,
+    out_ref, rows_ref, extra_ref, rows_extra_ref, total_ref, column_ref,
+    got_ref, near_ref, far_ref, middle_ref, own_ref, table_ref, edge_sem, table_sem,
+    wide_ref, upper_ref, sums_ref,
+):
+    planes, slots, blocks, chunk, images, peers = sizes
+    step, first = pl.program_id(0), place_ref[0]
+    count = images // peers
+    stride = count * slots + 2 * count + PARAMETERS
+    one_plane = pl.ds(0, GRID)
+    edges = (
+        pltpu.make_async_copy(got_hbm, got_ref, edge_sem.at[0]),
+        pltpu.make_async_copy(near_hbm, near_ref, edge_sem.at[1]),
+        pltpu.make_async_copy(far_hbm, far_ref, edge_sem.at[2]),
+        pltpu.make_async_copy(middle_hbm, middle_ref, edge_sem.at[3]),
+        pltpu.make_async_copy(mean_hbm.at[one_plane], own_ref.at[0], edge_sem.at[4]),
+        pltpu.make_async_copy(comp_hbm.at[:, one_plane], own_ref.at[pl.ds(1, COMPS)], edge_sem.at[5]),
+    )
+
+    def copies(part):
+        at = pl.ds(part * chunk, chunk)
+        return (pltpu.make_async_copy(table_hbm.at[at], table_ref.at[at], table_sem.at[part]),)
 
     @pl.when(step == 0)
     def _():
-        zero_ref[...] = jnp.zeros_like(zero_ref)
-
-    @pl.when(step == tables)
-    def _():
-        for part in range(planes):
-            blanks(part).start()
-
-    @pl.when(step == pl.num_programs(0) - 1)
-    def _():
-        for part in range(planes):
-            blanks(part).wait()
+        for copy in edges:
+            copy.start()
 
     @pl.when(step == 0)
     def _():
-        column_ref[...] = columns(parameter_rows(every_ref, images))
+        for part in range(slots // chunk):
+            copies(part)[0].start()
+        edges[0].wait()
+        for tile in range(GRID // LANES):
+            wide_ref[tile] = got_ref[:, tile * LANES : (tile + 1) * LANES].astype(f32)
+        for image in range(count):
+            span = slice(image * peers, (image + 1) * peers)
+            start = stride - PARAMETERS + image
+            column_ref[span, :] = wide_ref[0, pl.ds(start, peers, stride=stride), :]
+            for odd in range(2):
+                start = count * slots + image * 2 + odd
+                at = (odd * count + image) * peers
+                for tile in range(GRID // LANES):
+                    part = wide_ref[tile, pl.ds(start, peers, stride=stride), :]
+                    rows_extra_ref[at : at + peers, tile * LANES : (tile + 1) * LANES] = part.astype(bf16)
+        sums_ref[...] = jnp.zeros_like(sums_ref)
+        for copy in edges[1:]:
+            copy.wait()
+
+    @pl.when(step < slots // chunk)
+    def _():
+        copies(step)[0].wait()
 
     tilt = column_ref[:, 0:1].astype(i32)
     weight = column_ref[:, 1:2] / 16.0
-    own_rows = planes * blocks
-
-    edges = (
-        pltpu.make_async_copy(near_hbm, near_ref, edge_sem.at[0]),
-        pltpu.make_async_copy(far_hbm, far_ref, edge_sem.at[1]),
-    )
 
     @pl.when(step == 0)
     def _():
-        for copy in edges:
-            copy.start()
-        order_ref[...] = slot_order(slots, blocks)
-        sums_ref[...] = jnp.zeros_like(sums_ref)
-
-    @pl.when(step == tables - 1)
-    def _():
-        for copy in edges:
-            copy.wait()
         at_up, at_low = window_rows(first + planes - HALF), window_rows(first - HALF)
         row = iota((GRID, at_up.shape[1]), 0)
         order = (at_up == (row % blocks) * slots + row // blocks).astype(f32).astype(bf16)
@@ -241,127 +293,80 @@
         mixing_low = jnp.concatenate([parts[0][0], parts[1][0]], axis=0).astype(bf16)
         mixing_own = jnp.concatenate([parts[0][1], parts[1][1]], axis=0).astype(bf16)
         weight2 = jnp.concatenate([weight, weight], axis=0)
-        fill = table_ref.shape[1] - own_rows - blocks
+        fill = upper_ref.shape[1] - blocks
         even = place_ref[1] % 2 == 0
         for chan in range(CHANS):
             at = slice(chan * GRID, (chan + 1) * GRID)
-            near, far = near_ref[chan], far_ref[chan]
-            upper = dot(order, jnp.where(even, near, far)).reshape(slots, blocks, GRID)
+            near, far, middle = near_ref[chan], far_ref[chan], middle_ref[chan]
+            upper = jnp.concatenate([jnp.where(even, near, far), middle], axis=0)
+            upper = dot(order, upper).reshape(slots, blocks, GRID)
             if fill:
                 upper = jnp.concatenate([upper, jnp.zeros((slots, fill, GRID), f32)], axis=1)
-            table_ref[:, own_rows:, at] = upper.astype(bf16)
-            own = mean_ref[:GRID, :] if chan == 0 else comp_ref[chan - 1, :GRID, :]
-            blended = dot(mixing_low, jnp.where(even, far, near)) + dot(mixing_own, own)
+            upper_ref[:, :, at] = upper.astype(bf16)
+            lower = jnp.concatenate([jnp.where(even, far, near), middle], axis=0)
+            blended = dot(mixing_low, lower) + dot(mixing_own, own_ref[chan])
             blended = blended.astype(bf16).astype(f32)
             extra_ref[:, at] = interpolate(blended, weight2, TILE - 1).astype(bf16)
 
-    @pl.when(step < tables)
-    def _():
-        order = order_ref[...]
-        rows = pl.ds(pl.multiple_of(step * pair * blocks, 16), pair * blocks)
-        for chan in range(CHANS):
-            pieces = []
-            for at in range(pair):
-                span = pl.ds(pl.multiple_of((step * pair + at) * GRID, GRID), GRID)
-                plane = mean_ref[span, :] if chan == 0 else comp_ref[chan - 1, span, :]
-                pieces.append(dot(order, plane).reshape(slots, blocks, GRID))
-            both = jnp.concatenate(pieces, axis=1).astype(bf16)
-            table_ref[:, rows, chan * GRID : (chan + 1) * GRID] = both
-
-    @pl.when(step >= tables)
-    def _():
-        lane = iota((images, table_ref.shape[1]), 1)
-        block_at, plane_at = lane % blocks, lane // blocks
-        plane_at = jnp.where(plane_at > planes, -1000, plane_at) + first
-        low_at = jnp.where(plane_at < first + planes, plane_at, -1000)
-        high_at = jnp.where(plane_at > first, plane_at - 1, -1000)
-        base = (block_at * slots - HALF) * tilt
-        for at in range(chunk):
-            slot = (step - tables) * chunk + at
-            numerator = base + slot * tilt
-            plane, depth = jnp.right_shift(numerator, 7) + HALF, jnp.bitwise_and(numerator, HALF - 1)
-            mixing = jnp.where(plane == low_at, HALF - depth, jnp.where(plane == high_at, depth, 0))
-            mixing = (mixing.astype(f32) * (1.0 / HALF)).astype(bf16)
-            blended = dot(mixing, table_ref[slot])
-            for chan in range(CHANS):
-                span = slice(chan * GRID, (chan + 1) * GRID)
-                part = blended[:, span].astype(bf16).astype(f32)
-                part = interpolate(part, weight, TILE - 1).astype(bf16)
-                out_ref[at, chan * images : (chan + 1) * images, :] = part
-        gram_sums(chunk, images, out_ref, sums_ref)
-
-    @pl.when(step == pl.num_programs(0) - 1)
-    def _():
-        lane = iota((images, LANES), 1)
-        total = jnp.zeros((images, LANES), f32)
-        for n in range(len(PAIRS)):
-            total = jnp.where(lane == n, jnp.sum(sums_ref[n], axis=1, keepdims=True), total)
-        gram_ref[...] = total
-
-
-def gram_sums(chunk, images, out_ref, sums_ref):
-    def accumulate(group, carry):
-        start = pl.multiple_of(group * 16, 16)
-        rows = pl.ds(start, 16)
-        sums = [sums_ref[n, rows, :] for n in range(len(PAIRS))]
-        for at in range(chunk):
-            for tile in range(GRID // LANES):
-                values = [
-                    out_ref[at, pl.ds(chan * images + start, 16), pl.ds(tile * LANES, LANES)].astype(f32)
-                    for chan in range(CHANS)
-                ]
-                for n, (k, l) in enumerate(PAIRS):
-                    sums[n] = sums[n] + values[k] * values[l]
-        for n in range(len(PAIRS)):
-            sums_ref[n, rows, :] = sums[n]
-        return carry
-
-    lax.fori_loop(0, images // 16, accumulate, 0)
-
-
-def project_kernel(
-    sizes, got_ref, slice_ref, gram_ref, rows_ref, extra_ref, total_ref, wide_ref, sums_ref
-):
-    slots, chunk, images, peers, count = sizes
-    stride = count * slots + 2 * count
-    step = pl.program_id(0)
-
-    @pl.when(step == 0)
-    def _():
-        for tile in range(GRID // LANES):
-            wide_ref[tile] = got_ref[:, tile * LANES : (tile + 1) * LANES].astype(f32)
-        sums_ref[...] = jnp.zeros_like(sums_ref)
-        for odd in range(2):
-            for image in range(count):
-                start = count * slots + image * 2 + odd
-                at = (odd * count + image) * peers
-                for tile in range(GRID // LANES):
-                    part = wide_ref[tile, pl.ds(start, peers, stride=stride), :]
-                    extra_ref[at : at + peers, tile * LANES : (tile + 1) * LANES] = part.astype(bf16)
-
-    for image in range(count):
-        span = slice(image * peers, (image + 1) * peers)
-        sums = [sums_ref[chan, span, :] for chan in range(CHANS)]
-        for at in range(chunk):
-            slot = step * chunk + at
+    lane = iota((images, planes * blocks + upper_ref.shape[1]), 1)
+    block_at, plane_at = lane % blocks, lane // blocks
+    plane_at = jnp.where(plane_at > planes, -1000, plane_at) + first
+    low_at = jnp.where(plane_at < first + planes, plane_at, -1000)
+    high_at = jnp.where(plane_at > first, plane_at - 1, -1000)
+    base = (block_at * slots - HALF) * tilt
+    for at in range(chunk):
+        slot = step * chunk + at
+        for image in range(count):
+            span = slice(image * peers, (image + 1) * peers)
             for tile in range(GRID // LANES):
                 part = wide_ref[tile, pl.ds(image * slots + slot, peers, stride=stride), :]
                 rows_ref[at, span, tile * LANES : (tile + 1) * LANES] = part.astype(bf16)
-                for chan in range(CHANS):
-                    at_rows = slice(chan * images + image * peers, chan * images + (image + 1) * peers)
-                    lanes = slice(tile * LANES, (tile + 1) * LANES)
-                    sums[chan] = sums[chan] + part * slice_ref[slot, at_rows, lanes].astype(f32)
+        numerator = base + slot * tilt
+        plane, depth = jnp.right_shift(numerator, 7) + HALF, jnp.bitwise_and(numerator, HALF - 1)
+        mixing = jnp.where(plane == low_at, HALF - depth, jnp.where(plane == high_at, depth, 0))
+        mixing = (mixing.astype(f32) * (1.0 / HALF)).astype(bf16)
         for chan in range(CHANS):
-            sums_ref[chan, span, :] = sums[chan]
+            span = slice(chan * GRID, (chan + 1) * GRID)
+            right = jnp.concatenate([table_ref[slot, :, span], upper_ref[slot, :, span]], axis=0)
+            part = dot(mixing, right).astype(bf16).astype(f32)
+            part = interpolate(part, weight, TILE - 1).astype(bf16)
+            out_ref[at, chan * images : (chan + 1) * images, :] = part
+    gram_sums(chunk, images, out_ref, rows_ref, sums_ref)
 
     @pl.when(step == pl.num_programs(0) - 1)
     def _():
-        lane = iota((images, LANES), 1)
-        total = gram_ref[...]
-        for chan in range(CHANS):
-            value = jnp.sum(sums_ref[chan], axis=1, keepdims=True)
-            total = jnp.where(lane == PROJECT_AT + chan, value, total)
+        row, lane = iota((images, LANES), 0), iota((images, LANES), 1)
+        total = own_products(images, sums_ref)
+        for image in range(count):
+            mine = (lane == NOISE_AT) & (row == image * peers + place_ref[1])
+            total = jnp.where(mine, noise_ref[image], total)
         total_ref[...] = total
+
+
+def gram_sums(chunk, images, out_ref, rows_ref, sums_ref):
+    for group in range(images // 16):
+        start = group * 16
+        slots = []
+        for at in range(chunk):
+            rows = [out_ref[at, chan * images + start : chan * images + start + 16, :] for chan in range(CHANS)]
+            rows.append(rows_ref[at, start : start + 16, :])
+            slots.append(jnp.concatenate(rows, axis=0))
+        block = jnp.concatenate(slots, axis=1)
+        product = lax.dot_general(block, block, (((1,), (1,)), ((), ())), preferred_element_type=f32)
+        sums_ref[group] = sums_ref[group] + product
+
+
+def own_products(images, sums_ref):
+    parts = []
+    for group in range(images // 16):
+        row, lane = iota((16, LANES), 0), iota((16, LANES), 1)
+        total = jnp.zeros((16, LANES), f32)
+        for n, (k, l) in enumerate(PAIRS):
+            block = sums_ref[group, k * 16 : (k + 1) * 16, :]
+            value = jnp.sum(jnp.where(lane == row + l * 16, block, 0.0), axis=1, keepdims=True)
+            total = jnp.where(lane == n, value, total)
+        parts.append(total)
+    return jnp.concatenate(parts, axis=0)
 
 
 def solve_rows(table, noise):
@@ -386,8 +391,7 @@
                 factor[row][col] = total * inverse[col]
     forward = []
     for row in range(COMPS):
-        at = PROJECT_AT + row + 1
-        total = (table[at : at + 1, :] - gram(row + 1, 0)) / count
+        total = (gram(row + 1, CHANS) - gram(row + 1, 0)) / count
         for col in range(row):
             total = total - factor[row][col] * forward[col]
         forward.append(total * inverse[row])
@@ -401,7 +405,7 @@
 
 
 def back_kernel(
-    sizes, place_ref, part_ref, other_ref, every_ref,
+    sizes, place_ref, part_ref, other_ref, column_ref,
     slice_ref, rows_ref, slice_extra_ref, rows_extra_ref, _,
     out_ref, latent_ref, reached_ref, reached_sem, stack_ref, row_ref, power_ref, tilt_ref, col_ref, free_ref, spill_ref, order_ref,
     depth_ref, share_at_ref, share_ref, combine_ref,
@@ -413,8 +417,9 @@
     @pl.when(step == 0)
     def _():
         table = jnp.transpose(part_ref[...] + other_ref[...])
-        tilt, frac, noise = parameter_rows(every_ref, images)
-        latent = solve_rows(table, noise)
+        values = jnp.transpose(column_ref[...])
+        tilt, frac = values[0:1, :], values[1:2, :]
+        latent = solve_rows(table, table[NOISE_AT : NOISE_AT + 1, :])
         free_ref[...] = columns(latent)
         count = latent_ref.shape[0]
         for image in range(count):
@@ -565,21 +570,29 @@
     count = images.shape[0]
     total = peers * count
     width = CHANS * GRID
-    chunk = max(1, 256 // total)
+    chunk = max(1, 1024 // total)
     steps = slots // chunk
-    pack_rows = count * slots + 2 * count
-    upper_rows = -(-blocks // 16) * 16
+    pack_rows = count * slots + 2 * count + PARAMETERS
     place = jnp.stack([me * planes, me]).astype(i32)
 
-    mine = jnp.concatenate([tilt.astype(f32), frac.astype(f32), noise_var])
-    mine = jnp.broadcast_to(jnp.pad(mine, (0, LANES - 3 * count)), (peers, 8, LANES))
-    every = lax.all_to_all(mine, "slab", split_axis=0, concat_axis=0, tiled=True)
+    packed = pl.pallas_call(
+        functools.partial(pack_kernel, (planes, slots, peers, count)),
+        out_shape=jax.ShapeDtypeStruct((peers, pack_rows, GRID), bf16),
+        in_specs=[smem(), smem(), smem(), whole((count * GRID, GRID))],
+        out_specs=whole((peers, pack_rows, GRID)),
+        scratch_shapes=[pltpu.VMEM((count * GRID, GRID), bf16)],
+        grid=(1,),
+        compiler_params=params(56),
+        name="pack",
+    )(tilt, shift, frac, images.reshape(count * GRID, GRID))
+    got = lax.all_to_all(packed, "slab", split_axis=0, concat_axis=0, tiled=True)
 
     wide = 2 * WINDOW
     top = planes - 1
-    near, far = pl.pallas_call(
+    edge_rows = (wide, wide, MIDDLE)
+    near, far, middle = pl.pallas_call(
         functools.partial(edges_kernel, planes),
-        out_shape=[jax.ShapeDtypeStruct((CHANS, wide, GRID), bf16)] * 2,
+        out_shape=[jax.ShapeDtypeStruct((CHANS, rows, GRID), bf16) for rows in edge_rows],
         grid=(1,),
         in_specs=[
             smem(),
@@ -588,111 +601,88 @@
             pl.BlockSpec((GRID, GRID), lambda n: (top, 0)),
             pl.BlockSpec((COMPS, GRID, GRID), lambda n: (0, top, 0)),
         ],
-        out_specs=[whole((CHANS, wide, GRID))] * 2,
+        out_specs=[whole((CHANS, rows, GRID)) for rows in edge_rows],
         compiler_params=params(56),
-        cost_estimate=pl.CostEstimate(flops=0, bytes_accessed=6 * CHANS * wide * GRID, transcendentals=0),
         name="edges",
     )(place, mean_volume, components, mean_volume, components)
+    half = peers // 2
+    pairs = [(n, n + 1 if n % 2 else n - 1) for n in range(1, peers - 1) if n not in (half - 1, half)]
+    middle = lax.ppermute(middle, "slab", [(half - 1, half), (half, half - 1)])
     near = lax.ppermute(near, "slab", [(n, n ^ 1) for n in range(peers)])
-    far = lax.ppermute(far, "slab", [(n, n + 1 if n % 2 else n - 1) for n in range(1, peers - 1)])
-
-    packed = pl.pallas_call(
-        functools.partial(pack_kernel, (planes, slots, peers, count)),
-        out_shape=jax.ShapeDtypeStruct((peers, pack_rows, GRID), bf16),
-        in_specs=[smem(), smem(), whole((count * GRID, GRID))],
-        out_specs=whole((peers, pack_rows, GRID)),
-        scratch_shapes=[pltpu.VMEM((count * GRID, GRID), bf16)],
-        grid=(1,),
-        compiler_params=params(56),
-        cost_estimate=pl.CostEstimate(
-            flops=0, bytes_accessed=2 * (count * GRID + peers * pack_rows) * GRID, transcendentals=0
-        ),
-        name="pack",
-    )(tilt, shift, images.reshape(count * GRID, GRID))
-    packed = pl.pallas_call(
-        after_kernel,
-        out_shape=pltpu.HBM(packed.shape, bf16),
-        in_specs=[hbm()] + [pl.BlockSpec(memory_space=pltpu.VMEM)] * 3,
-        out_specs=hbm(),
-        input_output_aliases={0: 0},
-        compiler_params=params(4),
-        name="after",
-    )(in_hbm(packed), *(pltpu.with_memory_space_constraint(value, pltpu.VMEM) for value in (every, near, far)))
-    got = lax.all_to_all(packed, "slab", split_axis=0, concat_axis=0, tiled=True)
+    far = lax.ppermute(far, "slab", pairs)
 
     pair = 2 if blocks % 16 else 1
     tables = planes // pair
-    table_rows = -(-(planes + 1) * blocks // 16) * 16
-    slices, slices_extra, gram, blank = pl.pallas_call(
-        functools.partial(extract_kernel, (planes, slots, blocks, chunk, total, pair)),
+    table, blank = pl.pallas_call(
+        functools.partial(table_kernel, (planes, slots, blocks, pair)),
         out_shape=[
-            pltpu.HBM((slots, CHANS * total, GRID), bf16),
-            jax.ShapeDtypeStruct((2 * total, width), bf16),
-            jax.ShapeDtypeStruct((total, LANES), f32),
+            pltpu.HBM((slots, planes * blocks, width), bf16),
             jax.ShapeDtypeStruct((COMPS, planes * GRID, GRID), bf16),
         ],
-        grid=(tables + steps,),
-        in_specs=[
-            smem(),
-            whole((peers, 8, LANES)),
+        grid=(tables,),
+        in_specs=[smem(), anywhere(), anywhere()],
+        out_specs=[
+            pl.BlockSpec((slots, pair * blocks, width), lambda n: (0, n, 0)),
             anywhere(),
-            anywhere(),
-            hbm(),
-            hbm(),
-        ],
-        out_specs=[
-            pl.BlockSpec((chunk, CHANS * total, GRID), lambda n: (jnp.maximum(n - tables, 0), 0, 0)),
-            whole((2 * total, width)),
-            whole((total, LANES)),
-            anywhere(),
         ],
         scratch_shapes=[
-            pltpu.VMEM((CHANS, wide, GRID), bf16),
-            pltpu.VMEM((CHANS, wide, GRID), bf16),
-            pltpu.SemaphoreType.DMA((2,)),
-            pltpu.VMEM((COMPS, GRID, GRID), bf16),
-            pltpu.SemaphoreType.DMA((planes,)),
             pltpu.VMEM((planes * GRID, GRID), bf16),
             pltpu.VMEM((COMPS, planes * GRID, GRID), bf16),
             pltpu.SemaphoreType.DMA((tables,)),
             pltpu.SemaphoreType.DMA((tables,)),
-            pltpu.VMEM((slots, table_rows, width), bf16),
             pltpu.VMEM((GRID, GRID), bf16),
-            pltpu.VMEM((len(PAIRS), total, LANES), f32),
-            pltpu.VMEM((total, LANES), f32),
-        ],
-        compiler_params=params(44),
-        name="extract",
-    )(place, every, mean_volume, components, in_hbm(near), in_hbm(far))
-
-    rows, rows_extra, partial = pl.pallas_call(
-        functools.partial(project_kernel, (slots, chunk, total, peers, count)),
+            pltpu.VMEM((COMPS, 16, GRID), bf16),
+            pltpu.SemaphoreType.DMA((planes, (GRID - wide) // 16)),
+        ],
+        compiler_params=params(30),
+        name="table",
+    )(place, mean_volume, components)
+
+    slices, rows, slices_extra, rows_extra, partial, columns_all = pl.pallas_call(
+        functools.partial(extract_kernel, (planes, slots, blocks, chunk, total, peers)),
         out_shape=[
+            jax.ShapeDtypeStruct((slots, CHANS * total, GRID), bf16),
             jax.ShapeDtypeStruct((slots, total, GRID), bf16),
+            jax.ShapeDtypeStruct((2 * total, width), bf16),
             jax.ShapeDtypeStruct((2 * total, GRID), bf16),
             jax.ShapeDtypeStruct((total, LANES), f32),
+            jax.ShapeDtypeStruct((total, LANES), f32),
         ],
         grid=(steps,),
-        in_specs=[
-            whole((peers * pack_rows, GRID)),
-            pl.BlockSpec(memory_space=pltpu.VMEM),
-            whole((total, LANES)),
-        ],
+        in_specs=[smem(), smem()] + [hbm()] * 7,
         out_specs=[
+            pl.BlockSpec((chunk, CHANS * total, GRID), lambda n: (n, 0, 0)),
             pl.BlockSpec((chunk, total, GRID), lambda n: (n, 0, 0)),
+            whole((2 * total, width)),
             whole((2 * total, GRID)),
             whole((total, LANES)),
+            whole((total, LANES)),
         ],
         scratch_shapes=[
+            pltpu.VMEM((peers * pack_rows, GRID), bf16),
+            pltpu.VMEM((CHANS, wide, GRID), bf16),
+            pltpu.VMEM((CHANS, wide, GRID), bf16),
+            pltpu.VMEM((CHANS, MIDDLE, GRID), bf16),
+            pltpu.VMEM((CHANS, GRID, GRID), bf16),
+            pltpu.VMEM((slots, planes * blocks, width), bf16),
+            pltpu.SemaphoreType.DMA((6,)),
+            pltpu.SemaphoreType.DMA((steps,)),
             pltpu.VMEM((GRID // LANES, peers * pack_rows, LANES), f32),
-            pltpu.VMEM((CHANS, total, LANES), f32),
-        ],
-        compiler_params=params(24),
-        name="project",
+            pltpu.VMEM((slots, -(-blocks // 16) * 16, width), bf16),
+            pltpu.VMEM((total // 16, LANES, LANES), f32),
+        ],
+        compiler_params=params(40),
+        name="extract",
     )(
-        got.reshape(peers * pack_rows, GRID),
-        pltpu.with_memory_space_constraint(slices, pltpu.VMEM),
-        gram,
+        place,
+        noise_var,
+        in_hbm(got.reshape(peers * pack_rows, GRID)),
+        in_hbm(near),
+        in_hbm(far),
+        in_hbm(middle),
+        in_hbm(mean_volume),
+        in_hbm(components),
+        in_hbm(table),
     )
 
     step = 1
@@ -714,7 +704,7 @@
             smem(),
             whole((total, LANES)),
             whole((total, LANES)),
-            whole((peers, 8, LANES)),
+            whole((total, LANES)),
             pl.BlockSpec(memory_space=pltpu.VMEM),
             pl.BlockSpec((chunk, total, GRID), lambda n: (jnp.minimum(n, last), 0, 0)),
             whole((2 * total, width)),
@@ -744,7 +734,7 @@
         input_output_aliases={8: 0},
         compiler_params=params(29),
         name="back",
-    )(place, *halves, every, pltpu.with_memory_space_constraint(slices, pltpu.VMEM), rows, slices_extra, rows_extra, blank)
+    )(place, *halves, columns_all, pltpu.with_memory_space_constraint(slices, pltpu.VMEM), rows, slices_extra, rows_extra, blank)
     return new_components, latents
 
 

time: 90.9 us -> 82 us (0.902)
  starting transfers between devices: 26 us -> 21 us
  Pallas kernels: 46.7 us -> 44.2 us
  waiting for transfers between devices: 10.7 us -> 9.51 us
    pallas_call x1, Pallas kernels: 24.3 us -> 14.1 us  [local(): pl.pallas_call(functools.partial(extract_kernel, (planes, slots, blocks,...]
    pallas_call x2 -> x1, Pallas kernels: 2.16 us -> 12.3 us  [local(): pl.pallas_call(functools.partial(table_kernel, (planes, slots, blocks, pa...]
    all_to_all x1 -> x0, starting transfers between devices: 8.63 us -> none  [local(): lax.all_to_all(mine, 'slab', split_axis=0, concat_axis=0, tiled=True)]
    all_to_all x1 -> x0, waiting for transfers between devices: 4.03 us -> none  [local(): lax.all_to_all(mine, 'slab', split_axis=0, concat_axis=0, tiled=True)]
    ppermute x4, starting transfers between devices: 8.53 us -> 11.9 us  [local(): lax.ppermute(partial, 'slab', [(n, n ^ step) for n in range(peers)])]
    all_to_all x1, waiting for transfers between devices: 0.01 us -> 2.97 us  [local(): lax.all_to_all(packed, 'slab', split_axis=0, concat_axis=0, tiled=True)]
    pallas_call x1, Pallas kernels: 14.7 us -> 12.2 us  [local(): pl.pallas_call(functools.partial(back_kernel, (planes, slots, blocks, chu...]
    unnamed x22 -> x16, local copies, waits for them, and re-layouts: 5 us -> 5.64 us
  transfers between devices with their start and end apart: 8 -> 8, of which waited for: 5 -> 5; matrix products, arithmetic and copies ran while one was open for 1% -> 1% of each run, Pallas kernels for 30% -> 18%
where the time goes in v4:
time: 82 us; the launch traced here: 81.8 us
  Pallas kernels  44.2 us (54%)
  starting transfers between devices  21 us (26%)
  waiting for transfers between devices  9.51 us (12%)
  local copies, waits for them, and re-layouts  5.64 us (7%)
    pallas_call x1, Pallas kernels, local(): pl.pallas_call(functools.partial(extract_kernel, (planes, slots, blocks,...  14.1 us
    pallas_call x1, Pallas kernels, local(): pl.pallas_call(functools.partial(table_kernel, (planes, slots, blocks, pa...  12.3 us
    pallas_call x1, Pallas kernels, local(): pl.pallas_call(functools.partial(back_kernel, (planes, slots, blocks, chu...  12.2 us
    ppermute x4, starting transfers between devices, local(): lax.ppermute(partial, 'slab', [(n, n ^ step) for n in range(peers)])  11.9 us
    all_to_all x1, starting transfers between devices, local(): lax.all_to_all(packed, 'slab', split_axis=0, concat_axis=0, tiled=True)  7.38 us
    ppermute x4, waiting for transfers between devices, local(): lax.ppermute(partial, 'slab', [(n, n ^ step) for n in range(peers)])  6.54 us
    unnamed x16, local copies, waits for them, and re-layouts  5.64 us
    all_to_all x1, waiting for transfers between devices, local(): lax.all_to_all(packed, 'slab', split_axis=0, concat_axis=0, tiled=True)  2.97 us
  transfers between devices with their start and end apart: 8, of which 5 were waited for; matrix products, arithmetic and copies ran while one was open for 1% of the time, Pallas kernels for 18%

profile of v4, /device:TPU:0, one launch (start us, length us, event | category | flops | bytes accessed | tf_op | source)
XLA Modules:
  0.0 81.8 jit_solution(13058847235268171889)
XLA Ops:
  0.6 2.8 %pack.1 = bf16[16,144,256]{2,1,0:T(8,128)(2,1)} custom-call(s32[4]{0:T(128)} %tilt_ref.1, s32[4]{0:T(128)} %shift_ref.1, s32[4]{0:T(128)} %frac_ref.1, bf16[1024,256]{1,0:T(8,128)(2,1)} %bitcast.5), custom_call_target="tpu_custom_call" | custom-call | tf_op jit(solution)/shard_map/pack/pallas_call | solution.py:578
  3.5 7.4 %all-to-all-start = ((bf16[16,144,256]{2,1,0:T(8,128)(2,1)}), bf16[16,144,256]{2,1,0:T(8,128)(2,1)S(1)}, u32[]{:S(2)}, u32[]{:S(2)}) async-start(bf16[16,144,256]{2,1,0:T(8,128)(2,1)} %pack.1), calls=%async_computation | async-start | bytes 2359296 | tf_op jit(solution)/shard_map/all_to_all | solution.py:588
  10.9 0.7 pad_add_fusion.place_ref
  11.5 0.0 copy-start.1
  11.5 0.0 copy-start.2
  11.5 2.8 %edges.1 = (bf16[7,160,256]{2,1,0:T(8,128)(2,1)}, bf16[7,160,256]{2,1,0:T(8,128)(2,1)}, bf16[7,32,256]{2,1,0:T(8,128)(2,1)}) custom-call(s32[2]{0:T(128)} %pad_add_fusion.place_ref, bf16[4096,256]{1,0:T(8,128)(2,1)} %mean_hbm.3, bf16[6,4096,256]{2,1,0:T(8,128)(2,1)} %comp_hbm.3, bf16[4096,256]{1,0:T(8,128)(2,1)} %mean_hbm.3, bf16[6,4096,256]{2,1,0:T(8,128)(2,1)} %comp_hbm.3), custom_call_target="tpu_custom_call" | custom-call | tf_op jit(solution)/shard_map/edges/pallas_call | solution.py:593
  14.3 0.0 copy-start.3
  14.3 0.4 collective-permute-start
  14.7 0.7 collective-permute-start.1
  15.4 0.7 collective-permute-start.2
  16.1 0.0 copy-done.1
  16.1 0.0 copy-done.2
  16.1 0.0 copy-start
  16.1 4.6 %copy-done = bf16[6,4096,256]{2,1,0:T(8,128)(2,1)S(1)} copy-done((bf16[6,4096,256]{2,1,0:T(8,128)(2,1)S(1)}, bf16[6,4096,256]{2,1,0:T(8,128)(2,1)}, u32[]{:S(2)}) %copy-start) | copy-done | bytes 12582936
  20.7 12.3 %table.1 = (bf16[32,128,1792]{2,1,0:T(8,128)(2,1)}, bf16[6,4096,256]{2,1,0:T(8,128)(2,1)}) custom-call(s32[2]{0:T(128)S(1)} %copy-done.2, bf16[4096,256]{1,0:T(8,128)(2,1)S(1)} %copy-done.1, bf16[6,4096,256]{2,1,0:T(8,128)(2,1)S(1)} %copy-done), custom_call_target="tpu_custom_call" | custom-call | tf_op jit(solution)/shard_map/table/pallas_call | solution.py:616
  33.0 0.0 collective-permute-done.2.middle_hbm
  33.0 0.0 copy-start.7
  33.0 0.0 collective-permute-done.near_hbm
  33.0 0.0 copy-start.5
  33.0 0.0 collective-permute-done.1.far_hbm
  33.0 0.0 copy-start.6
  33.0 3.0 %all-to-all-done = bf16[16,144,256]{2,1,0:T(8,128)(2,1)S(1)} async-done(((bf16[16,144,256]{2,1,0:T(8,128)(2,1)}), bf16[16,144,256]{2,1,0:T(8,128)(2,1)S(1)}, u32[]{:S(2)}, u32[]{:S(2)}) %all-to-all-start) | async-done | bytes 1179680 | tf_op jit(solution)/shard_map/all_to_all | solution.py:588
  36.0 0.0 copy-start.4
  36.0 0.0 copy-done.7
  36.0 0.0 copy-done.5
  36.0 0.0 copy-done.6
  36.0 1.0 %copy-done.4 = bf16[16,144,256]{2,1,0:T(8,128)(2,1)} copy-done((bf16[16,144,256]{2,1,0:T(8,128)(2,1)}, bf16[16,144,256]{2,1,0:T(8,128)(2,1)S(1)}, u32[]{:S(2)}) %copy-start.4) | copy-done | bytes 1179672
  37.0 0.0 copy-done.3
  37.0 14.1 %extract.1 = (bf16[32,448,256]{2,1,0:T(8,128)(2,1)S(1)}, bf16[32,64,256]{2,1,0:T(8,128)(2,1)S(1)}, bf16[128,1792]{1,0:T(8,128)(2,1)S(1)}, bf16[128,256]{1,0:T(8,...) custom-call(s32[2]{0:T(128)S(1)} %copy-done.2, f32[4]{0:T(128)S(1)} %copy-done.3, bf16[2304,256]{1,0:T(8,128)(2,1)} %bitcast.4, ...), custom_call_target="tpu_custom_call" | custom-call | tf_op jit(solution)/shard_map/extract/pallas_call | solution.py:641
  51.1 3.3 %collective-permute-start.3 = (f32[64,128]{1,0:T(8,128)S(1)}, f32[64,128]{1,0:T(8,128)S(1)}, u32[]{:S(2)}, u32[]{:S(2)}) collective-permute-start(f32[64,128]{1,0:T(8,128)S(1)} %get-tuple-element.17), channel_id=1, source_target_pairs={{0,1},{1,0},{2,3},{3,2},{4,5},{5,4},{6,7},{7,6},{8,9},{9,8},{10,11... | collective-permute-start | bytes 98312 | tf_op jit(solution)/shard_map/ppermute | solution.py:690
  54.4 0.9 %collective-permute-done.3 = f32[64,128]{1,0:T(8,128)S(1)} collective-permute-done((f32[64,128]{1,0:T(8,128)S(1)}, f32[64,128]{1,0:T(8,128)S(1)}, u32[]{:S(2)}, u32[]{:S(2)}) %collective-permute-start.3) | collective-permute-done | bytes 32800 | tf_op jit(solution)/shard_map/ppermute | solution.py:690
  55.3 2.6 %collective-permute-start.4 = (f32[64,128]{1,0:T(8,128)S(1)}, f32[64,128]{1,0:T(8,128)S(1)}, u32[]{:S(2)}, u32[]{:S(2)}) collective-permute-start(f32[64,128]{1,0:T(8,128)S(1)} %add.9), channel_id=1, source_target_pairs={{0,2},{1,3},{2,0},{3,1},{4,6},{5,7},{6,4},{7,5},{8,10},{9,11},{10,... | collective-permute-start | bytes 98312 | tf_op jit(solution)/shard_map/ppermute | solution.py:690
  57.9 1.9 %collective-permute-done.4 = f32[64,128]{1,0:T(8,128)S(1)} collective-permute-done((f32[64,128]{1,0:T(8,128)S(1)}, f32[64,128]{1,0:T(8,128)S(1)}, u32[]{:S(2)}, u32[]{:S(2)}) %collective-permute-start.4) | collective-permute-done | bytes 32800 | tf_op jit(solution)/shard_map/ppermute | solution.py:690
  59.8 3.1 %collective-permute-start.5 = (f32[64,128]{1,0:T(8,128)S(1)}, f32[64,128]{1,0:T(8,128)S(1)}, u32[]{:S(2)}, u32[]{:S(2)}) collective-permute-start(f32[64,128]{1,0:T(8,128)S(1)} %add.10), channel_id=1, source_target_pairs={{0,4},{1,5},{2,6},{3,7},{4,0},{5,1},{6,2},{7,3},{8,12},{9,13},{10,... | collective-permute-start | bytes 98312 | tf_op jit(solution)/shard_map/ppermute | solution.py:690
  62.8 1.9 %collective-permute-done.5 = f32[64,128]{1,0:T(8,128)S(1)} collective-permute-done((f32[64,128]{1,0:T(8,128)S(1)}, f32[64,128]{1,0:T(8,128)S(1)}, u32[]{:S(2)}, u32[]{:S(2)}) %collective-permute-start.5) | collective-permute-done | bytes 32800 | tf_op jit(solution)/shard_map/ppermute | solution.py:690
  64.7 2.9 %collective-permute-start.6 = (f32[64,128]{1,0:T(8,128)S(1)}, f32[64,128]{1,0:T(8,128)S(1)}, u32[]{:S(2)}, u32[]{:S(2)}) collective-permute-start(f32[64,128]{1,0:T(8,128)S(1)} %add.11.part_ref), channel_id=1, source_target_pairs={{0,8},{1,9},{2,10},{3,11},{4,12},{5,13},{6,14},{7,15},{8,0},{9,1},... | collective-permute-start | bytes 98312 | tf_op jit(solution)/shard_map/ppermute | solution.py:692
  67.6 1.9 %collective-permute-done.6.other_ref = f32[64,128]{1,0:T(8,128)S(1)} collective-permute-done((f32[64,128]{1,0:T(8,128)S(1)}, f32[64,128]{1,0:T(8,128)S(1)}, u32[]{:S(2)}, u32[]{:S(2)}) %collective-permute-start.6) | collective-permute-done | bytes 32800 | tf_op jit(solution)/shard_map/ppermute | solution.py:692
  69.5 12.2 %back.1 = (bf16[6,4096,256]{2,1,0:T(8,128)(2,1)}, f32[4,6]{1,0:T(4,128)}) custom-call(s32[2]{0:T(128)S(1)} %copy-done.2, f32[64,128]{1,0:T(8,128)S(1)} %add.11.part_ref, f32[64,128]{1,0:T(8,128)S(1)} %collective-permute-done.6.other_ref, f32[64,128]{1,0:T(8,128)S(1)} %get-tuple-element.18.column_ref, ...), custom_call_target="tpu_custom_call", output_to_operand_aliasing={{0}: (8, {})} | custom-call | tf_op jit(solution)/shard_map/back/pallas_call | solution.py:696
  (3 shorter events, 0.0 us)
Async XLA Ops:
  3.5 32.5 %all-to-all-start = ((bf16[16,144,256]{2,1,0:T(8,128)(2,1)}), bf16[16,144,256]{2,1,0:T(8,128)(2,1)S(1)}, u32[]{:S(2)}, u32[]{:S(2)}) async-start(bf16[16,144,256]{2,1,0:T(8,128)(2,1)} %pack.1), calls=%async_computation | async-start | bytes 2359296 | tf_op jit(solution)/shard_map/all_to_all | solution.py:588
  11.5 4.6 %copy-start.1 = (bf16[4096,256]{1,0:T(8,128)(2,1)S(1)}, bf16[4096,256]{1,0:T(8,128)(2,1)}, u32[]{:S(2)}) copy-start(bf16[4096,256]{1,0:T(8,128)(2,1)} %mean_hbm.3) | copy-start | bytes 6291460
  11.5 4.6 %copy-start.2 = (s32[2]{0:T(128)S(1)}, s32[2]{0:T(128)}, u32[]{:S(2)}) copy-start(s32[2]{0:T(128)} %pad_add_fusion.place_ref) | copy-start | bytes 28
  14.3 22.7 %copy-start.3 = (f32[4]{0:T(128)S(1)}, f32[4]{0:T(128)}, u32[]{:S(2)}) copy-start(f32[4]{0:T(128)} %noise_ref.1) | copy-start | bytes 52
  14.3 18.7 %collective-permute-start = (bf16[7,160,256]{2,1,0:T(8,128)(2,1)}, bf16[7,160,256]{2,1,0:T(8,128)(2,1)S(1)}, u32[]{:S(2)}, u32[]{:S(2)}) collective-permute-start(bf16[7,160,256]{2,1,0:T(8,128)(2,1)} %get-tuple-element.13), channel_id=1, source_target_pairs={{0,1},{1,0},{2,3},{3,2},{4,5},{5,4},{6,7},{7,6},{8,9},{9,8},{10,11... | collective-permute-start | bytes 1720328 | tf_op jit(solution)/shard_map/ppermute | solution.py:611
  14.7 18.3 %collective-permute-start.1 = (bf16[7,160,256]{2,1,0:T(8,128)(2,1)}, bf16[7,160,256]{2,1,0:T(8,128)(2,1)S(1)}, u32[]{:S(2)}, u32[]{:S(2)}) collective-permute-start(bf16[7,160,256]{2,1,0:T(8,128)(2,1)} %get-tuple-element.14), channel_id=1, source_target_pairs={{1,2},{2,1},{3,4},{4,3},{5,6},{6,5},{9,10},{10,9},{11,12},{12,11},... | collective-permute-start | bytes 1720328 | tf_op jit(solution)/shard_map/ppermute | solution.py:612
  15.4 17.5 %collective-permute-start.2 = (bf16[7,32,256]{2,1,0:T(8,128)(2,1)}, bf16[7,32,256]{2,1,0:T(8,128)(2,1)S(1)}, u32[]{:S(2)}, u32[]{:S(2)}) collective-permute-start(bf16[7,32,256]{2,1,0:T(8,128)(2,1)} %get-tuple-element.15), channel_id=1, source_target_pairs={{7,8},{8,7},{23,24},{24,23}} | collective-permute-start | bytes 344072 | tf_op jit(solution)/shard_map/ppermute | solution.py:610
  16.1 4.6 %copy-start = (bf16[6,4096,256]{2,1,0:T(8,128)(2,1)S(1)}, bf16[6,4096,256]{2,1,0:T(8,128)(2,1)}, u32[]{:S(2)}) copy-start(bf16[6,4096,256]{2,1,0:T(8,128)(2,1)} %comp_hbm.3) | copy-start | bytes 37748740
  33.0 3.0 %copy-start.7 = (bf16[7,32,256]{2,1,0:T(8,128)(2,1)}, bf16[7,32,256]{2,1,0:T(8,128)(2,1)S(1)}, u32[]{:S(2)}) copy-start(bf16[7,32,256]{2,1,0:T(8,128)(2,1)S(1)} %collective-permute-done.2.middle_hbm) | copy-start | bytes 344068
  33.0 3.0 %copy-start.5 = (bf16[7,160,256]{2,1,0:T(8,128)(2,1)}, bf16[7,160,256]{2,1,0:T(8,128)(2,1)S(1)}, u32[]{:S(2)}) copy-start(bf16[7,160,256]{2,1,0:T(8,128)(2,1)S(1)} %collective-permute-done.near_hbm) | copy-start | bytes 1720324
  33.0 3.0 %copy-start.6 = (bf16[7,160,256]{2,1,0:T(8,128)(2,1)}, bf16[7,160,256]{2,1,0:T(8,128)(2,1)S(1)}, u32[]{:S(2)}) copy-start(bf16[7,160,256]{2,1,0:T(8,128)(2,1)S(1)} %collective-permute-done.1.far_hbm) | copy-start | bytes 1720324
  36.0 1.1 %copy-start.4 = (bf16[16,144,256]{2,1,0:T(8,128)(2,1)}, bf16[16,144,256]{2,1,0:T(8,128)(2,1)S(1)}, u32[]{:S(2)}) copy-start(bf16[16,144,256]{2,1,0:T(8,128)(2,1)S(1)} %all-to-all-done) | copy-start | bytes 3538948
  51.1 4.2 %collective-permute-start.3 = (f32[64,128]{1,0:T(8,128)S(1)}, f32[64,128]{1,0:T(8,128)S(1)}, u32[]{:S(2)}, u32[]{:S(2)}) collective-permute-start(f32[64,128]{1,0:T(8,128)S(1)} %get-tuple-element.17), channel_id=1, source_target_pairs={{0,1},{1,0},{2,3},{3,2},{4,5},{5,4},{6,7},{7,6},{8,9},{9,8},{10,11... | collective-permute-start | bytes 98312 | tf_op jit(solution)/shard_map/ppermute | solution.py:690
  55.3 4.5 %collective-permute-start.4 = (f32[64,128]{1,0:T(8,128)S(1)}, f32[64,128]{1,0:T(8,128)S(1)}, u32[]{:S(2)}, u32[]{:S(2)}) collective-permute-start(f32[64,128]{1,0:T(8,128)S(1)} %add.9), channel_id=1, source_target_pairs={{0,2},{1,3},{2,0},{3,1},{4,6},{5,7},{6,4},{7,5},{8,10},{9,11},{10,... | collective-permute-start | bytes 98312 | tf_op jit(solution)/shard_map/ppermute | solution.py:690
  59.8 5.0 %collective-permute-start.5 = (f32[64,128]{1,0:T(8,128)S(1)}, f32[64,128]{1,0:T(8,128)S(1)}, u32[]{:S(2)}, u32[]{:S(2)}) collective-permute-start(f32[64,128]{1,0:T(8,128)S(1)} %add.10), channel_id=1, source_target_pairs={{0,4},{1,5},{2,6},{3,7},{4,0},{5,1},{6,2},{7,3},{8,12},{9,13},{10,... | collective-permute-start | bytes 98312 | tf_op jit(solution)/shard_map/ppermute | solution.py:690
  64.7 4.8 %collective-permute-start.6 = (f32[64,128]{1,0:T(8,128)S(1)}, f32[64,128]{1,0:T(8,128)S(1)}, u32[]{:S(2)}, u32[]{:S(2)}) collective-permute-start(f32[64,128]{1,0:T(8,128)S(1)} %add.11.part_ref), channel_id=1, source_target_pairs={{0,8},{1,9},{2,10},{3,11},{4,12},{5,13},{6,14},{7,15},{8,0},{9,1},... | collective-permute-start | bytes 98312 | tf_op jit(solution)/shard_map/ppermute | solution.py:692

commit v5 on v4

--- a/solution.py
+++ b/solution.py
@@ -691,7 +691,7 @@
         step *= 2
     halves = partial, lax.ppermute(partial, "slab", [(n, n ^ step) for n in range(peers)])
 
-    out_planes = 2
+    out_planes = min(16, planes)
     last = steps - 1
     new_components, latents = pl.pallas_call(
         functools.partial(back_kernel, (planes, slots, blocks, chunk, total, steps, out_planes)),

time: 82 us -> 80.8 us (0.985)
  Pallas kernels: 44.2 us -> 42.8 us
    pallas_call x1, Pallas kernels: 12.2 us -> 10.8 us  [local(): pl.pallas_call(functools.partial(back_kernel, (planes, slots, blocks, chu...]
  transfers between devices with their start and end apart: 8 -> 8, of which waited for: 5 -> 5; matrix products, arithmetic and copies ran while one was open for 1% -> 1% of each run, Pallas kernels for 18% -> 19%
where the time goes in v5:
time: 80.8 us; the launch traced here: 80.5 us
  Pallas kernels  42.8 us (53%)
  starting transfers between devices  21 us (26%)
  waiting for transfers between devices  9.5 us (12%)
  local copies, waits for them, and re-layouts  5.64 us (7%)
  between operations  0.92 us (1%)
    pallas_call x1, Pallas kernels, local(): pl.pallas_call(functools.partial(extract_kernel, (planes, slots, blocks,...  14.1 us
    pallas_call x1, Pallas kernels, local(): pl.pallas_call(functools.partial(table_kernel, (planes, slots, blocks, pa...  12.3 us
    ppermute x4, starting transfers between devices, local(): lax.ppermute(partial, 'slab', [(n, n ^ step) for n in range(peers)])  11.9 us
    pallas_call x1, Pallas kernels, local(): pl.pallas_call(functools.partial(back_kernel, (planes, slots, blocks, chu...  10.8 us
    all_to_all x1, starting transfers between devices, local(): lax.all_to_all(packed, 'slab', split_axis=0, concat_axis=0, tiled=True)  7.39 us
    ppermute x4, waiting for transfers between devices, local(): lax.ppermute(partial, 'slab', [(n, n ^ step) for n in range(peers)])  6.53 us
    unnamed x16, local copies, waits for them, and re-layouts  5.64 us
    all_to_all x1, waiting for transfers between devices, local(): lax.all_to_all(packed, 'slab', split_axis=0, concat_axis=0, tiled=True)  2.96 us
  transfers between devices with their start and end apart: 8, of which 5 were waited for; matrix products, arithmetic and copies ran while one was open for 1% of the time, Pallas kernels for 19%

profile of v5, /device:TPU:0, one launch (start us, length us, event | category | flops | bytes accessed | tf_op | source)
XLA Modules:
  0.0 80.5 jit_solution(5072867190912923241)
XLA Ops:
  0.6 2.8 %pack.1 = bf16[16,144,256]{2,1,0:T(8,128)(2,1)} custom-call(s32[4]{0:T(128)} %tilt_ref.1, s32[4]{0:T(128)} %shift_ref.1, s32[4]{0:T(128)} %frac_ref.1, bf16[1024,256]{1,0:T(8,128)(2,1)} %bitcast.5), custom_call_target="tpu_custom_call" | custom-call | tf_op jit(solution)/shard_map/pack/pallas_call | solution.py:578
  3.5 7.4 %all-to-all-start = ((bf16[16,144,256]{2,1,0:T(8,128)(2,1)}), bf16[16,144,256]{2,1,0:T(8,128)(2,1)S(1)}, u32[]{:S(2)}, u32[]{:S(2)}) async-start(bf16[16,144,256]{2,1,0:T(8,128)(2,1)} %pack.1), calls=%async_computation | async-start | bytes 2359296 | tf_op jit(solution)/shard_map/all_to_all | solution.py:588
  10.9 0.7 pad_add_fusion.place_ref
  11.5 0.0 copy-start.1
  11.5 0.0 copy-start.2
  11.5 2.8 %edges.1 = (bf16[7,160,256]{2,1,0:T(8,128)(2,1)}, bf16[7,160,256]{2,1,0:T(8,128)(2,1)}, bf16[7,32,256]{2,1,0:T(8,128)(2,1)}) custom-call(s32[2]{0:T(128)} %pad_add_fusion.place_ref, bf16[4096,256]{1,0:T(8,128)(2,1)} %mean_hbm.3, bf16[6,4096,256]{2,1,0:T(8,128)(2,1)} %comp_hbm.3, bf16[4096,256]{1,0:T(8,128)(2,1)} %mean_hbm.3, bf16[6,4096,256]{2,1,0:T(8,128)(2,1)} %comp_hbm.3), custom_call_target="tpu_custom_call" | custom-call | tf_op jit(solution)/shard_map/edges/pallas_call | solution.py:593
  14.3 0.0 copy-start.3
  14.3 0.4 collective-permute-start
  14.7 0.7 collective-permute-start.1
  15.4 0.7 collective-permute-start.2
  16.1 0.0 copy-done.1
  16.1 0.0 copy-done.2
  16.1 0.0 copy-start
  16.1 4.6 %copy-done = bf16[6,4096,256]{2,1,0:T(8,128)(2,1)S(1)} copy-done((bf16[6,4096,256]{2,1,0:T(8,128)(2,1)S(1)}, bf16[6,4096,256]{2,1,0:T(8,128)(2,1)}, u32[]{:S(2)}) %copy-start) | copy-done | bytes 12582936
  20.7 12.3 %table.1 = (bf16[32,128,1792]{2,1,0:T(8,128)(2,1)}, bf16[6,4096,256]{2,1,0:T(8,128)(2,1)}) custom-call(s32[2]{0:T(128)S(1)} %copy-done.2, bf16[4096,256]{1,0:T(8,128)(2,1)S(1)} %copy-done.1, bf16[6,4096,256]{2,1,0:T(8,128)(2,1)S(1)} %copy-done), custom_call_target="tpu_custom_call" | custom-call | tf_op jit(solution)/shard_map/table/pallas_call | solution.py:616
  33.0 0.0 collective-permute-done.2.middle_hbm
  33.0 0.0 copy-start.7
  33.0 0.0 collective-permute-done.near_hbm
  33.0 0.0 copy-start.5
  33.0 0.0 collective-permute-done.1.far_hbm
  33.0 0.0 copy-start.6
  33.0 3.0 %all-to-all-done = bf16[16,144,256]{2,1,0:T(8,128)(2,1)S(1)} async-done(((bf16[16,144,256]{2,1,0:T(8,128)(2,1)}), bf16[16,144,256]{2,1,0:T(8,128)(2,1)S(1)}, u32[]{:S(2)}, u32[]{:S(2)}) %all-to-all-start) | async-done | bytes 1179680 | tf_op jit(solution)/shard_map/all_to_all | solution.py:588
  36.0 0.0 copy-start.4
  36.0 0.0 copy-done.7
  36.0 0.0 copy-done.5
  36.0 0.0 copy-done.6
  36.0 1.0 %copy-done.4 = bf16[16,144,256]{2,1,0:T(8,128)(2,1)} copy-done((bf16[16,144,256]{2,1,0:T(8,128)(2,1)}, bf16[16,144,256]{2,1,0:T(8,128)(2,1)S(1)}, u32[]{:S(2)}) %copy-start.4) | copy-done | bytes 1179672
  37.0 0.0 copy-done.3
  37.0 14.1 %extract.1 = (bf16[32,448,256]{2,1,0:T(8,128)(2,1)S(1)}, bf16[32,64,256]{2,1,0:T(8,128)(2,1)S(1)}, bf16[128,1792]{1,0:T(8,128)(2,1)S(1)}, bf16[128,256]{1,0:T(8,...) custom-call(s32[2]{0:T(128)S(1)} %copy-done.2, f32[4]{0:T(128)S(1)} %copy-done.3, bf16[2304,256]{1,0:T(8,128)(2,1)} %bitcast.4, ...), custom_call_target="tpu_custom_call" | custom-call | tf_op jit(solution)/shard_map/extract/pallas_call | solution.py:641
  51.1 3.3 %collective-permute-start.3 = (f32[64,128]{1,0:T(8,128)S(1)}, f32[64,128]{1,0:T(8,128)S(1)}, u32[]{:S(2)}, u32[]{:S(2)}) collective-permute-start(f32[64,128]{1,0:T(8,128)S(1)} %get-tuple-element.17), channel_id=1, source_target_pairs={{0,1},{1,0},{2,3},{3,2},{4,5},{5,4},{6,7},{7,6},{8,9},{9,8},{10,11... | collective-permute-start | bytes 98312 | tf_op jit(solution)/shard_map/ppermute | solution.py:690
  54.4 0.9 %collective-permute-done.3 = f32[64,128]{1,0:T(8,128)S(1)} collective-permute-done((f32[64,128]{1,0:T(8,128)S(1)}, f32[64,128]{1,0:T(8,128)S(1)}, u32[]{:S(2)}, u32[]{:S(2)}) %collective-permute-start.3) | collective-permute-done | bytes 32800 | tf_op jit(solution)/shard_map/ppermute | solution.py:690
  55.3 2.6 %collective-permute-start.4 = (f32[64,128]{1,0:T(8,128)S(1)}, f32[64,128]{1,0:T(8,128)S(1)}, u32[]{:S(2)}, u32[]{:S(2)}) collective-permute-start(f32[64,128]{1,0:T(8,128)S(1)} %add.9), channel_id=1, source_target_pairs={{0,2},{1,3},{2,0},{3,1},{4,6},{5,7},{6,4},{7,5},{8,10},{9,11},{10,... | collective-permute-start | bytes 98312 | tf_op jit(solution)/shard_map/ppermute | solution.py:690
  57.9 1.9 %collective-permute-done.4 = f32[64,128]{1,0:T(8,128)S(1)} collective-permute-done((f32[64,128]{1,0:T(8,128)S(1)}, f32[64,128]{1,0:T(8,128)S(1)}, u32[]{:S(2)}, u32[]{:S(2)}) %collective-permute-start.4) | collective-permute-done | bytes 32800 | tf_op jit(solution)/shard_map/ppermute | solution.py:690
  59.8 3.0 %collective-permute-start.5 = (f32[64,128]{1,0:T(8,128)S(1)}, f32[64,128]{1,0:T(8,128)S(1)}, u32[]{:S(2)}, u32[]{:S(2)}) collective-permute-start(f32[64,128]{1,0:T(8,128)S(1)} %add.10), channel_id=1, source_target_pairs={{0,4},{1,5},{2,6},{3,7},{4,0},{5,1},{6,2},{7,3},{8,12},{9,13},{10,... | collective-permute-start | bytes 98312 | tf_op jit(solution)/shard_map/ppermute | solution.py:690
  62.8 1.9 %collective-permute-done.5 = f32[64,128]{1,0:T(8,128)S(1)} collective-permute-done((f32[64,128]{1,0:T(8,128)S(1)}, f32[64,128]{1,0:T(8,128)S(1)}, u32[]{:S(2)}, u32[]{:S(2)}) %collective-permute-start.5) | collective-permute-done | bytes 32800 | tf_op jit(solution)/shard_map/ppermute | solution.py:690
  64.7 2.9 %collective-permute-start.6 = (f32[64,128]{1,0:T(8,128)S(1)}, f32[64,128]{1,0:T(8,128)S(1)}, u32[]{:S(2)}, u32[]{:S(2)}) collective-permute-start(f32[64,128]{1,0:T(8,128)S(1)} %add.11.part_ref), channel_id=1, source_target_pairs={{0,8},{1,9},{2,10},{3,11},{4,12},{5,13},{6,14},{7,15},{8,0},{9,1},... | collective-permute-start | bytes 98312 | tf_op jit(solution)/shard_map/ppermute | solution.py:692
  67.7 1.9 %collective-permute-done.6.other_ref = f32[64,128]{1,0:T(8,128)S(1)} collective-permute-done((f32[64,128]{1,0:T(8,128)S(1)}, f32[64,128]{1,0:T(8,128)S(1)}, u32[]{:S(2)}, u32[]{:S(2)}) %collective-permute-start.6) | collective-permute-done | bytes 32800 | tf_op jit(solution)/shard_map/ppermute | solution.py:692
  69.5 10.8 %back.1 = (bf16[6,4096,256]{2,1,0:T(8,128)(2,1)}, f32[4,6]{1,0:T(4,128)}) custom-call(s32[2]{0:T(128)S(1)} %copy-done.2, f32[64,128]{1,0:T(8,128)S(1)} %add.11.part_ref, f32[64,128]{1,0:T(8,128)S(1)} %collective-permute-done.6.other_ref, f32[64,128]{1,0:T(8,128)S(1)} %get-tuple-element.18.column_ref, ...), custom_call_target="tpu_custom_call", output_to_operand_aliasing={{0}: (8, {})} | custom-call | tf_op jit(solution)/shard_map/back/pallas_call | solution.py:696
  (3 shorter events, 0.0 us)
Async XLA Ops:
  3.5 32.5 %all-to-all-start = ((bf16[16,144,256]{2,1,0:T(8,128)(2,1)}), bf16[16,144,256]{2,1,0:T(8,128)(2,1)S(1)}, u32[]{:S(2)}, u32[]{:S(2)}) async-start(bf16[16,144,256]{2,1,0:T(8,128)(2,1)} %pack.1), calls=%async_computation | async-start | bytes 2359296 | tf_op jit(solution)/shard_map/all_to_all | solution.py:588
  11.5 4.6 %copy-start.1 = (bf16[4096,256]{1,0:T(8,128)(2,1)S(1)}, bf16[4096,256]{1,0:T(8,128)(2,1)}, u32[]{:S(2)}) copy-start(bf16[4096,256]{1,0:T(8,128)(2,1)} %mean_hbm.3) | copy-start | bytes 6291460
  11.5 4.6 %copy-start.2 = (s32[2]{0:T(128)S(1)}, s32[2]{0:T(128)}, u32[]{:S(2)}) copy-start(s32[2]{0:T(128)} %pad_add_fusion.place_ref) | copy-start | bytes 28
  14.3 22.7 %copy-start.3 = (f32[4]{0:T(128)S(1)}, f32[4]{0:T(128)}, u32[]{:S(2)}) copy-start(f32[4]{0:T(128)} %noise_ref.1) | copy-start | bytes 52
  14.3 18.7 %collective-permute-start = (bf16[7,160,256]{2,1,0:T(8,128)(2,1)}, bf16[7,160,256]{2,1,0:T(8,128)(2,1)S(1)}, u32[]{:S(2)}, u32[]{:S(2)}) collective-permute-start(bf16[7,160,256]{2,1,0:T(8,128)(2,1)} %get-tuple-element.13), channel_id=1, source_target_pairs={{0,1},{1,0},{2,3},{3,2},{4,5},{5,4},{6,7},{7,6},{8,9},{9,8},{10,11... | collective-permute-start | bytes 1720328 | tf_op jit(solution)/shard_map/ppermute | solution.py:611
  14.7 18.3 %collective-permute-start.1 = (bf16[7,160,256]{2,1,0:T(8,128)(2,1)}, bf16[7,160,256]{2,1,0:T(8,128)(2,1)S(1)}, u32[]{:S(2)}, u32[]{:S(2)}) collective-permute-start(bf16[7,160,256]{2,1,0:T(8,128)(2,1)} %get-tuple-element.14), channel_id=1, source_target_pairs={{1,2},{2,1},{3,4},{4,3},{5,6},{6,5},{9,10},{10,9},{11,12},{12,11},... | collective-permute-start | bytes 1720328 | tf_op jit(solution)/shard_map/ppermute | solution.py:612
  15.4 17.6 %collective-permute-start.2 = (bf16[7,32,256]{2,1,0:T(8,128)(2,1)}, bf16[7,32,256]{2,1,0:T(8,128)(2,1)S(1)}, u32[]{:S(2)}, u32[]{:S(2)}) collective-permute-start(bf16[7,32,256]{2,1,0:T(8,128)(2,1)} %get-tuple-element.15), channel_id=1, source_target_pairs={{7,8},{8,7},{23,24},{24,23}} | collective-permute-start | bytes 344072 | tf_op jit(solution)/shard_map/ppermute | solution.py:610
  16.1 4.6 %copy-start = (bf16[6,4096,256]{2,1,0:T(8,128)(2,1)S(1)}, bf16[6,4096,256]{2,1,0:T(8,128)(2,1)}, u32[]{:S(2)}) copy-start(bf16[6,4096,256]{2,1,0:T(8,128)(2,1)} %comp_hbm.3) | copy-start | bytes 37748740
  33.0 3.0 %copy-start.7 = (bf16[7,32,256]{2,1,0:T(8,128)(2,1)}, bf16[7,32,256]{2,1,0:T(8,128)(2,1)S(1)}, u32[]{:S(2)}) copy-start(bf16[7,32,256]{2,1,0:T(8,128)(2,1)S(1)} %collective-permute-done.2.middle_hbm) | copy-start | bytes 344068
  33.0 3.0 %copy-start.5 = (bf16[7,160,256]{2,1,0:T(8,128)(2,1)}, bf16[7,160,256]{2,1,0:T(8,128)(2,1)S(1)}, u32[]{:S(2)}) copy-start(bf16[7,160,256]{2,1,0:T(8,128)(2,1)S(1)} %collective-permute-done.near_hbm) | copy-start | bytes 1720324
  33.0 3.0 %copy-start.6 = (bf16[7,160,256]{2,1,0:T(8,128)(2,1)}, bf16[7,160,256]{2,1,0:T(8,128)(2,1)S(1)}, u32[]{:S(2)}) copy-start(bf16[7,160,256]{2,1,0:T(8,128)(2,1)S(1)} %collective-permute-done.1.far_hbm) | copy-start | bytes 1720324
  36.0 1.1 %copy-start.4 = (bf16[16,144,256]{2,1,0:T(8,128)(2,1)}, bf16[16,144,256]{2,1,0:T(8,128)(2,1)S(1)}, u32[]{:S(2)}) copy-start(bf16[16,144,256]{2,1,0:T(8,128)(2,1)S(1)} %all-to-all-done) | copy-start | bytes 3538948
  51.1 4.2 %collective-permute-start.3 = (f32[64,128]{1,0:T(8,128)S(1)}, f32[64,128]{1,0:T(8,128)S(1)}, u32[]{:S(2)}, u32[]{:S(2)}) collective-permute-start(f32[64,128]{1,0:T(8,128)S(1)} %get-tuple-element.17), channel_id=1, source_target_pairs={{0,1},{1,0},{2,3},{3,2},{4,5},{5,4},{6,7},{7,6},{8,9},{9,8},{10,11... | collective-permute-start | bytes 98312 | tf_op jit(solution)/shard_map/ppermute | solution.py:690
  55.3 4.5 %collective-permute-start.4 = (f32[64,128]{1,0:T(8,128)S(1)}, f32[64,128]{1,0:T(8,128)S(1)}, u32[]{:S(2)}, u32[]{:S(2)}) collective-permute-start(f32[64,128]{1,0:T(8,128)S(1)} %add.9), channel_id=1, source_target_pairs={{0,2},{1,3},{2,0},{3,1},{4,6},{5,7},{6,4},{7,5},{8,10},{9,11},{10,... | collective-permute-start | bytes 98312 | tf_op jit(solution)/shard_map/ppermute | solution.py:690
  59.8 4.9 %collective-permute-start.5 = (f32[64,128]{1,0:T(8,128)S(1)}, f32[64,128]{1,0:T(8,128)S(1)}, u32[]{:S(2)}, u32[]{:S(2)}) collective-permute-start(f32[64,128]{1,0:T(8,128)S(1)} %add.10), channel_id=1, source_target_pairs={{0,4},{1,5},{2,6},{3,7},{4,0},{5,1},{6,2},{7,3},{8,12},{9,13},{10,... | collective-permute-start | bytes 98312 | tf_op jit(solution)/shard_map/ppermute | solution.py:690
  64.7 4.8 %collective-permute-start.6 = (f32[64,128]{1,0:T(8,128)S(1)}, f32[64,128]{1,0:T(8,128)S(1)}, u32[]{:S(2)}, u32[]{:S(2)}) collective-permute-start(f32[64,128]{1,0:T(8,128)S(1)} %add.11.part_ref), channel_id=1, source_target_pairs={{0,8},{1,9},{2,10},{3,11},{4,12},{5,13},{6,14},{7,15},{8,0},{9,1},... | collective-permute-start | bytes 98312 | tf_op jit(solution)/shard_map/ppermute | solution.py:692

commit v6 on v5

--- a/solution.py
+++ b/solution.py
@@ -220,9 +220,9 @@
 
 
 def extract_kernel(
-    sizes, place_ref, noise_ref, got_hbm, near_hbm, far_hbm, middle_hbm, mean_hbm, comp_hbm, table_hbm,
+    sizes, place_ref, noise_ref, got_ref, near_hbm, far_hbm, middle_hbm, mean_hbm, comp_hbm, table_hbm,
     out_ref, rows_ref, extra_ref, rows_extra_ref, total_ref, column_ref,
-    got_ref, near_ref, far_ref, middle_ref, own_ref, table_ref, edge_sem, table_sem,
+    near_ref, far_ref, middle_ref, own_ref, table_ref, edge_sem, table_sem,
     wide_ref, upper_ref, sums_ref,
 ):
     planes, slots, blocks, chunk, images, peers = sizes
@@ -231,12 +231,11 @@
     stride = count * slots + 2 * count + PARAMETERS
     one_plane = pl.ds(0, GRID)
     edges = (
-        pltpu.make_async_copy(got_hbm, got_ref, edge_sem.at[0]),
-        pltpu.make_async_copy(near_hbm, near_ref, edge_sem.at[1]),
-        pltpu.make_async_copy(far_hbm, far_ref, edge_sem.at[2]),
-        pltpu.make_async_copy(middle_hbm, middle_ref, edge_sem.at[3]),
-        pltpu.make_async_copy(mean_hbm.at[one_plane], own_ref.at[0], edge_sem.at[4]),
-        pltpu.make_async_copy(comp_hbm.at[:, one_plane], own_ref.at[pl.ds(1, COMPS)], edge_sem.at[5]),
+        pltpu.make_async_copy(near_hbm, near_ref, edge_sem.at[0]),
+        pltpu.make_async_copy(far_hbm, far_ref, edge_sem.at[1]),
+        pltpu.make_async_copy(middle_hbm, middle_ref, edge_sem.at[2]),
+        pltpu.make_async_copy(mean_hbm.at[one_plane], own_ref.at[0], edge_sem.at[3]),
+        pltpu.make_async_copy(comp_hbm.at[:, one_plane], own_ref.at[pl.ds(1, COMPS)], edge_sem.at[4]),
     )
 
     def copies(part):
@@ -252,7 +251,6 @@
     def _():
         for part in range(slots // chunk):
             copies(part)[0].start()
-        edges[0].wait()
         for tile in range(GRID // LANES):
             wide_ref[tile] = got_ref[:, tile * LANES : (tile + 1) * LANES].astype(f32)
         for image in range(count):
@@ -266,7 +264,7 @@
                     part = wide_ref[tile, pl.ds(start, peers, stride=stride), :]
                     rows_extra_ref[at : at + peers, tile * LANES : (tile + 1) * LANES] = part.astype(bf16)
         sums_ref[...] = jnp.zeros_like(sums_ref)
-        for copy in edges[1:]:
+        for copy in edges:
             copy.wait()
 
     @pl.when(step < slots // chunk)
@@ -549,6 +547,10 @@
     return pl.BlockSpec(memory_space=pl.ANY)
 
 
+def in_vmem(value):
+    return pltpu.with_memory_space_constraint(value, pltpu.VMEM)
+
+
 def in_hbm(value):
     return pltpu.with_memory_space_constraint(value, pltpu.HBM)
 
@@ -634,7 +636,7 @@
             pltpu.VMEM((COMPS, 16, GRID), bf16),
             pltpu.SemaphoreType.DMA((planes, (GRID - wide) // 16)),
         ],
-        compiler_params=params(30),
+        compiler_params=params(52),
         name="table",
     )(place, mean_volume, components)
 
@@ -649,7 +651,7 @@
             jax.ShapeDtypeStruct((total, LANES), f32),
         ],
         grid=(steps,),
-        in_specs=[smem(), smem()] + [hbm()] * 7,
+        in_specs=[smem(), smem(), pl.BlockSpec(memory_space=pltpu.VMEM)] + [hbm()] * 6,
         out_specs=[
             pl.BlockSpec((chunk, CHANS * total, GRID), lambda n: (n, 0, 0)),
             pl.BlockSpec((chunk, total, GRID), lambda n: (n, 0, 0)),
@@ -659,13 +661,12 @@
             whole((total, LANES)),
         ],
         scratch_shapes=[
-            pltpu.VMEM((peers * pack_rows, GRID), bf16),
             pltpu.VMEM((CHANS, wide, GRID), bf16),
             pltpu.VMEM((CHANS, wide, GRID), bf16),
             pltpu.VMEM((CHANS, MIDDLE, GRID), bf16),
             pltpu.VMEM((CHANS, GRID, GRID), bf16),
             pltpu.VMEM((slots, planes * blocks, width), bf16),
-            pltpu.SemaphoreType.DMA((6,)),
+            pltpu.SemaphoreType.DMA((5,)),
             pltpu.SemaphoreType.DMA((steps,)),
             pltpu.VMEM((GRID // LANES, peers * pack_rows, LANES), f32),
             pltpu.VMEM((slots, -(-blocks // 16) * 16, width), bf16),
@@ -676,7 +677,7 @@
     )(
         place,
         noise_var,
-        in_hbm(got.reshape(peers * pack_rows, GRID)),
+        in_vmem(got.reshape(peers * pack_rows, GRID)),
         in_hbm(near),
         in_hbm(far),
         in_hbm(middle),

time: 80.8 us -> 79.9 us (0.989)
  local copies, waits for them, and re-layouts: 5.64 us -> 0.02 us
  waiting for transfers between devices: 9.5 us -> 12.3 us
  Pallas kernels: 42.8 us -> 44.3 us
    unnamed x16 -> x10, local copies, waits for them, and re-layouts: 5.64 us -> 0.02 us
    all_to_all x1, waiting for transfers between devices: 2.96 us -> 5.72 us  [local(): lax.all_to_all(packed, 'slab', split_axis=0, concat_axis=0, tiled=True)]
    pallas_call x1, Pallas kernels: 12.3 us -> 14.3 us  [local(): pl.pallas_call(functools.partial(table_kernel, (planes, slots, blocks, pa...]
  transfers between devices with their start and end apart: 8 -> 8, of which waited for: 5 -> 5; matrix products, arithmetic and copies ran while one was open for 1% -> 1% of each run, Pallas kernels for 19% -> 21%
where the time goes in v6:
time: 79.9 us; the launch traced here: 79.6 us
  Pallas kernels  44.3 us (55%)
  starting transfers between devices  21.6 us (27%)
  waiting for transfers between devices  12.3 us (15%)
    pallas_call x1, Pallas kernels, local(): pl.pallas_call(functools.partial(table_kernel, (planes, slots, blocks, pa...  14.3 us
    pallas_call x1, Pallas kernels, local(): pl.pallas_call(functools.partial(extract_kernel, (planes, slots, blocks,...  13.7 us
    ppermute x4, starting transfers between devices, local(): lax.ppermute(partial, 'slab', [(n, n ^ step) for n in range(peers)])  12.5 us
    pallas_call x1, Pallas kernels, local(): pl.pallas_call(functools.partial(back_kernel, (planes, slots, blocks, chu...  10.8 us
    all_to_all x1, starting transfers between devices, local(): lax.all_to_all(packed, 'slab', split_axis=0, concat_axis=0, tiled=True)  7.38 us
    ppermute x4, waiting for transfers between devices, local(): lax.ppermute(partial, 'slab', [(n, n ^ step) for n in range(peers)])  6.53 us
    all_to_all x1, waiting for transfers between devices, local(): lax.all_to_all(packed, 'slab', split_axis=0, concat_axis=0, tiled=True)  5.72 us
    pallas_call x1, Pallas kernels, local(): pl.pallas_call(functools.partial(pack_kernel, (planes, slots, peers, coun...  2.82 us
  transfers between devices with their start and end apart: 8, of which 5 were waited for; matrix products, arithmetic and copies ran while one was open for 1% of the time, Pallas kernels for 21%

profile of v6, /device:TPU:0, one launch (start us, length us, event | category | flops | bytes accessed | tf_op | source)
XLA Modules:
  0.0 79.6 jit_solution(15730078631392597999)
XLA Ops:
  0.6 2.8 %pack.1 = bf16[16,144,256]{2,1,0:T(8,128)(2,1)} custom-call(s32[4]{0:T(128)} %tilt_ref.1, s32[4]{0:T(128)} %shift_ref.1, s32[4]{0:T(128)} %frac_ref.1, bf16[1024,256]{1,0:T(8,128)(2,1)} %bitcast.5), custom_call_target="tpu_custom_call" | custom-call | tf_op jit(solution)/shard_map/pack/pallas_call | solution.py:580
  3.4 7.4 %all-to-all-start = ((bf16[16,144,256]{2,1,0:T(8,128)(2,1)}), bf16[16,144,256]{2,1,0:T(8,128)(2,1)S(1)}, u32[]{:S(2)}, u32[]{:S(2)}) async-start(bf16[16,144,256]{2,1,0:T(8,128)(2,1)} %pack.1), calls=%async_computation | async-start | bytes 2359296 | tf_op jit(solution)/shard_map/all_to_all | solution.py:590
  10.8 0.6 pad_add_fusion.place_ref
  11.4 0.0 copy-start
  11.5 2.6 %edges.1 = (bf16[7,160,256]{2,1,0:T(8,128)(2,1)}, bf16[7,160,256]{2,1,0:T(8,128)(2,1)}, bf16[7,32,256]{2,1,0:T(8,128)(2,1)}) custom-call(s32[2]{0:T(128)} %pad_add_fusion.place_ref, bf16[4096,256]{1,0:T(8,128)(2,1)} %mean_hbm.3, bf16[6,4096,256]{2,1,0:T(8,128)(2,1)} %comp_hbm.3, bf16[4096,256]{1,0:T(8,128)(2,1)} %mean_hbm.3, bf16[6,4096,256]{2,1,0:T(8,128)(2,1)} %comp_hbm.3), custom_call_target="tpu_custom_call" | custom-call | tf_op jit(solution)/shard_map/edges/pallas_call | solution.py:595
  14.1 0.0 copy-start.1
  14.1 0.4 collective-permute-start
  14.5 0.7 collective-permute-start.1
  15.2 0.7 collective-permute-start.2
  15.9 0.0 copy-done
  15.9 14.3 %table.1 = (bf16[32,128,1792]{2,1,0:T(8,128)(2,1)}, bf16[6,4096,256]{2,1,0:T(8,128)(2,1)}) custom-call(s32[2]{0:T(128)S(1)} %copy-done, bf16[4096,256]{1,0:T(8,128)(2,1)} %mean_hbm.3, bf16[6,4096,256]{2,1,0:T(8,128)(2,1)} %comp_hbm.3), custom_call_target="tpu_custom_call" | custom-call | tf_op jit(solution)/shard_map/table/pallas_call | solution.py:618
  30.2 0.0 collective-permute-done.2.middle_hbm
  30.2 0.0 copy-start.4
  30.2 0.0 collective-permute-done.near_hbm
  30.2 0.0 copy-start.2
  30.2 0.0 collective-permute-done.1.far_hbm
  30.2 0.0 copy-start.3
  30.2 5.7 %all-to-all-done = bf16[16,144,256]{2,1,0:T(8,128)(2,1)S(1)} async-done(((bf16[16,144,256]{2,1,0:T(8,128)(2,1)}), bf16[16,144,256]{2,1,0:T(8,128)(2,1)S(1)}, u32[]{:S(2)}, u32[]{:S(2)}) %all-to-all-start) | async-done | bytes 1179680 | tf_op jit(solution)/shard_map/all_to_all | solution.py:590
  36.0 0.0 copy-done.4
  36.0 0.0 copy-done.2
  36.0 0.0 copy-done.3
  36.0 0.0 copy-done.1
  36.0 13.7 %extract.1 = (bf16[32,448,256]{2,1,0:T(8,128)(2,1)S(1)}, bf16[32,64,256]{2,1,0:T(8,128)(2,1)S(1)}, bf16[128,1792]{1,0:T(8,128)(2,1)S(1)}, bf16[128,256]{1,0:T(8,...) custom-call(s32[2]{0:T(128)S(1)} %copy-done, f32[4]{0:T(128)S(1)} %copy-done.1, ...), custom_call_target="tpu_custom_call" | custom-call | tf_op jit(solution)/shard_map/extract/pallas_call | solution.py:643
  49.7 3.8 %collective-permute-start.3 = (f32[64,128]{1,0:T(8,128)S(1)}, f32[64,128]{1,0:T(8,128)S(1)}, u32[]{:S(2)}, u32[]{:S(2)}) collective-permute-start(f32[64,128]{1,0:T(8,128)S(1)} %get-tuple-element.17), channel_id=1, source_target_pairs={{0,1},{1,0},{2,3},{3,2},{4,5},{5,4},{6,7},{7,6},{8,9},{9,8},{10,11... | collective-permute-start | bytes 98312 | tf_op jit(solution)/shard_map/ppermute | solution.py:691
  53.5 0.9 %collective-permute-done.3 = f32[64,128]{1,0:T(8,128)S(1)} collective-permute-done((f32[64,128]{1,0:T(8,128)S(1)}, f32[64,128]{1,0:T(8,128)S(1)}, u32[]{:S(2)}, u32[]{:S(2)}) %collective-permute-start.3) | collective-permute-done | bytes 32800 | tf_op jit(solution)/shard_map/ppermute | solution.py:691
  54.4 2.6 %collective-permute-start.4 = (f32[64,128]{1,0:T(8,128)S(1)}, f32[64,128]{1,0:T(8,128)S(1)}, u32[]{:S(2)}, u32[]{:S(2)}) collective-permute-start(f32[64,128]{1,0:T(8,128)S(1)} %add.9), channel_id=1, source_target_pairs={{0,2},{1,3},{2,0},{3,1},{4,6},{5,7},{6,4},{7,5},{8,10},{9,11},{10,... | collective-permute-start | bytes 98312 | tf_op jit(solution)/shard_map/ppermute | solution.py:691
  57.0 1.9 %collective-permute-done.4 = f32[64,128]{1,0:T(8,128)S(1)} collective-permute-done((f32[64,128]{1,0:T(8,128)S(1)}, f32[64,128]{1,0:T(8,128)S(1)}, u32[]{:S(2)}, u32[]{:S(2)}) %collective-permute-start.4) | collective-permute-done | bytes 32800 | tf_op jit(solution)/shard_map/ppermute | solution.py:691
  58.9 3.2 %collective-permute-start.5 = (f32[64,128]{1,0:T(8,128)S(1)}, f32[64,128]{1,0:T(8,128)S(1)}, u32[]{:S(2)}, u32[]{:S(2)}) collective-permute-start(f32[64,128]{1,0:T(8,128)S(1)} %add.10), channel_id=1, source_target_pairs={{0,4},{1,5},{2,6},{3,7},{4,0},{5,1},{6,2},{7,3},{8,12},{9,13},{10,... | collective-permute-start | bytes 98312 | tf_op jit(solution)/shard_map/ppermute | solution.py:691
  62.0 1.9 %collective-permute-done.5 = f32[64,128]{1,0:T(8,128)S(1)} collective-permute-done((f32[64,128]{1,0:T(8,128)S(1)}, f32[64,128]{1,0:T(8,128)S(1)}, u32[]{:S(2)}, u32[]{:S(2)}) %collective-permute-start.5) | collective-permute-done | bytes 32800 | tf_op jit(solution)/shard_map/ppermute | solution.py:691
  63.9 2.9 %collective-permute-start.6 = (f32[64,128]{1,0:T(8,128)S(1)}, f32[64,128]{1,0:T(8,128)S(1)}, u32[]{:S(2)}, u32[]{:S(2)}) collective-permute-start(f32[64,128]{1,0:T(8,128)S(1)} %add.11.part_ref), channel_id=1, source_target_pairs={{0,8},{1,9},{2,10},{3,11},{4,12},{5,13},{6,14},{7,15},{8,0},{9,1},... | collective-permute-start | bytes 98312 | tf_op jit(solution)/shard_map/ppermute | solution.py:693
  66.9 1.9 %collective-permute-done.6.other_ref = f32[64,128]{1,0:T(8,128)S(1)} collective-permute-done((f32[64,128]{1,0:T(8,128)S(1)}, f32[64,128]{1,0:T(8,128)S(1)}, u32[]{:S(2)}, u32[]{:S(2)}) %collective-permute-start.6) | collective-permute-done | bytes 32800 | tf_op jit(solution)/shard_map/ppermute | solution.py:693
  68.8 10.8 %back.1 = (bf16[6,4096,256]{2,1,0:T(8,128)(2,1)}, f32[4,6]{1,0:T(4,128)}) custom-call(s32[2]{0:T(128)S(1)} %copy-done, f32[64,128]{1,0:T(8,128)S(1)} %add.11.part_ref, f32[64,128]{1,0:T(8,128)S(1)} %collective-permute-done.6.other_ref, f32[64,128]{1,0:T(8,128)S(1)} %get-tuple-element.18.column_ref, ...), custom_call_target="tpu_custom_call", output_to_operand_aliasing={{0}: (8, {})} | custom-call | tf_op jit(solution)/shard_map/back/pallas_call | solution.py:697
  (3 shorter events, 0.0 us)
Async XLA Ops:
  3.4 32.5 %all-to-all-start = ((bf16[16,144,256]{2,1,0:T(8,128)(2,1)}), bf16[16,144,256]{2,1,0:T(8,128)(2,1)S(1)}, u32[]{:S(2)}, u32[]{:S(2)}) async-start(bf16[16,144,256]{2,1,0:T(8,128)(2,1)} %pack.1), calls=%async_computation | async-start | bytes 2359296 | tf_op jit(solution)/shard_map/all_to_all | solution.py:590
  11.4 4.4 %copy-start = (s32[2]{0:T(128)S(1)}, s32[2]{0:T(128)}, u32[]{:S(2)}) copy-start(s32[2]{0:T(128)} %pad_add_fusion.place_ref) | copy-start | bytes 28
  14.1 21.9 %copy-start.1 = (f32[4]{0:T(128)S(1)}, f32[4]{0:T(128)}, u32[]{:S(2)}) copy-start(f32[4]{0:T(128)} %noise_ref.1) | copy-start | bytes 52
  14.1 16.1 %collective-permute-start = (bf16[7,160,256]{2,1,0:T(8,128)(2,1)}, bf16[7,160,256]{2,1,0:T(8,128)(2,1)S(1)}, u32[]{:S(2)}, u32[]{:S(2)}) collective-permute-start(bf16[7,160,256]{2,1,0:T(8,128)(2,1)} %get-tuple-element.13), channel_id=1, source_target_pairs={{0,1},{1,0},{2,3},{3,2},{4,5},{5,4},{6,7},{7,6},{8,9},{9,8},{10,11... | collective-permute-start | bytes 1720328 | tf_op jit(solution)/shard_map/ppermute | solution.py:613
  14.5 15.7 %collective-permute-start.1 = (bf16[7,160,256]{2,1,0:T(8,128)(2,1)}, bf16[7,160,256]{2,1,0:T(8,128)(2,1)S(1)}, u32[]{:S(2)}, u32[]{:S(2)}) collective-permute-start(bf16[7,160,256]{2,1,0:T(8,128)(2,1)} %get-tuple-element.14), channel_id=1, source_target_pairs={{1,2},{2,1},{3,4},{4,3},{5,6},{6,5},{9,10},{10,9},{11,12},{12,11},... | collective-permute-start | bytes 1720328 | tf_op jit(solution)/shard_map/ppermute | solution.py:614
  15.2 15.0 %collective-permute-start.2 = (bf16[7,32,256]{2,1,0:T(8,128)(2,1)}, bf16[7,32,256]{2,1,0:T(8,128)(2,1)S(1)}, u32[]{:S(2)}, u32[]{:S(2)}) collective-permute-start(bf16[7,32,256]{2,1,0:T(8,128)(2,1)} %get-tuple-element.15), channel_id=1, source_target_pairs={{7,8},{8,7},{23,24},{24,23}} | collective-permute-start | bytes 344072 | tf_op jit(solution)/shard_map/ppermute | solution.py:612
  30.2 5.8 %copy-start.4 = (bf16[7,32,256]{2,1,0:T(8,128)(2,1)}, bf16[7,32,256]{2,1,0:T(8,128)(2,1)S(1)}, u32[]{:S(2)}) copy-start(bf16[7,32,256]{2,1,0:T(8,128)(2,1)S(1)} %collective-permute-done.2.middle_hbm) | copy-start | bytes 344068
  30.2 5.8 %copy-start.2 = (bf16[7,160,256]{2,1,0:T(8,128)(2,1)}, bf16[7,160,256]{2,1,0:T(8,128)(2,1)S(1)}, u32[]{:S(2)}) copy-start(bf16[7,160,256]{2,1,0:T(8,128)(2,1)S(1)} %collective-permute-done.near_hbm) | copy-start | bytes 1720324
  30.2 5.7 %copy-start.3 = (bf16[7,160,256]{2,1,0:T(8,128)(2,1)}, bf16[7,160,256]{2,1,0:T(8,128)(2,1)S(1)}, u32[]{:S(2)}) copy-start(bf16[7,160,256]{2,1,0:T(8,128)(2,1)S(1)} %collective-permute-done.1.far_hbm) | copy-start | bytes 1720324
  49.7 4.7 %collective-permute-start.3 = (f32[64,128]{1,0:T(8,128)S(1)}, f32[64,128]{1,0:T(8,128)S(1)}, u32[]{:S(2)}, u32[]{:S(2)}) collective-permute-start(f32[64,128]{1,0:T(8,128)S(1)} %get-tuple-element.17), channel_id=1, source_target_pairs={{0,1},{1,0},{2,3},{3,2},{4,5},{5,4},{6,7},{7,6},{8,9},{9,8},{10,11... | collective-permute-start | bytes 98312 | tf_op jit(solution)/shard_map/ppermute | solution.py:691
  54.4 4.5 %collective-permute-start.4 = (f32[64,128]{1,0:T(8,128)S(1)}, f32[64,128]{1,0:T(8,128)S(1)}, u32[]{:S(2)}, u32[]{:S(2)}) collective-permute-start(f32[64,128]{1,0:T(8,128)S(1)} %add.9), channel_id=1, source_target_pairs={{0,2},{1,3},{2,0},{3,1},{4,6},{5,7},{6,4},{7,5},{8,10},{9,11},{10,... | collective-permute-start | bytes 98312 | tf_op jit(solution)/shard_map/ppermute | solution.py:691
  58.9 5.0 %collective-permute-start.5 = (f32[64,128]{1,0:T(8,128)S(1)}, f32[64,128]{1,0:T(8,128)S(1)}, u32[]{:S(2)}, u32[]{:S(2)}) collective-permute-start(f32[64,128]{1,0:T(8,128)S(1)} %add.10), channel_id=1, source_target_pairs={{0,4},{1,5},{2,6},{3,7},{4,0},{5,1},{6,2},{7,3},{8,12},{9,13},{10,... | collective-permute-start | bytes 98312 | tf_op jit(solution)/shard_map/ppermute | solution.py:691
  63.9 4.8 %collective-permute-start.6 = (f32[64,128]{1,0:T(8,128)S(1)}, f32[64,128]{1,0:T(8,128)S(1)}, u32[]{:S(2)}, u32[]{:S(2)}) collective-permute-start(f32[64,128]{1,0:T(8,128)S(1)} %add.11.part_ref), channel_id=1, source_target_pairs={{0,8},{1,9},{2,10},{3,11},{4,12},{5,13},{6,14},{7,15},{8,0},{9,1},... | collective-permute-start | bytes 98312 | tf_op jit(solution)/shard_map/ppermute | solution.py:693
